TPU v7x, 32 devices: a whole 2x2x4 slice. The times are simulated.
32 devices in a mesh: row: 8 (over y, x, core), col: 4 (over z).
Axes of the slice: x: 2, y: 2, z: 4, core: 2. Of those that a mesh axis runs over, the one named last changes fastest.
Arguments:
- inputs: bfloat16 [8192, 2048], P('row', 'col'), may hold values from -6 to 6
- segments: int32 [8, 1024], P('row'), may hold values from 0 to 7, never falling along the last dimension, each value on 1 to 256 neighbouring positions
- routes: int32 [8192, 4], P('row'), may hold values from 0 to 7, all different within a row
- gain_attn: float32 [2048], P('col'), may hold values from 0.5 to 1.5
- w_query: bfloat16 [2048, 2048], P('row', 'col'), may hold values from -0.125 to 0.125
- w_key: bfloat16 [2048, 2048], P('row', 'col'), may hold values from -0.125 to 0.125
- w_value: bfloat16 [2048, 2048], P('row', 'col'), may hold values from -0.125 to 0.125
- b_query: float32 [2048], P('col'), may hold values from -1.2 to 1.2
- b_key: float32 [2048], P('col'), may hold values from -1.2 to 1.2
- b_value: float32 [2048], P('col'), may hold values from -1.2 to 1.2
- w_out: bfloat16 [2048, 2048], P('col', 'row'), may hold values from -0.75 to 0.75
- gain_ffn: float32 [2048], P('col'), may hold values from 0.5 to 1.5
- w_router: bfloat16 [2048, 8], P('row'), may hold values from -0.0625 to 0.0625
- w_expert_gate: bfloat16 [8, 2048, 1408], P('col', 'row'), may hold values from -0.125 to 0.125
- w_expert_up: bfloat16 [8, 2048, 1408], P('col', 'row'), may hold values from -0.125 to 0.125
- w_expert_down: bfloat16 [8, 1408, 2048], P('col', None, 'row'), may hold values from -0.625 to 0.625
- w_shared_gate: bfloat16 [2048, 5632], P('row', 'col'), may hold values from -0.125 to 0.125
- w_shared_up: bfloat16 [2048, 5632], P('row', 'col'), may hold values from -0.125 to 0.125
- w_shared_down: bfloat16 [5632, 2048], P('col', 'row'), may hold values from -0.15625 to 0.15625
- w_shared_mix: bfloat16 [2048], P('row'), may hold values from -0.125 to 0.125
- cotangent: bfloat16 [8192, 2048], P('row', 'col'), may hold values from -6 to 6
Outputs:
- output: float32 [8192, 2048], P('row', 'col')
- input_grad: float32 [8192, 2048], P('row', 'col')
- grad_gain_attn: float32 [2048], P('col')
- grad_w_query: float32 [2048, 2048], P('row', 'col')
- grad_w_key: float32 [2048, 2048], P('row', 'col')
- grad_w_value: float32 [2048, 2048], P('row', 'col')
- grad_b_query: float32 [2048], P('col')
- grad_b_key: float32 [2048], P('col')
- grad_b_value: float32 [2048], P('col')
- grad_w_out: float32 [2048, 2048], P('col', 'row')
- grad_gain_ffn: float32 [2048], P('col')
- grad_w_router: float32 [2048, 8], P('row')
- grad_w_expert_gate: float32 [8, 2048, 1408], P('col', 'row')
- grad_w_expert_up: float32 [8, 2048, 1408], P('col', 'row')
- grad_w_expert_down: float32 [8, 1408, 2048], P('col', None, 'row')
- grad_w_shared_gate: float32 [2048, 5632], P('row', 'col')
- grad_w_shared_up: float32 [2048, 5632], P('row', 'col')
- grad_w_shared_down: float32 [5632, 2048], P('col', 'row')
- grad_w_shared_mix: float32 [2048], P('row')
Inputs may be any that keep to these rules, and one draw needn't show every extreme that they name: `segments`: within each sequence of 1024 tokens the segment numbers never fall. `routes`: each token names 4 different experts.
All inputs are finite; a program needn't handle non-finite values.
Results may differ from a plain program's by a relative error of at most 0.033.
Values may be sent and summed in bfloat16 or wider, within the bound.
No kernel may reach another device: no remote copies, remote signals or barrier semaphores. Data moves between devices by JAX's collectives and lax.ppermute only.
A program may use at most 320 MiB of HBM per device.

v0:
```python
import jax
import jax.numpy as jnp
from jax import lax
from jax.sharding import PartitionSpec as P

D = 2048
HEAD_DIM = 128
EXPERTS = 8
TOP = 4
CAP = 576


EPSILON = 1e-06
THETA = 1000000.0
NEGATIVE = -1e30


def times_transposed(left_side, right_side, precision=None):
    return lax.dot_general(
        left_side,
        right_side,
        (((1,), (1,)), ((), ())),
        precision=precision,
        preferred_element_type=jnp.float32,
    )


def transposed_times(left_side, right_side, precision=None):
    return lax.dot_general(
        left_side,
        right_side,
        (((0,), (0,)), ((), ())),
        precision=precision,
        preferred_element_type=jnp.float32,
    )


def column_total(values):
    return lax.psum(jnp.sum(values, axis=1), "col")


def rotary_tables(length, head_dim):
    position = jnp.arange(length).astype(jnp.float32)
    exponent = jnp.arange(head_dim // 2).astype(jnp.float32) * (2.0 / head_dim)
    angles = position[:, None] * jnp.exp(-exponent * jnp.log(THETA))[None, :]
    return (jnp.cos(angles)[:, None, :], jnp.sin(angles)[:, None, :])


def rotate(values, cosine_table, sine_table):
    half_dim = values.shape[-1] // 2
    first_half = values[..., :half_dim]
    second_half = values[..., half_dim:]
    return jnp.concatenate(
        [
            first_half * cosine_table - second_half * sine_table,
            second_half * cosine_table + first_half * sine_table,
        ],
        axis=-1,
    )


def rotate_back(values, cosine_table, sine_table):
    half_dim = values.shape[-1] // 2
    first_half = values[..., :half_dim]
    second_half = values[..., half_dim:]
    return jnp.concatenate(
        [
            first_half * cosine_table + second_half * sine_table,
            second_half * cosine_table - first_half * sine_table,
        ],
        axis=-1,
    )


def route_slots(routes_seq):
    flat_routes = routes_seq.reshape(-1)
    onehot = (flat_routes[:, None] == jnp.arange(EXPERTS)[None, :]).astype(jnp.int32)
    position_in = jnp.sum(jnp.cumsum(onehot, axis=0) * onehot, axis=1) - 1
    keep_pair = position_in < CAP
    slot_pair = jnp.where(keep_pair, flat_routes * CAP + position_in, EXPERTS * CAP)
    token_pair = jnp.arange(flat_routes.shape[0]) // TOP
    slot_token = jnp.zeros((EXPERTS * CAP,), jnp.int32).at[slot_pair].set(token_pair, mode="drop")
    slot_live = jnp.zeros((EXPERTS * CAP,), jnp.float32).at[slot_pair].set(1.0, mode="drop")
    safe_slot = jnp.minimum(slot_pair, EXPERTS * CAP - 1)
    return (slot_token, slot_live, slot_pair, safe_slot, keep_pair.astype(jnp.float32))


def local(
    inputs,
    segments,
    routes,
    gain_attn,
    w_query,
    w_key,
    w_value,
    b_query,
    b_key,
    b_value,
    w_out,
    gain_ffn,
    w_router,
    w_expert_gate,
    w_expert_up,
    w_expert_down,
    w_shared_gate,
    w_shared_up,
    w_shared_down,
    w_shared_mix,
    cotangent,
):
    f32 = jnp.float32
    bf16 = jnp.bfloat16
    highest = lax.Precision.HIGHEST
    length = inputs.shape[0]
    part_width = inputs.shape[1]
    col_start = lax.axis_index("col") * part_width
    head_dim = HEAD_DIM
    scale_factor = head_dim ** (-0.5)
    segment_row = segments[0]
    local_experts = w_expert_gate.shape[0]
    local_slots = local_experts * CAP
    slot_first = lax.axis_index("col") * local_slots
    inputs32 = inputs.astype(f32)
    inverse_attn = lax.rsqrt(column_total(inputs32 * inputs32) / D + EPSILON)
    normed = lax.all_gather(
        (inputs32 * inverse_attn[:, None] * gain_attn).astype(bf16), "col", axis=1, tiled=True
    )
    gathered = (
        lax.all_gather(w_query, "row", axis=0, tiled=True),
        lax.all_gather(w_key, "row", axis=0, tiled=True),
        lax.all_gather(w_value, "row", axis=0, tiled=True),
        lax.all_gather(w_out, "row", axis=1, tiled=True),
        lax.all_gather(w_router, "row", axis=0, tiled=True),
        lax.all_gather(w_shared_mix, "row", axis=0, tiled=True),
        lax.all_gather(w_expert_gate, "row", axis=1, tiled=True),
        lax.all_gather(w_expert_up, "row", axis=1, tiled=True),
        lax.all_gather(w_expert_down, "row", axis=2, tiled=True),
        lax.all_gather(w_shared_gate, "row", axis=0, tiled=True),
        lax.all_gather(w_shared_up, "row", axis=0, tiled=True),
        lax.all_gather(w_shared_down, "row", axis=1, tiled=True),
    )
    (
        all_query,
        all_key,
        all_value,
        all_out,
        all_router,
        all_mix,
        all_expert_gate,
        all_expert_up,
        all_expert_down,
        all_shared_gate,
        all_shared_up,
        all_shared_down,
    ) = gathered
    cosine_table, sine_table = rotary_tables(length, head_dim)
    local_heads = all_query.shape[1] // head_dim
    query_pre = (jnp.dot(normed, all_query, preferred_element_type=f32) + b_query).reshape(
        length, local_heads, head_dim
    )
    key_pre = (jnp.dot(normed, all_key, preferred_element_type=f32) + b_key).reshape(
        length, local_heads, head_dim
    )
    value_heads = (
        (jnp.dot(normed, all_value, preferred_element_type=f32) + b_value)
        .astype(bf16)
        .reshape(length, local_heads, head_dim)
    )
    query_rot = rotate(query_pre, cosine_table, sine_table).astype(bf16)
    key_rot = rotate(key_pre, cosine_table, sine_table).astype(bf16)
    block_rows = min(512, length)
    block_count = length // block_rows
    position = jnp.arange(length)
    query_blocks = query_rot.reshape(block_count, block_rows, local_heads, head_dim)
    block_starts = jnp.arange(block_count) * block_rows

    def block_scores(query_block, block_start):
        query_pos = block_start + jnp.arange(block_rows)
        query_seg = lax.dynamic_slice_in_dim(segment_row, block_start, block_rows)
        allowed = (position[None, :] <= query_pos[:, None]) & (
            segment_row[None, :] == query_seg[:, None]
        )
        raw_scores = (
            jnp.einsum("qhd,khd->hqk", query_block, key_rot, preferred_element_type=f32)
            * scale_factor
        )
        return jnp.where(allowed[None], raw_scores, NEGATIVE)

    def attend(members):
        query_block, block_start = members
        masked = block_scores(query_block, block_start)
        largest = jnp.max(masked, axis=-1, keepdims=True)
        unnormed = jnp.exp(masked - largest)
        row_total = jnp.sum(unnormed, axis=-1, keepdims=True)
        weights_soft = (unnormed / row_total).astype(bf16)
        block_out = jnp.einsum(
            "hqk,khd->qhd", weights_soft, value_heads, preferred_element_type=f32
        )
        return (block_out, (largest + jnp.log(row_total))[..., 0])

    attended_blocks, log_totals = lax.map(attend, (query_blocks, block_starts))
    mixed_heads = attended_blocks.reshape(length, local_heads * head_dim).astype(bf16)
    attended = lax.psum_scatter(
        jnp.dot(mixed_heads, all_out, preferred_element_type=f32).astype(jnp.bfloat16),
        "col",
        scatter_dimension=1,
        tiled=True,
    ).astype(jnp.float32)
    residual = inputs32 + attended
    inverse_ffn = lax.rsqrt(column_total(residual * residual) / D + EPSILON)
    normed_ffn = lax.all_gather(
        (residual * inverse_ffn[:, None] * gain_ffn).astype(bf16), "col", axis=1, tiled=True
    )
    router_probs = jax.nn.softmax(
        jnp.dot(normed_ffn, all_router, preferred_element_type=f32), axis=-1
    )
    gate_pair = jnp.take_along_axis(router_probs, routes, axis=1).reshape(-1)
    slot_token, slot_live, slot_pair, safe_slot, keep_pair = route_slots(routes)
    local_pair = safe_slot - slot_first
    pair_here = ((local_pair >= 0) & (local_pair < local_slots)).astype(f32)
    local_index = jnp.clip(local_pair, 0, local_slots - 1)
    local_table = local_index.reshape(length, TOP)
    keep_table = (keep_pair * pair_here).reshape(length, TOP)
    combine_table = (gate_pair * keep_pair * pair_here).reshape(length, TOP)
    token_here = lax.dynamic_slice_in_dim(slot_token, slot_first, local_slots)
    live_here = lax.dynamic_slice_in_dim(slot_live, slot_first, local_slots)
    buffer = (jnp.take(normed_ffn, token_here, axis=0) * live_here.astype(bf16)[:, None]).reshape(
        local_experts, CAP, D
    )
    gate_part = jnp.einsum("ecd,edf->ecf", buffer, all_expert_gate, preferred_element_type=f32)
    up_part = jnp.einsum("ecd,edf->ecf", buffer, all_expert_up, preferred_element_type=f32)
    gate_sigmoid = jax.nn.sigmoid(gate_part)
    activated = (gate_part * gate_sigmoid * up_part).astype(bf16)
    expert_flat = jnp.einsum(
        "ecf,efd->ecd", activated, all_expert_down, preferred_element_type=f32
    ).reshape(local_slots, D)
    routed = jnp.zeros((length, D), f32)
    for route_index in range(TOP):
        routed = (
            routed
            + jnp.take(expert_flat, local_table[:, route_index], axis=0)
            * combine_table[:, route_index : route_index + 1]
        )
    shared_gate_part = jnp.dot(normed_ffn, all_shared_gate, preferred_element_type=f32)
    shared_up_part = jnp.dot(normed_ffn, all_shared_up, preferred_element_type=f32)
    shared_sigmoid = jax.nn.sigmoid(shared_gate_part)
    shared_act = (shared_gate_part * shared_sigmoid * shared_up_part).astype(bf16)
    shared_inner = jnp.dot(shared_act, all_shared_down, preferred_element_type=f32)
    mix_gate = jax.nn.sigmoid(jnp.dot(normed_ffn, all_mix, preferred_element_type=f32))
    ffn_slice = lax.psum_scatter(
        (routed + mix_gate[:, None] * shared_inner).astype(jnp.bfloat16),
        "col",
        scatter_dimension=1,
        tiled=True,
    ).astype(jnp.float32)
    output = residual + ffn_slice
    back_weights = (
        lax.all_gather(w_query, "row", axis=0, tiled=True),
        lax.all_gather(w_key, "row", axis=0, tiled=True),
        lax.all_gather(w_value, "row", axis=0, tiled=True),
        lax.all_gather(w_out, "row", axis=1, tiled=True),
        lax.all_gather(w_router, "row", axis=0, tiled=True),
        lax.all_gather(w_shared_mix, "row", axis=0, tiled=True),
        lax.all_gather(w_expert_gate, "row", axis=1, tiled=True),
        lax.all_gather(w_expert_up, "row", axis=1, tiled=True),
        lax.all_gather(w_expert_down, "row", axis=2, tiled=True),
        lax.all_gather(w_shared_gate, "row", axis=0, tiled=True),
        lax.all_gather(w_shared_up, "row", axis=0, tiled=True),
        lax.all_gather(w_shared_down, "row", axis=1, tiled=True),
    )
    (
        all_query,
        all_key,
        all_value,
        all_out,
        all_router,
        all_mix,
        all_expert_gate,
        all_expert_up,
        all_expert_down,
        all_shared_gate,
        all_shared_up,
        all_shared_down,
    ) = back_weights
    cotangent32 = cotangent.astype(f32)
    cotangent_full = lax.all_gather(cotangent, "col", axis=1, tiled=True)
    slot_weight = (
        jnp.zeros((EXPERTS * CAP,), f32).at[slot_pair].set(gate_pair * keep_pair, mode="drop")
    )
    weight_here = lax.dynamic_slice_in_dim(slot_weight, slot_first, local_slots)
    cotangent_slot = jnp.take(cotangent_full, token_here, axis=0)
    grad_expert_out = (
        (cotangent_slot.astype(f32) * weight_here[:, None])
        .astype(bf16)
        .reshape(local_experts, CAP, D)
    )
    dots_here = jnp.sum(expert_flat * cotangent_slot.astype(f32), axis=1) * live_here
    slot_dots = lax.dynamic_update_slice_in_dim(
        jnp.zeros((EXPERTS * CAP,), f32), dots_here, slot_first, 0
    )
    mix_dots = jnp.sum(shared_inner * cotangent_full.astype(f32), axis=1)
    slot_dots, mix_dots = lax.psum((slot_dots, mix_dots), "col")
    grad_gate = (jnp.take(slot_dots, safe_slot) * keep_pair).reshape(length, TOP)
    expert_ids = jnp.arange(EXPERTS)
    grad_probs = jnp.sum(
        (routes[:, :, None] == expert_ids[None, None, :]).astype(f32) * grad_gate[:, :, None],
        axis=1,
    )
    grad_logits = router_probs * (
        grad_probs - jnp.sum(router_probs * grad_probs, axis=1, keepdims=True)
    )
    grad_mix = mix_dots * mix_gate * (1.0 - mix_gate)
    grad_act = jnp.einsum(
        "ecd,efd->ecf", grad_expert_out, all_expert_down, preferred_element_type=f32
    )
    grad_expert_down = jnp.einsum(
        "ecf,ecd->efd", activated, grad_expert_out, preferred_element_type=f32
    )
    grad_gate_in = (
        grad_act * up_part * gate_sigmoid * (1.0 + gate_part * (1.0 - gate_sigmoid))
    ).astype(bf16)
    grad_up_in = (grad_act * gate_part * gate_sigmoid).astype(bf16)
    grad_expert_gate = jnp.einsum("ecd,ecf->edf", buffer, grad_gate_in, preferred_element_type=f32)
    grad_expert_up = jnp.einsum("ecd,ecf->edf", buffer, grad_up_in, preferred_element_type=f32)
    grad_buffer = (
        jnp.einsum("ecf,edf->ecd", grad_gate_in, all_expert_gate, preferred_element_type=f32)
        + jnp.einsum("ecf,edf->ecd", grad_up_in, all_expert_up, preferred_element_type=f32)
    ).reshape(local_slots, D)
    grad_normed_ffn = jnp.zeros((length, D), f32)
    for route_index in range(TOP):
        grad_normed_ffn = (
            grad_normed_ffn
            + jnp.take(grad_buffer, local_table[:, route_index], axis=0)
            * keep_table[:, route_index : route_index + 1]
        )
    grad_inner = (mix_gate[:, None] * cotangent_full.astype(f32)).astype(bf16)
    grad_shared_down = transposed_times(shared_act, grad_inner)
    grad_shared_act = times_transposed(grad_inner, all_shared_down)
    grad_sg_in = (
        grad_shared_act
        * shared_up_part
        * shared_sigmoid
        * (1.0 + shared_gate_part * (1.0 - shared_sigmoid))
    ).astype(bf16)
    grad_su_in = (grad_shared_act * shared_gate_part * shared_sigmoid).astype(bf16)
    grad_shared_gate = transposed_times(normed_ffn, grad_sg_in)
    grad_shared_up = transposed_times(normed_ffn, grad_su_in)
    grad_normed_ffn = (
        grad_normed_ffn
        + times_transposed(grad_sg_in, all_shared_gate)
        + times_transposed(grad_su_in, all_shared_up)
    )
    grad_ffn_slice = lax.psum_scatter(
        grad_normed_ffn.astype(jnp.bfloat16), "col", scatter_dimension=1, tiled=True
    ).astype(jnp.float32)
    router_slice = lax.dynamic_slice_in_dim(all_router, col_start, part_width, 0).astype(f32)
    mix_slice = lax.dynamic_slice_in_dim(all_mix, col_start, part_width, 0).astype(f32)
    grad_ffn_slice = (
        grad_ffn_slice
        + times_transposed(grad_logits, router_slice, highest)
        + grad_mix[:, None] * mix_slice[None, :]
    )
    normed_ffn32 = normed_ffn.astype(f32)
    grad_router = transposed_times(normed_ffn32, grad_logits, highest)
    grad_mix_weight = jnp.dot(grad_mix, normed_ffn32, precision=highest)
    ffn_stat = column_total(residual * gain_ffn * grad_ffn_slice)
    grad_gain_ffn = jnp.sum(grad_ffn_slice * residual * inverse_ffn[:, None], axis=0)
    grad_residual = (
        cotangent32
        + gain_ffn * grad_ffn_slice * inverse_ffn[:, None]
        - residual * (inverse_ffn**3 * ffn_stat / D)[:, None]
    )
    grad_res_full = lax.all_gather(grad_residual.astype(bf16), "col", axis=1, tiled=True)
    grad_mixed = times_transposed(grad_res_full, all_out).astype(bf16)
    grad_out_weight = transposed_times(mixed_heads, grad_res_full)
    grad_mixed_blocks = grad_mixed.reshape(block_count, block_rows, local_heads, head_dim)

    def attend_back(carry, members):
        key_sum, value_sum = carry
        query_block, block_start, log_total, grad_block = members
        masked = block_scores(query_block, block_start)
        weights_soft = jnp.exp(masked - log_total[..., None])
        grad_soft = jnp.einsum("qhd,khd->hqk", grad_block, value_heads, preferred_element_type=f32)
        inner_sum = jnp.sum(weights_soft * grad_soft, axis=-1, keepdims=True)
        grad_scores = (weights_soft * (grad_soft - inner_sum)).astype(bf16)
        grad_query = (
            jnp.einsum("hqk,khd->qhd", grad_scores, key_rot, preferred_element_type=f32)
            * scale_factor
        )
        key_sum = (
            key_sum
            + jnp.einsum("hqk,qhd->khd", grad_scores, query_block, preferred_element_type=f32)
            * scale_factor
        )
        value_sum = value_sum + jnp.einsum(
            "hqk,qhd->khd", weights_soft.astype(bf16), grad_block, preferred_element_type=f32
        )
        return ((key_sum, value_sum), grad_query)

    zero_heads = jnp.zeros((length, local_heads, head_dim), f32)
    (grad_key_rot, grad_value), grad_query_blocks = lax.scan(
        attend_back,
        (zero_heads, zero_heads),
        (query_blocks, block_starts, log_totals, grad_mixed_blocks),
    )
    grad_query_pre = (
        rotate_back(
            grad_query_blocks.reshape(length, local_heads, head_dim), cosine_table, sine_table
        )
        .reshape(length, local_heads * head_dim)
        .astype(bf16)
    )
    grad_key_pre = (
        rotate_back(grad_key_rot, cosine_table, sine_table)
        .reshape(length, local_heads * head_dim)
        .astype(bf16)
    )
    grad_value_pre = grad_value.reshape(length, local_heads * head_dim).astype(bf16)
    grad_query_weight = transposed_times(normed, grad_query_pre)
    grad_key_weight = transposed_times(normed, grad_key_pre)
    grad_value_weight = transposed_times(normed, grad_value_pre)
    grad_bias_query = jnp.sum(grad_query_pre.astype(f32), axis=0)
    grad_bias_key = jnp.sum(grad_key_pre.astype(f32), axis=0)
    grad_bias_value = jnp.sum(grad_value_pre.astype(f32), axis=0)
    grad_normed = (
        times_transposed(grad_query_pre, all_query)
        + times_transposed(grad_key_pre, all_key)
        + times_transposed(grad_value_pre, all_value)
    )
    grad_attn_slice = lax.psum_scatter(
        grad_normed.astype(jnp.bfloat16), "col", scatter_dimension=1, tiled=True
    ).astype(jnp.float32)
    attn_stat = column_total(inputs32 * gain_attn * grad_attn_slice)
    grad_gain_attn = jnp.sum(grad_attn_slice * inputs32 * inverse_attn[:, None], axis=0)
    input_grad = (
        grad_residual
        + gain_attn * grad_attn_slice * inverse_attn[:, None]
        - inputs32 * (inverse_attn**3 * attn_stat / D)[:, None]
    )
    summed = (
        lax.psum_scatter(
            grad_query_weight.astype(jnp.bfloat16), "row", scatter_dimension=0, tiled=True
        ).astype(jnp.float32),
        lax.psum_scatter(
            grad_key_weight.astype(jnp.bfloat16), "row", scatter_dimension=0, tiled=True
        ).astype(jnp.float32),
        lax.psum_scatter(
            grad_value_weight.astype(jnp.bfloat16), "row", scatter_dimension=0, tiled=True
        ).astype(jnp.float32),
        lax.psum_scatter(
            grad_out_weight.astype(jnp.bfloat16), "row", scatter_dimension=1, tiled=True
        ).astype(jnp.float32),
        lax.psum_scatter(
            grad_router.astype(jnp.bfloat16), "row", scatter_dimension=0, tiled=True
        ).astype(jnp.float32),
        lax.psum_scatter(
            grad_mix_weight.astype(jnp.bfloat16), "row", scatter_dimension=0, tiled=True
        ).astype(jnp.float32),
        lax.psum_scatter(
            grad_expert_gate.astype(jnp.bfloat16), "row", scatter_dimension=1, tiled=True
        ).astype(jnp.float32),
        lax.psum_scatter(
            grad_expert_up.astype(jnp.bfloat16), "row", scatter_dimension=1, tiled=True
        ).astype(jnp.float32),
        lax.psum_scatter(
            grad_expert_down.astype(jnp.bfloat16), "row", scatter_dimension=2, tiled=True
        ).astype(jnp.float32),
        lax.psum_scatter(
            grad_shared_gate.astype(jnp.bfloat16), "row", scatter_dimension=0, tiled=True
        ).astype(jnp.float32),
        lax.psum_scatter(
            grad_shared_up.astype(jnp.bfloat16), "row", scatter_dimension=0, tiled=True
        ).astype(jnp.float32),
        lax.psum_scatter(
            grad_shared_down.astype(jnp.bfloat16), "row", scatter_dimension=1, tiled=True
        ).astype(jnp.float32),
    )
    small_sums = lax.psum(
        (grad_gain_attn, grad_gain_ffn, grad_bias_query, grad_bias_key, grad_bias_value), "row"
    )
    return (
        output,
        input_grad,
        small_sums[0],
        summed[0],
        summed[1],
        summed[2],
        small_sums[2],
        small_sums[3],
        small_sums[4],
        summed[3],
        small_sums[1],
        summed[4],
        summed[6],
        summed[7],
        summed[8],
        summed[9],
        summed[10],
        summed[11],
        summed[5],
    )


def solution(mesh):
    in_specs = (
        P("row", "col"),
        P("row", None),
        P("row", None),
        P("col"),
        P("row", "col"),
        P("row", "col"),
        P("row", "col"),
        P("col"),
        P("col"),
        P("col"),
        P("col", "row"),
        P("col"),
        P("row", None),
        P("col", "row", None),
        P("col", "row", None),
        P("col", None, "row"),
        P("row", "col"),
        P("row", "col"),
        P("col", "row"),
        P("row"),
        P("row", "col"),
    )
    out_specs = (
        P("row", "col"),
        P("row", "col"),
        P("col"),
        P("row", "col"),
        P("row", "col"),
        P("row", "col"),
        P("col"),
        P("col"),
        P("col"),
        P("col", "row"),
        P("col"),
        P("row", None),
        P("col", "row", None),
        P("col", "row", None),
        P("col", None, "row"),
        P("row", "col"),
        P("row", "col"),
        P("col", "row"),
        P("row"),
    )
    return jax.shard_map(local, mesh=mesh, in_specs=in_specs, out_specs=out_specs, check_vma=False)
```

profile of v0, /device:TPU:0, one launch (start us, length us, event | category | flops | bytes accessed | tf_op | source)
XLA Modules:
  0.0 2098.2 jit_solution(9739771651192432525)
XLA Ops:
  9.5 13.5 psum.77
  40.6 82.9 %all-gather.16.cloned.1.call-done = bf16[1024,2048]{1,0:T(8,128)(2,1)} async-done(((bf16[1024,512]{1,0:T(8,128)(2,1)}), bf16[1024,2048]{1,0:T(8,128)(2,1)}) %all-gather.16.cloned.1.call-update) | async-done | bytes 4194320 | tf_op jit(solution)/shard_map/all_gather | solution.py:125
  129.4 22.4 %all-gather.20.cloned.1.call-done = bf16[2048,512]{1,0:T(8,128)(2,1)} async-done(((bf16[256,512]{1,0:T(8,128)(2,1)}), bf16[2048,512]{1,0:T(8,128)(2,1)}) %all-gather.20.cloned.1.call-update) | async-done | bytes 2097168 | tf_op jit(solution)/shard_map/all_gather | solution.py:130
  163.7 17.8 all-gather.18.cloned.1.call-done
  200.2 24.8 %while.28 = (s32[]{:T(128)}, bf16[2,512,4,128]{3,1,2,0:T(8,128)(2,1)}, f32[2,4,512]{2,1,0:T(4,128)S(1)}, s32[2]{0:T(128)S(1)}, s32[1,1024]{1,0:T(1,128)S(1)}, /*...) while((s32[]{:T(128)}, ...), condition=%wide.region_5.6_spmd.clone, body=%wide.region_2.5_spmd.clone.sunk | while | flops 1100478976 | bytes 39401720 | solution.py:201
  236.0 76.1 %reduce-scatter.16.cloned.1.call-done = bf16[1024,512]{1,0:T(8,128)(2,1)} async-done(((bf16[1024,2048]{1,0:T(8,128)(2,1)}), bf16[1024,512]{1,0:T(8,128)(2,1)}) %reduce-scatter.16.cloned.1.call-update) | async-done | bytes 1048592 | tf_op jit(solution)/shard_map/reduce_scatter | solution.py:203
  357.9 15.5 scatter_custom_fusion
  373.5 15.5 scatter_custom_fusion.1
  395.1 13.6 gather_fusion.7
  408.7 68.0 %all-gather.26.cloned.1.call-done = bf16[1024,2048]{1,0:T(8,128)(2,1)} async-done(((bf16[1024,512]{1,0:T(8,128)(2,1)}), bf16[1024,2048]{1,0:T(8,128)(2,1)}) %all-gather.26.cloned.1.call-update) | async-done | bytes 4194320 | tf_op jit(solution)/shard_map/all_gather | solution.py:211
  480.0 13.4 gather_fusion.2
  498.4 46.6 %all-gather.28.cloned.1.call-done = bf16[2,2048,1408]{2,1,0:T(8,128)(2,1)} async-done(((bf16[2,256,1408]{2,1,0:T(8,128)(2,1)}), bf16[2,2048,1408]{2,1,0:T(8,128)(2,1)}) %all-gather.28.cloned.1.call-update) | async-done | bytes 11534352 | tf_op jit(solution)/shard_map/all_gather | solution.py:135
  545.0 14.3 fusion.101
  559.3 55.3 %all-gather.30.cloned.1.call-done = bf16[2,2048,1408]{2,1,0:T(8,128)(2,1)} async-done(((bf16[2,256,1408]{2,1,0:T(8,128)(2,1)}), bf16[2,2048,1408]{2,1,0:T(8,128)(2,1)}) %all-gather.30.cloned.1.call-update) | async-done | bytes 11534352 | tf_op jit(solution)/shard_map/all_gather | solution.py:136
  614.6 15.4 multiply_convert_fusion.3
  630.0 56.5 %all-gather.32.cloned.1.call-done = bf16[2,1408,2048]{2,1,0:T(8,128)(2,1)} async-done(((bf16[2,1408,256]{2,1,0:T(8,128)(2,1)}), bf16[2,1408,2048]{2,1,0:T(8,128)(2,1)}) %all-gather.32.cloned.1.call-update) | async-done | bytes 11534352 | tf_op jit(solution)/shard_map/all_gather | solution.py:137
  704.7 27.1 %all-gather.36.cloned.1.call-done = bf16[2048,1408]{1,0:T(8,128)(2,1)} async-done(((bf16[256,1408]{1,0:T(8,128)(2,1)}), bf16[2048,1408]{1,0:T(8,128)(2,1)}) %all-gather.36.cloned.1.call-update) | async-done | bytes 5767184 | tf_op jit(solution)/shard_map/all_gather | solution.py:139
  743.6 33.7 %all-gather.34.cloned.1.call-done = bf16[2048,1408]{1,0:T(8,128)(2,1)} async-done(((bf16[256,1408]{1,0:T(8,128)(2,1)}), bf16[2048,1408]{1,0:T(8,128)(2,1)}) %all-gather.34.cloned.1.call-update) | async-done | bytes 5767184 | tf_op jit(solution)/shard_map/all_gather | solution.py:138
  788.9 34.6 %all-gather.38.cloned.1.call-done = bf16[1408,2048]{1,0:T(8,128)(2,1)} async-done(((bf16[1408,256]{1,0:T(8,128)(2,1)}), bf16[1408,2048]{1,0:T(8,128)(2,1)}) %all-gather.38.cloned.1.call-update) | async-done | bytes 5767184 | tf_op jit(solution)/shard_map/all_gather | solution.py:140
  823.5 16.4 multiply_convert_fusion.4
  851.8 19.8 all-reduce.2
  871.6 23.0 %gather_fusion = f32[4096]{0:T(1024)S(1)} fusion(f32[4608]{0:T(1024)S(1)} %get-tuple-element.387, s32[4096]{0:T(1024)S(1)} %broadcast_clamp_fusion), kind=kCustom, calls=%fused_computation.10 | custom fusion | bytes 49152 | tf_op jit(solution)/shard_map/jit(_take)/gather | solution.py:303
  904.4 24.5 %gather_fusion.1 = f32[4096]{0:T(1024)S(1)} fusion(f32[1024,8]{0,1:T(8,128)S(1)} %get-tuple-element.395, s32[4096]{0:T(1024)S(1)} %copy-done.4), kind=kCustom, calls=%fused_computation.11 | custom fusion | bytes 65536 | tf_op jit(solution)/shard_map/jit(take_along_axis)/gather | solution.py:217
  931.5 15.7 scatter_custom_fusion.2
  952.9 17.4 multiply_convert_fusion.1
  970.4 13.7 fusion.106
  984.0 15.2 convolution_add_fusion
  1037.1 13.0 gather_fusion.8
  1062.2 20.7 fusion.45
  1083.7 73.4 %reduce-scatter.20.cloned.1.call-done = bf16[1024,512]{1,0:T(8,128)(2,1)} async-done(((bf16[1024,2048]{1,0:T(8,128)(2,1)}), bf16[1024,512]{1,0:T(8,128)(2,1)}) %reduce-scatter.20.cloned.1.call-update) | async-done | bytes 1048592 | tf_op jit(solution)/shard_map/reduce_scatter | solution.py:353
  1220.3 14.7 convolution_convert_fusion
  1236.9 14.6 convolution_convert_fusion.1
  1253.4 14.6 convolution_convert_fusion.2
  1281.3 43.9 %while.29 = (s32[]{:T(128)}, f32[1024,4,128]{0,2,1:T(8,128)S(1)}, f32[1024,4,128]{0,2,1:T(8,128)}, f32[2,512,4,128]{3,1,0,2:T(8,128)}, bf16[2,512,4,128]{3,1,2,0...) while((s32[]{:T(128)}, f32[1024,4,128]{0,2,1:T(8,128)S(1)}, ...), condition=%wide.region_29.32_spmd.clone, body=%wide.region_27.31_spmd.clone.sunk | while | flops 2720266752 | bytes 105978200 | solution.py:401
  1371.9 12.7 gather_fusion.6
  1384.6 12.8 gather_fusion.5
  1410.1 12.8 gather_fusion.4
  1423.0 19.4 fusion.50
  1479.4 88.0 %reduce-scatter.38.cloned.1.call-done = bf16[2,1408,256]{2,1,0:T(8,128)(2,1)} async-done(((bf16[2,1408,2048]{2,1,0:T(8,128)(2,1)}), bf16[2,1408,256]{2,1,0:T(8,128)(2,1)}) %reduce-scatter.38.cloned.1.call-update) | async-done | bytes 1441808 | tf_op jit(solution)/shard_map/reduce_scatter | solution.py:465
  1570.6 87.2 %reduce-scatter.36.cloned.1.call-done = bf16[2,256,1408]{2,1,0:T(8,128)(2,1)} async-done(((bf16[2,2048,1408]{2,1,0:T(8,128)(2,1)}), bf16[2,256,1408]{2,1,0:T(8,128)(2,1)}) %reduce-scatter.36.cloned.1.call-update) | async-done | bytes 1441808 | tf_op jit(solution)/shard_map/reduce_scatter | solution.py:462
  1661.0 87.1 %reduce-scatter.34.cloned.1.call-done = bf16[2,256,1408]{2,1,0:T(8,128)(2,1)} async-done(((bf16[2,2048,1408]{2,1,0:T(8,128)(2,1)}), bf16[2,256,1408]{2,1,0:T(8,128)(2,1)}) %reduce-scatter.34.cloned.1.call-update) | async-done | bytes 1441808 | tf_op jit(solution)/shard_map/reduce_scatter | solution.py:459
  1751.3 41.3 %reduce-scatter.30.cloned.1.call-done = bf16[512,256]{1,0:T(8,128)(2,1)} async-done(((bf16[512,2048]{1,0:T(8,128)(2,1)}), bf16[512,256]{1,0:T(8,128)(2,1)}) %reduce-scatter.30.cloned.1.call-update) | async-done | bytes 262160 | tf_op jit(solution)/shard_map/reduce_scatter | solution.py:450
  1794.3 43.1 %reduce-scatter.28.cloned.1.call-done = bf16[256,512]{1,0:T(8,128)(2,1)} async-done(((bf16[2048,512]{1,0:T(8,128)(2,1)}), bf16[256,512]{1,0:T(8,128)(2,1)}) %reduce-scatter.28.cloned.1.call-update) | async-done | bytes 262160 | tf_op jit(solution)/shard_map/reduce_scatter | solution.py:447
  1839.3 43.2 %reduce-scatter.24.cloned.1.call-done = bf16[256,512]{1,0:T(8,128)(2,1)} async-done(((bf16[2048,512]{1,0:T(8,128)(2,1)}), bf16[256,512]{1,0:T(8,128)(2,1)}) %reduce-scatter.24.cloned.1.call-update) | async-done | bytes 262160 | tf_op jit(solution)/shard_map/reduce_scatter | solution.py:441
  1884.2 43.5 %reduce-scatter.26.cloned.1.call-done = bf16[256,512]{1,0:T(8,128)(2,1)} async-done(((bf16[2048,512]{1,0:T(8,128)(2,1)}), bf16[256,512]{1,0:T(8,128)(2,1)}) %reduce-scatter.26.cloned.1.call-update) | async-done | bytes 262160 | tf_op jit(solution)/shard_map/reduce_scatter | solution.py:444
  1929.6 77.3 %reduce-scatter.22.cloned.1.call-done = bf16[1024,512]{1,0:T(8,128)(2,1)} async-done(((bf16[1024,2048]{1,0:T(8,128)(2,1)}), bf16[1024,512]{1,0:T(8,128)(2,1)}) %reduce-scatter.22.cloned.1.call-update) | async-done | bytes 1048592 | tf_op jit(solution)/shard_map/reduce_scatter | solution.py:430
  2009.0 24.2 %all-reduce.1 = (f32[512]{0:T(512)}, f32[512]{0:T(512)}, f32[512]{0:T(512)}, f32[512]{0:T(512)}, f32[512]{0:T(512)}) all-reduce(f32[512]{0:T(512)S(1)} %get-tuple-element.337, f32[512]{0:T(512)S(1)} %bitcast.282, f32[512]{0:T(512)S(1)} %bitcast.283, f32[512]{0:T(512)S(1)} %bitcast.281, ...), channel_id=1, replica_groups=mesh['row'=8,'col'=4] {'row'}, use_global_device_ids=true, to_apply=%region_34.37 | all-reduce | flops 2560 | bytes 20480 | tf_op jit(solution)/shard_map/psum | solution.py:478
  2044.9 42.0 %reduce-scatter.18.cloned.1.call-done = bf16[1024,512]{1,0:T(8,128)(2,1)} async-done(((bf16[1024,2048]{1,0:T(8,128)(2,1)}), bf16[1024,512]{1,0:T(8,128)(2,1)}) %reduce-scatter.18.cloned.1.call-update) | async-done | bytes 1048592 | tf_op jit(solution)/shard_map/reduce_scatter | solution.py:250
  (496 shorter events, 519.3 us)
Async XLA Ops:
  7.2 116.3 %copy-start.99 = (f32[512]{0:T(512)S(1)}, f32[512]{0:T(512)}, u32[]{:S(2)}) copy-start(f32[512]{0:T(512)} %param.38) | copy-start | bytes 6148
  7.2 33.4 %all-gather.22.cloned.1.call-start = ((), (), s32[]{:S(2)}) async-start(), calls=%async_computation.18 | async-start | bytes 2359296 | tf_op jit(solution)/shard_map/all_gather | solution.py:131
  7.9 115.6 %all-gather.16.cloned.1.call-start = ((), (), s32[]{:S(2)}) async-start(), calls=%async_computation.15 | async-start | bytes 5242880 | tf_op jit(solution)/shard_map/all_gather | solution.py:125
  26.1 125.8 %all-gather.20.cloned.1.call-start = ((), (), s32[]{:S(2)}) async-start(), calls=%async_computation.17 | async-start | bytes 2359296 | tf_op jit(solution)/shard_map/all_gather | solution.py:130
  26.8 154.7 %all-gather.18.cloned.1.call-start = ((), (), s32[]{:S(2)}) async-start(), calls=%async_computation.16 | async-start | bytes 2359296 | tf_op jit(solution)/shard_map/all_gather | solution.py:129
  27.4 201.5 %all-gather.24.cloned.1.call-start = ((), (), s32[]{:S(2)}) async-start(), calls=%async_computation.19 | async-start | bytes 2359296 | tf_op jit(solution)/shard_map/all_gather | solution.py:132
  28.0 284.2 %reduce-scatter.16.cloned.1.call-start = ((), (), s32[]{:S(2)}) async-start(), calls=%async_computation.20 | async-start | bytes 5242880 | tf_op jit(solution)/shard_map/reduce_scatter | solution.py:203
  31.1 120.7 %copy-start.100 = (f32[512]{0:T(512)S(1)}, f32[512]{0:T(512)}, u32[]{:S(2)}) copy-start(f32[512]{0:T(512)} %param.37) | copy-start | bytes 6148
  235.2 90.1 %copy-start.72 = (f32[512]{0:T(512)S(1)}, f32[512]{0:T(512)}, u32[]{:S(2)}) copy-start(f32[512]{0:T(512)} %param.40) | copy-start | bytes 6148
  235.2 159.9 %all-gather.40.cloned.1.call-start = ((), (), s32[]{:S(2)}) async-start(), calls=%async_computation.29 | async-start | bytes 5242880 | tf_op jit(solution)/shard_map/all_gather | solution.py:286
  236.0 240.7 %all-gather.26.cloned.1.call-start = ((), (), s32[]{:S(2)}) async-start(), calls=%async_computation.21 | async-start | bytes 5242880 | tf_op jit(solution)/shard_map/all_gather | solution.py:211
  328.0 217.0 %all-gather.28.cloned.1.call-start = ((), (), s32[]{:S(2)}) async-start(), calls=%async_computation.22 | async-start | bytes 12976128 | tf_op jit(solution)/shard_map/all_gather | solution.py:135
  328.7 285.9 %all-gather.30.cloned.1.call-start = ((), (), s32[]{:S(2)}) async-start(), calls=%async_computation.23 | async-start | bytes 12976128 | tf_op jit(solution)/shard_map/all_gather | solution.py:136
  329.3 357.3 %all-gather.32.cloned.1.call-start = ((), (), s32[]{:S(2)}) async-start(), calls=%async_computation.24 | async-start | bytes 12976128 | tf_op jit(solution)/shard_map/all_gather | solution.py:137
  330.0 401.8 %all-gather.36.cloned.1.call-start = ((), (), s32[]{:S(2)}) async-start(), calls=%async_computation.26 | async-start | bytes 6488064 | tf_op jit(solution)/shard_map/all_gather | solution.py:139
  330.6 446.6 %all-gather.34.cloned.1.call-start = ((), (), s32[]{:S(2)}) async-start(), calls=%async_computation.25 | async-start | bytes 6488064 | tf_op jit(solution)/shard_map/all_gather | solution.py:138
  331.4 492.1 %all-gather.38.cloned.1.call-start = ((), (), s32[]{:S(2)}) async-start(), calls=%async_computation.27 | async-start | bytes 6488064 | tf_op jit(solution)/shard_map/all_gather | solution.py:140
  331.9 825.2 %reduce-scatter.20.cloned.1.call-start = ((), (), s32[]{:S(2)}) async-start(), calls=%async_computation.30 | async-start | bytes 5242880 | tf_op jit(solution)/shard_map/reduce_scatter | solution.py:353
  341.9 134.7 %copy-start.43 = (bf16[8,1,256]{2,1,0:T(2,128)(2,1)}, bf16[8,1,256]{2,1,0:T(2,128)(2,1)S(1)}, u32[]{:S(2)}) copy-start(bf16[8,1,256]{2,1,0:T(2,128)(2,1)S(1)} %all-gather) | copy-start | bytes 12292
  389.2 308.1 %copy-start.69 = (pred[1152]{0:T(1024)(128)(4,1)}, pred[1152]{0:T(1024)(128)(4,1)S(1)}, u32[]{:S(2)}) copy-start(pred[1152]{0:T(1024)(128)(4,1)S(1)} %get-tuple-element.405) | copy-start | bytes 3460
  480.0 343.5 %copy-start.78 = (f32[1024]{0:T(1024)}, f32[1024]{0:T(1024)S(1)}, u32[]{:S(2)}) copy-start(f32[1024]{0:T(1024)S(1)} %add_divide_fusion.2) | copy-start | bytes 12292
  1083.0 90.1 %copy-start.65 = (f32[1024]{0:T(1024)S(1)}, f32[1024]{0:T(1024)}, u32[]{:S(2)}) copy-start(f32[1024]{0:T(1024)} %copy-done.64) | copy-start | bytes 12292
  1083.0 90.1 %copy-start.18 = (bf16[1024,512]{1,0:T(8,128)(2,1)S(1)}, bf16[1024,512]{1,0:T(8,128)(2,1)}, u32[]{:S(2)}) copy-start(bf16[1024,512]{1,0:T(8,128)(2,1)} %param.49) | copy-start | bytes 3145732
  1083.0 185.1 %all-gather.42.cloned.1.call-start = ((), (), s32[]{:S(2)}) async-start(), calls=%async_computation.31 | async-start | bytes 5242880 | tf_op jit(solution)/shard_map/all_gather | solution.py:373
  1083.7 92.6 %copy-start.76 = (f32[1024]{0:T(1024)}, f32[1024]{0:T(1024)S(1)}, u32[]{:S(2)}) copy-start(f32[1024]{0:T(1024)S(1)} %subtract_multiply_fusion.3) | copy-start | bytes 12292
  1176.4 285.3 %reduce-scatter.32.cloned.1.call-start = ((), (), s32[]{:S(2)}) async-start(), calls=%async_computation.37 | async-start | bytes 36864 | tf_op jit(solution)/shard_map/reduce_scatter | solution.py:453
  1181.1 281.8 %reduce-scatter.44.cloned.1.call-start = ((), (), s32[]{:S(2)}) async-start(), calls=%async_computation.43 | async-start | bytes 6488064 | tf_op jit(solution)/shard_map/reduce_scatter | solution.py:474
  1193.0 272.2 %reduce-scatter.40.cloned.1.call-start = ((), (), s32[]{:S(2)}) async-start(), calls=%async_computation.41 | async-start | bytes 6488064 | tf_op jit(solution)/shard_map/reduce_scatter | solution.py:468
  1205.7 271.4 %reduce-scatter.42.cloned.1.call-start = ((), (), s32[]{:S(2)}) async-start(), calls=%async_computation.42 | async-start | bytes 6488064 | tf_op jit(solution)/shard_map/reduce_scatter | solution.py:471
  1218.4 349.1 %reduce-scatter.38.cloned.1.call-start = ((), (), s32[]{:S(2)}) async-start(), calls=%async_computation.40 | async-start | bytes 12976128 | tf_op jit(solution)/shard_map/reduce_scatter | solution.py:465
  1235.1 422.7 %reduce-scatter.36.cloned.1.call-start = ((), (), s32[]{:S(2)}) async-start(), calls=%async_computation.39 | async-start | bytes 12976128 | tf_op jit(solution)/shard_map/reduce_scatter | solution.py:462
  1251.5 496.6 %reduce-scatter.34.cloned.1.call-start = ((), (), s32[]{:S(2)}) async-start(), calls=%async_computation.38 | async-start | bytes 12976128 | tf_op jit(solution)/shard_map/reduce_scatter | solution.py:459
  1268.0 524.5 %reduce-scatter.30.cloned.1.call-start = ((), (), s32[]{:S(2)}) async-start(), calls=%async_computation.36 | async-start | bytes 2359296 | tf_op jit(solution)/shard_map/reduce_scatter | solution.py:450
  1281.2 556.2 %reduce-scatter.28.cloned.1.call-start = ((), (), s32[]{:S(2)}) async-start(), calls=%async_computation.35 | async-start | bytes 2359296 | tf_op jit(solution)/shard_map/reduce_scatter | solution.py:447
  1333.9 548.5 %reduce-scatter.24.cloned.1.call-start = ((), (), s32[]{:S(2)}) async-start(), calls=%async_computation.33 | async-start | bytes 2359296 | tf_op jit(solution)/shard_map/reduce_scatter | solution.py:441
  1350.2 577.6 %reduce-scatter.26.cloned.1.call-start = ((), (), s32[]{:S(2)}) async-start(), calls=%async_computation.34 | async-start | bytes 2359296 | tf_op jit(solution)/shard_map/reduce_scatter | solution.py:444
  1357.8 649.1 %reduce-scatter.22.cloned.1.call-start = ((), (), s32[]{:S(2)}) async-start(), calls=%async_computation.32 | async-start | bytes 5242880 | tf_op jit(solution)/shard_map/reduce_scatter | solution.py:430
  1371.2 715.6 %reduce-scatter.18.cloned.1.call-start = ((), (), s32[]{:S(2)}) async-start(), calls=%async_computation.28 | async-start | bytes 5242880 | tf_op jit(solution)/shard_map/reduce_scatter | solution.py:250
  1660.9 345.9 %copy-start.11 = (bf16[1024,512]{1,0:T(8,128)(2,1)S(1)}, bf16[1024,512]{1,0:T(8,128)(2,1)}, u32[]{:S(2)}) copy-start(bf16[1024,512]{1,0:T(8,128)(2,1)} %param.29) | copy-start | bytes 3145732
  1660.9 345.9 %copy-start.46 = (f32[1024]{0:T(1024)S(1)}, f32[1024]{0:T(1024)}, u32[]{:S(2)}) copy-start(f32[1024]{0:T(1024)} %copy-done.45) | copy-start | bytes 12292
  1660.9 345.9 %copy-start.71 = (f32[512]{0:T(512)S(1)}, f32[512]{0:T(512)}, u32[]{:S(2)}) copy-start(f32[512]{0:T(512)} %param.32) | copy-start | bytes 6148
  1660.9 348.1 %copy-start.97 = (f32[512]{0:T(512)S(1)}, f32[512]{0:T(512)}, u32[]{:S(2)}) copy-start(f32[512]{0:T(512)} %get-tuple-element.335) | copy-start | bytes 6148
  1660.9 383.9 %copy-start.63 = (f32[1024]{0:T(1024)S(1)}, f32[1024]{0:T(1024)}, u32[]{:S(2)}) copy-start(f32[1024]{0:T(1024)} %copy-done.62) | copy-start | bytes 12292
  1661.0 425.9 %copy-start.15 = (bf16[1024,512]{1,0:T(8,128)(2,1)S(1)}, bf16[1024,512]{1,0:T(8,128)(2,1)}, u32[]{:S(2)}) copy-start(bf16[1024,512]{1,0:T(8,128)(2,1)} %reduce-scatter.16.cloned.1.call-done) | copy-start | bytes 3145732
  1661.0 425.9 %copy-start.19 = (bf16[1024,512]{1,0:T(8,128)(2,1)S(1)}, bf16[1024,512]{1,0:T(8,128)(2,1)}, u32[]{:S(2)}) copy-start(bf16[1024,512]{1,0:T(8,128)(2,1)} %param.49) | copy-start | bytes 3145732
  1661.0 425.9 %copy-start.51 = (f32[1024]{0:T(1024)S(1)}, f32[1024]{0:T(1024)}, u32[]{:S(2)}) copy-start(f32[1024]{0:T(1024)} %copy-done.49) | copy-start | bytes 12292
  1661.0 425.8 %copy-start.68 = (f32[1024]{0:T(1024)S(1)}, f32[1024]{0:T(1024)}, u32[]{:S(2)}) copy-start(f32[1024]{0:T(1024)} %copy-done.67) | copy-start | bytes 12292
  1661.0 425.8 %copy-start.74 = (f32[512]{0:T(512)S(1)}, f32[512]{0:T(512)}, u32[]{:S(2)}) copy-start(f32[512]{0:T(512)} %param.40) | copy-start | bytes 6148
  (101 other events, 1509.0 us)
Sparse Core Ops, SparseCore 0:
  9.9 30.5 all-gather.21
  42.7 80.7 all-gather.15
  125.4 26.4 all-gather.19
  153.6 27.8 all-gather.17
  183.2 28.1 all-gather.23
  235.3 76.7 reduce-scatter.15
  313.8 81.2 all-gather.39
  397.3 79.2 all-gather.25
  478.7 66.2 all-gather.27
  546.9 67.6 all-gather.29
  616.6 69.8 all-gather.31
  688.5 43.3 all-gather.35
  733.9 43.3 all-gather.33
  779.1 44.3 all-gather.37
  1083.1 73.9 reduce-scatter.19
  1176.5 79.1 all-gather.41
  1259.1 29.7 reduce-scatter.31
  1292.6 59.0 reduce-scatter.43
  1355.1 59.0 reduce-scatter.39
  1417.9 59.2 reduce-scatter.41
  1480.7 86.7 reduce-scatter.37
  1571.0 86.7 reduce-scatter.35
  1661.3 86.7 reduce-scatter.33
  1751.3 41.2 reduce-scatter.29
  1796.2 41.2 reduce-scatter.27
  1841.2 41.2 reduce-scatter.23
  1886.5 41.2 reduce-scatter.25
  1930.1 76.7 reduce-scatter.21
  2009.2 77.5 reduce-scatter.17
where the time goes:
time: 2110 us; the launch traced here: 2100 us
  waiting for transfers between devices  1180 us (56%)
  matrix products  370 us (18%)
  local copies, waits for them, and re-layouts  279 us (13%)
  blocking collectives  123 us (6%)
  other arithmetic  122 us (6%)
    reduce_scatter x1, waiting for transfers between devices, local(): lax.psum_scatter(grad_expert_down.astype(jnp.bfloat16), 'row', scatter_di...  88 us
    reduce_scatter x1, waiting for transfers between devices, local(): lax.psum_scatter(grad_expert_up.astype(jnp.bfloat16), 'row', scatter_dime...  87.2 us
    reduce_scatter x1, waiting for transfers between devices, local(): lax.psum_scatter(grad_expert_gate.astype(jnp.bfloat16), 'row', scatter_di...  87.1 us
    all_gather x1, waiting for transfers between devices, local(): lax.all_gather((inputs32 * inverse_attn[:, None] * gain_attn).astype(bf16...  82.9 us
    reduce_scatter x1, waiting for transfers between devices, local(): lax.psum_scatter(grad_normed.astype(jnp.bfloat16), 'col', scatter_dimensi...  77.3 us
    reduce_scatter x1, waiting for transfers between devices, local(): lax.psum_scatter(jnp.dot(mixed_heads, all_out, preferred_element_type=f32...  76.1 us
    reduce_scatter x1, waiting for transfers between devices, local(): lax.psum_scatter(grad_normed_ffn.astype(jnp.bfloat16), 'col', scatter_dim...  73.4 us
    dot_general x8, matrix products, times_transposed(): lax.dot_general(left_side, right_side, (((1,), (1,)), ((), ())), precisio...  72.3 us
  transfers between devices with their start and end apart: 29, of which 24 were waited for; matrix products, arithmetic and copies ran while one was open for 24% of the time, Pallas kernels for 0%

commit v1 on v0

v1 whole, which is shorter than its diff:
```python
import functools

import jax
import jax.numpy as jnp
from jax import lax
from jax.experimental import pallas as pl
from jax.experimental.pallas import tpu as pltpu
from jax.sharding import PartitionSpec as P

HEAD_DIM = 128
EXPERTS = 8
TOP = 4
CAP = 576
SPAN = 256

EPSILON = 1e-06
THETA = 1000000.0
NEGATIVE = -1e30

f32 = jnp.float32
bf16 = jnp.bfloat16


def dot_nn(left, right):
    return jnp.dot(left, right, preferred_element_type=f32)


def dot_nt(left, right):
    return lax.dot_general(left, right, (((1,), (1,)), ((), ())), preferred_element_type=f32)


def dot_tn(left, right):
    return lax.dot_general(left, right, (((0,), (0,)), ((), ())), preferred_element_type=f32)


def batch_nn(left, right):
    return jnp.einsum("ecd,edf->ecf", left, right, preferred_element_type=f32)


def batch_nt(left, right):
    return jnp.einsum("ecf,edf->ecd", left, right, preferred_element_type=f32)


def batch_tn(left, right):
    return jnp.einsum("ecd,ecf->edf", left, right, preferred_element_type=f32)


def line_gather(block, count, me):
    width = block.shape[1]
    full = jnp.zeros((block.shape[0], count * width), block.dtype)
    full = lax.dynamic_update_slice_in_dim(full, block, me * width, 1)
    up = down = block
    for step in range(1, count):
        up = lax.ppermute(up, "col", [(i, i + 1) for i in range(step - 1, count - 1)])
        down = lax.ppermute(down, "col", [(i, i - 1) for i in range(1, count - step + 1)])
        from_below = me >= step
        from_above = me + step < count
        full = lax.dynamic_update_slice_in_dim(
            full, jnp.where(from_below, up, block), jnp.where(from_below, me - step, me) * width, 1
        )
        full = lax.dynamic_update_slice_in_dim(
            full, jnp.where(from_above, down, block), jnp.where(from_above, me + step, me) * width, 1
        )
    return full


def line_scatter(partial, count, me):
    width = partial.shape[1] // count

    def block(index):
        return lax.dynamic_slice_in_dim(partial, index * width, width, 1)

    up = down = None
    for far in range(count - 1, 0, -1):
        up_out, down_out = block(me + far), block(me - far)
        if up is not None:
            up_out = (up_out.astype(f32) + up.astype(f32)).astype(bf16)
            down_out = (down_out.astype(f32) + down.astype(f32)).astype(bf16)
        up = lax.ppermute(up_out, "col", [(i, i + 1) for i in range(count - far)])
        down = lax.ppermute(down_out, "col", [(i, i - 1) for i in range(far, count)])
    return block(me).astype(f32) + up.astype(f32) + down.astype(f32)


def all_of_col(block, count, me):
    full = jnp.zeros((count,) + block.shape, block.dtype)
    full = lax.dynamic_update_slice_in_dim(full, block[None], me, 0)
    for step in range(1, count):
        got = lax.ppermute(block, "col", [(i, (i + step) % count) for i in range(count)])
        full = lax.dynamic_update_slice_in_dim(full, got[None], lax.rem(me + count - step, count), 0)
    return full


def spans(length):
    return [(max(0, first - SPAN), first, first + SPAN) for first in range(0, length, SPAN)]


def turned(values, cosine, sine):
    return values * cosine + pltpu.roll(values, HEAD_DIM // 2, 1) * sine


def turned_back(values, cosine, sine):
    return values * cosine - pltpu.roll(values, HEAD_DIM // 2, 1) * sine


def soft_weights(query, key, seg_col, seg_row, low, first, high):
    scores = dot_nt(query, key) * HEAD_DIM ** (-0.5)
    shape = (high - first, high - low)
    at_query = first + lax.broadcasted_iota(jnp.int32, shape, 0)
    at_key = low + lax.broadcasted_iota(jnp.int32, shape, 1)
    allowed = (at_key <= at_query) & (seg_col[first:high, :] == seg_row[:, low:high])
    scores = jnp.where(allowed, scores, NEGATIVE)
    weights = jnp.exp(scores - jnp.max(scores, axis=1, keepdims=True))
    return weights / jnp.sum(weights, axis=1, keepdims=True)


def attend_kernel(pre, bias, cosine, sine, seg_col, seg_row, mixed, turned_out):
    length = pre.shape[0]
    d = HEAD_DIM
    pre_q = pre[:, :d] + bias[:, :d]
    pre_k = pre[:, d : 2 * d] + bias[:, d : 2 * d]
    turned_out[:, :d] = turned(pre_q, cosine[...], sine[...]).astype(bf16)
    turned_out[:, d : 2 * d] = turned(pre_k, cosine[...], sine[...]).astype(bf16)
    turned_out[:, 2 * d :] = (pre[:, 2 * d :] + bias[:, 2 * d :]).astype(bf16)
    for low, first, high in spans(length):
        weights = soft_weights(
            turned_out[first:high, :d], turned_out[low:high, d : 2 * d], seg_col, seg_row, low, first, high
        )
        mixed[first:high, :] = dot_nn(weights.astype(bf16), turned_out[low:high, 2 * d :]).astype(bf16)


def attend_back_kernel(heads, cosine, sine, seg_col, seg_row, grad_mixed, grad_pre, grad_bias, key_sum, value_sum):
    length = heads.shape[0]
    d = HEAD_DIM
    scale = d ** (-0.5)
    key_sum[...] = jnp.zeros_like(key_sum)
    value_sum[...] = jnp.zeros_like(value_sum)
    query_bias = jnp.zeros((1, d), f32)
    for low, first, high in spans(length):
        query, key, value = heads[first:high, :d], heads[low:high, d : 2 * d], heads[low:high, 2 * d :]
        grad = grad_mixed[first:high, :]
        weights = soft_weights(query, key, seg_col, seg_row, low, first, high)
        grad_soft = dot_nt(grad, value)
        inner = jnp.sum(weights * grad_soft, axis=1, keepdims=True)
        grad_scores = (weights * (grad_soft - inner)).astype(bf16)
        grad_query = dot_nn(grad_scores, key) * scale
        grad_query = turned_back(grad_query, cosine[first:high, :], sine[first:high, :]).astype(bf16)
        grad_pre[first:high, :d] = grad_query
        query_bias += jnp.sum(grad_query.astype(f32), axis=0, keepdims=True)
        key_sum[low:high, :] += dot_tn(grad_scores, query) * scale
        value_sum[low:high, :] += dot_tn(weights.astype(bf16), grad)
    grad_key = turned_back(key_sum[...], cosine[...], sine[...]).astype(bf16)
    grad_value = value_sum[...].astype(bf16)
    grad_pre[:, d : 2 * d] = grad_key
    grad_pre[:, 2 * d :] = grad_value
    grad_bias[:, :d] = query_bias
    grad_bias[:, d : 2 * d] = jnp.sum(grad_key.astype(f32), axis=0, keepdims=True)
    grad_bias[:, 2 * d :] = jnp.sum(grad_value.astype(f32), axis=0, keepdims=True)


def head_spec(rows, width):
    return pl.BlockSpec((rows, width), lambda h: (0, h))


def whole_spec(array):
    return pl.BlockSpec(array.shape, lambda h: (0, 0))


def attend(pre, bias, cosine, sine, seg_col, seg_row):
    length, width = pre.shape
    heads = width // (3 * HEAD_DIM)
    return pl.pallas_call(
        attend_kernel,
        grid=(heads,),
        in_specs=[
            head_spec(length, 3 * HEAD_DIM),
            head_spec(1, 3 * HEAD_DIM),
            whole_spec(cosine),
            whole_spec(sine),
            whole_spec(seg_col),
            whole_spec(seg_row),
        ],
        out_specs=[head_spec(length, HEAD_DIM), head_spec(length, 3 * HEAD_DIM)],
        out_shape=[
            jax.ShapeDtypeStruct((length, heads * HEAD_DIM), bf16),
            jax.ShapeDtypeStruct((length, width), bf16),
        ],
        compiler_params=pltpu.CompilerParams(vmem_limit_bytes=32 << 20),
        cost_estimate=pl.CostEstimate(
            flops=heads * length * 2 * SPAN * HEAD_DIM * 4, bytes_accessed=10 * length * width, transcendentals=0
        ),
    )(pre, bias, cosine, sine, seg_col, seg_row)


def attend_back(heads_pre, cosine, sine, seg_col, seg_row, grad_mixed):
    length, width = heads_pre.shape
    heads = width // (3 * HEAD_DIM)
    return pl.pallas_call(
        attend_back_kernel,
        grid=(heads,),
        in_specs=[
            head_spec(length, 3 * HEAD_DIM),
            whole_spec(cosine),
            whole_spec(sine),
            whole_spec(seg_col),
            whole_spec(seg_row),
            head_spec(length, HEAD_DIM),
        ],
        out_specs=[head_spec(length, 3 * HEAD_DIM), head_spec(1, 3 * HEAD_DIM)],
        out_shape=[
            jax.ShapeDtypeStruct((length, width), bf16),
            jax.ShapeDtypeStruct((1, width), f32),
        ],
        scratch_shapes=[pltpu.VMEM((length, HEAD_DIM), f32), pltpu.VMEM((length, HEAD_DIM), f32)],
        compiler_params=pltpu.CompilerParams(vmem_limit_bytes=32 << 20),
        cost_estimate=pl.CostEstimate(
            flops=heads * length * 2 * SPAN * HEAD_DIM * 10, bytes_accessed=8 * length * width, transcendentals=0
        ),
    )(heads_pre, cosine, sine, seg_col, seg_row, grad_mixed)


def rotary_tables(length):
    position = jnp.arange(length).astype(f32)
    exponent = jnp.arange(HEAD_DIM // 2).astype(f32) * (2.0 / HEAD_DIM)
    angles = position[:, None] * jnp.exp(-exponent * jnp.log(THETA))[None, :]
    cosine, sine = jnp.cos(angles), jnp.sin(angles)
    return jnp.concatenate([cosine, cosine], 1), jnp.concatenate([-sine, sine], 1)


def by_head(parts):
    rows = parts[0].shape[0]
    split = [part.reshape(rows, -1, 1, HEAD_DIM) for part in parts]
    return jnp.concatenate(split, axis=2).reshape(rows, -1)


def from_heads(joined):
    split = joined.reshape(joined.shape[0], -1, 3, HEAD_DIM)
    return [split[:, :, i].reshape(joined.shape[0], -1) for i in range(3)]


def two_terms(values):
    high = values.astype(bf16)
    return high, (values - high.astype(f32)).astype(bf16)


def local(
    rows,
    cols,
    inputs,
    segments,
    routes,
    gain_attn,
    w_query,
    w_key,
    w_value,
    b_query,
    b_key,
    b_value,
    w_out,
    gain_ffn,
    w_router,
    w_expert_gate,
    w_expert_up,
    w_expert_down,
    w_shared_gate,
    w_shared_up,
    w_shared_down,
    w_shared_mix,
    cotangent,
):
    length, part = inputs.shape
    width = part * cols
    experts, depth, hidden = w_expert_gate.shape
    hidden_shared = w_shared_gate.shape[1]
    head_width = w_query.shape[1]
    alike = hidden == hidden_shared
    col = lax.axis_index("col")
    row = lax.axis_index("row")

    def mine(array, axis=1):
        return lax.dynamic_slice_in_dim(array, col * part, part, axis)

    all_heads = lax.all_gather(by_head([w_query, w_key, w_value]), "row", axis=0, tiled=True)
    out_rows = line_gather(w_out.T, cols, col).T
    all_out = lax.all_gather(out_rows, "row", axis=1, tiled=True)
    expert_in = jnp.concatenate([w_expert_gate, w_expert_up], axis=2)
    shared_in = jnp.concatenate([w_shared_gate, w_shared_up], axis=1)[None]
    shared_down = w_shared_down[None]
    if alike:
        all_in = lax.all_gather(jnp.concatenate([expert_in, shared_in], 0), "row", axis=1, tiled=True)
        all_down = lax.all_gather(jnp.concatenate([w_expert_down, shared_down], 0), "row", axis=2, tiled=True)
        expert_in, shared_in = all_in[:experts], all_in[experts]
        expert_down, shared_down = all_down[:experts], all_down[experts]
    else:
        expert_in = lax.all_gather(expert_in, "row", axis=1, tiled=True)
        shared_in = lax.all_gather(shared_in, "row", axis=1, tiled=True)[0]
        expert_down = lax.all_gather(w_expert_down, "row", axis=2, tiled=True)
        shared_down = lax.all_gather(shared_down, "row", axis=2, tiled=True)[0]
    w_small = jnp.concatenate([w_router, w_shared_mix[:, None]], 1)
    all_small = lax.all_gather(w_small, "row", axis=0, tiled=True)
    gains = lax.all_gather(jnp.stack([gain_attn, gain_ffn]), "col", axis=1, tiled=True)

    named = jnp.any(routes[:, :, None] == jnp.arange(EXPERTS)[None, None, :], axis=1)
    at = jnp.arange(length)
    earlier = (at[None, :] < at[:, None]).astype(bf16)
    place = dot_nn(earlier, named.astype(bf16))
    kept = named & (place < CAP)
    place_here = lax.dynamic_slice_in_dim(jnp.where(kept, place, -1.0), col * experts, experts, 1)
    slots = (place_here[:, :, None] == jnp.arange(CAP).astype(f32)[None, None, :]).astype(bf16)
    slots = slots.reshape(length, experts * CAP)

    cosine, sine = rotary_tables(length)
    seg_row = segments
    seg_col = segments.T

    inputs_full = line_gather(inputs, cols, col)
    inputs_wide = inputs_full.astype(f32)
    inverse_attn = lax.rsqrt(jnp.mean(inputs_wide * inputs_wide, axis=1, keepdims=True) + EPSILON)
    normed = (inputs_wide * inverse_attn * gains[0][None, :]).astype(bf16)
    bias = by_head([b_query[None], b_key[None], b_value[None]])
    mixed, heads_pre = attend(dot_nn(normed, all_heads), bias, cosine, sine, seg_col, seg_row)
    mixed_full = line_gather(mixed, cols, col)
    residual = inputs_wide + dot_nn(mixed_full, all_out)
    inverse_ffn = lax.rsqrt(jnp.mean(residual * residual, axis=1, keepdims=True) + EPSILON)
    normed_ffn = (residual * inverse_ffn * gains[1][None, :]).astype(bf16)
    residual_mine = mine(residual)

    cotangent_full = line_gather(cotangent, cols, col)

    logits = dot_nn(normed_ffn, all_small)
    probs = jax.nn.softmax(logits[:, :EXPERTS], axis=-1)
    mix_gate = jax.nn.sigmoid(logits[:, EXPERTS:])
    probs_here = lax.dynamic_slice_in_dim(probs, col * experts, experts, 1)
    slot_gates = sum(dot_tn(slots, term) for term in two_terms(probs_here))
    slot_gate = jnp.concatenate(
        [slot_gates[e * CAP : (e + 1) * CAP, e : e + 1][None] for e in range(experts)], axis=0
    )

    buffer = dot_tn(slots, normed_ffn).astype(bf16).reshape(experts, CAP, width)
    expert_pre = batch_nn(buffer, expert_in).astype(bf16)
    shared_pre = dot_nn(normed_ffn, shared_in).astype(bf16)

    def halves(pre):
        half = pre.shape[-1] // 2
        return pre[..., :half].astype(f32), pre[..., half:].astype(f32)

    def activated(pre, scale):
        gate, up = halves(pre)
        return (gate * jax.nn.sigmoid(gate) * up * scale).astype(bf16)

    expert_act = activated(expert_pre, slot_gate)
    shared_act = activated(shared_pre, mix_gate)
    cotangent_slot = dot_tn(slots, cotangent_full).astype(bf16).reshape(experts, CAP, width)
    grad_expert_down = batch_tn(expert_act, cotangent_slot).astype(bf16)
    grad_shared_down = dot_tn(shared_act, cotangent_full).astype(bf16)[None]
    expert_out = batch_nn(expert_act, expert_down).astype(bf16).reshape(experts * CAP, width)
    ffn_partial = (dot_nn(slots, expert_out) + dot_nn(shared_act, shared_down)).astype(bf16)
    output = residual_mine + line_scatter(ffn_partial, cols, col)

    def pre_back(pre, grad_act, scale):
        gate, up = halves(pre)
        sigmoid = jax.nn.sigmoid(gate)
        silu = gate * sigmoid
        dots = jnp.sum(silu * up * grad_act, axis=-1)
        scaled = grad_act * scale
        grad_gate = scaled * up * sigmoid * (1.0 + gate * (1.0 - sigmoid))
        grad_up = scaled * silu
        stat = jnp.sum(grad_gate * gate + grad_up * up, axis=-1)
        return jnp.concatenate([grad_gate.astype(bf16), grad_up.astype(bf16)], axis=-1), dots, stat

    grad_expert_pre, expert_dots, expert_stat = pre_back(
        expert_pre, batch_nt(cotangent_slot, expert_down), slot_gate
    )
    grad_shared_pre, shared_dots, shared_stat = pre_back(
        shared_pre, dot_nt(cotangent_full, shared_down), mix_gate
    )
    grad_buffer = batch_nt(grad_expert_pre, expert_in).astype(bf16).reshape(experts * CAP, width)
    grad_partial = (dot_nn(slots, grad_buffer) + dot_nt(grad_shared_pre, shared_in)).astype(bf16)
    grad_expert_in = batch_tn(buffer, grad_expert_pre).astype(bf16)
    grad_shared_in = dot_tn(normed_ffn, grad_shared_pre).astype(bf16)[None]

    told = []
    stat_sum = shared_stat
    for e in range(experts):
        terms = jnp.stack([*two_terms(expert_dots[e]), *two_terms(expert_stat[e])], axis=1)
        found = dot_nn(slots[:, e * CAP : (e + 1) * CAP], terms)
        told.append(found[:, 0] + found[:, 1])
        stat_sum = stat_sum + found[:, 2] + found[:, 3]
    told = all_of_col(jnp.stack([*told, shared_dots, stat_sum]), cols, col)
    grad_probs = told[:, :experts].reshape(EXPERTS, length).T
    grad_mix = jnp.sum(told[:, experts], axis=0)[:, None] * mix_gate * (1.0 - mix_gate)
    grad_logits = probs * (grad_probs - jnp.sum(probs * grad_probs, axis=1, keepdims=True))
    grad_small = jnp.concatenate([grad_logits, grad_mix], axis=1)
    ffn_stat = (
        jnp.sum(told[:, experts + 1], axis=0)[:, None] + jnp.sum(grad_small * logits, axis=1, keepdims=True)
    ) / inverse_ffn

    grad_ffn = line_scatter(grad_partial, cols, col) + dot_nt(
        grad_small.astype(bf16), mine(all_small, 0)
    )
    grad_gain_ffn = jnp.sum(grad_ffn * residual_mine * inverse_ffn, axis=0)
    grad_residual = (
        cotangent.astype(f32)
        + gain_ffn[None, :] * grad_ffn * inverse_ffn
        - residual_mine * (inverse_ffn**3 * ffn_stat / width)
    )
    grad_res_full = line_gather(grad_residual.astype(bf16), cols, col)

    out_mine = lax.dynamic_slice_in_dim(all_out, col * head_width, head_width, 0)
    grad_mixed = dot_nt(grad_res_full, out_mine).astype(bf16)
    grad_out = dot_tn(grad_res_full, mixed).astype(bf16)
    grad_heads, grad_bias = attend_back(heads_pre, cosine, sine, seg_col, seg_row, grad_mixed)
    normed_partial = dot_nt(grad_heads, all_heads).astype(bf16)
    weighed = normed_partial.astype(f32) * inputs_wide
    attn_stat = jnp.sum(all_of_col(jnp.sum(weighed * gains[0][None, :], axis=1)[None], cols, col), axis=0)
    grad_gain_attn = jnp.sum(weighed * inverse_attn, axis=0)
    grad_qkv = dot_tn(normed, grad_heads).astype(bf16)
    grad_attn = line_scatter(normed_partial, cols, col)
    inputs_mine = inputs.astype(f32)
    input_grad = (
        grad_residual
        + gain_attn[None, :] * grad_attn * inverse_attn
        - inputs_mine * (inverse_attn**3 * attn_stat.reshape(-1, 1) / width)
    )

    def scattered(values, axis):
        return lax.psum_scatter(values, "row", scatter_dimension=axis, tiled=True).astype(f32)

    if alike:
        down = scattered(jnp.concatenate([grad_expert_down, grad_shared_down], 0), 2)
        into = scattered(jnp.concatenate([grad_expert_in, grad_shared_in], 0), 1)
        grad_expert_down, grad_shared_down = down[:experts], down[experts]
        grad_expert_in, grad_shared_in = into[:experts], into[experts]
    else:
        grad_expert_down = scattered(grad_expert_down, 2)
        grad_shared_down = scattered(grad_shared_down, 2)[0]
        grad_expert_in = scattered(grad_expert_in, 1)
        grad_shared_in = scattered(grad_shared_in, 1)[0]
    attention = scattered(jnp.concatenate([grad_qkv, grad_out], 1), 0)
    grad_query, grad_key, grad_value = from_heads(attention[:, : 3 * head_width])
    grad_out = attention[:, 3 * head_width :].T

    grad_small_weights = lax.psum(dot_tn(grad_small.astype(bf16), normed_ffn), "row")
    grad_small_weights = lax.dynamic_slice_in_dim(grad_small_weights, row * depth, depth, 1)
    spread = jnp.zeros((4, width), f32)
    vectors = jnp.concatenate([grad_gain_ffn[None], jnp.stack(from_heads(grad_bias))[:, 0]], 0)
    spread = lax.dynamic_update_slice_in_dim(spread, vectors, col * part, 1)
    sums = mine(lax.psum(jnp.concatenate([grad_gain_attn[None], spread], 0), ("row", "col")))
    return (
        output,
        input_grad,
        sums[0],
        grad_query,
        grad_key,
        grad_value,
        sums[2],
        sums[3],
        sums[4],
        grad_out,
        sums[1],
        grad_small_weights[:EXPERTS].T,
        grad_expert_in[:, :, :hidden],
        grad_expert_in[:, :, hidden:],
        grad_expert_down,
        grad_shared_in[:, :hidden_shared],
        grad_shared_in[:, hidden_shared:],
        grad_shared_down,
        grad_small_weights[EXPERTS],
    )


def solution(mesh):
    in_specs = (
        P("row", "col"),
        P("row", None),
        P("row", None),
        P("col"),
        P("row", "col"),
        P("row", "col"),
        P("row", "col"),
        P("col"),
        P("col"),
        P("col"),
        P("col", "row"),
        P("col"),
        P("row", None),
        P("col", "row", None),
        P("col", "row", None),
        P("col", None, "row"),
        P("row", "col"),
        P("row", "col"),
        P("col", "row"),
        P("row"),
        P("row", "col"),
    )
    out_specs = (
        P("row", "col"),
        P("row", "col"),
        P("col"),
        P("row", "col"),
        P("row", "col"),
        P("row", "col"),
        P("col"),
        P("col"),
        P("col"),
        P("col", "row"),
        P("col"),
        P("row", None),
        P("col", "row", None),
        P("col", "row", None),
        P("col", None, "row"),
        P("row", "col"),
        P("row", "col"),
        P("col", "row"),
        P("row"),
    )
    body = functools.partial(local, mesh.shape["row"], mesh.shape["col"])
    return jax.shard_map(body, mesh=mesh, in_specs=in_specs, out_specs=out_specs, check_vma=False)
```

time: 2110 us -> 1160 us (0.55)
  waiting for transfers between devices: 1180 us -> 393 us
  local copies, waits for them, and re-layouts: 279 us -> 50.5 us
  starting transfers between devices: 1.63 us -> 134 us
  matrix products: 370 us -> 313 us
  blocking collectives: 123 us -> 90.6 us
  Pallas kernels: 0 us -> 25.9 us
    reduce_scatter x15 -> x3, waiting for transfers between devices: 712 us -> 52.5 us  [scattered(): lax.psum_scatter(values, 'row', scatter_dimension=axis, tiled=True)]
    all_gather x14 -> x4, waiting for transfers between devices: 460 us -> 23.7 us  [the longest x1 23.7 us: local(): lax.all_gather(jnp.concatenate([w_expert_down, shared_down], 0), 'row', a...]
    ppermute x0 -> x54, waiting for transfers between devices: none -> 317 us  [the longest x15 149 us: line_gather(): lax.ppermute(down, 'col', [(i, i - 1) for i in range(1, count - step + 1)])]
    gather x18 -> x0, local copies, waits for them, and re-layouts: 179 us -> none  [the longest x4 51 us: local(): jnp.take(expert_flat, local_table[:, route_index], axis=0)]
    ppermute x0 -> x54, starting transfers between devices: none -> 133 us  [the longest x15 35.5 us: line_gather(): lax.ppermute(up, 'col', [(i, i + 1) for i in range(step - 1, count - 1)])]
    dot_general x49 -> x29, matrix products: 370 us -> 313 us  [the longest x10 88.5 us: dot_nn(): return jnp.dot(left, right, preferred_element_type=f32)]
    psum x6 -> x1, blocking collectives: 90.9 us -> 40.3 us  [local(): lax.psum(jnp.concatenate([grad_gain_attn[None], spread], 0), ('row', 'col'))]
    concatenate x2 -> x10, other arithmetic: 1.16 us -> 50.4 us  [the longest x1 27.5 us: local(): into = scattered(jnp.concatenate([grad_expert_in, grad_shared_in], 0), 1)]
  transfers between devices with their start and end apart: 29 -> 62, of which waited for: 24 -> 27; matrix products, arithmetic and copies ran while one was open for 24% -> 31% of each run, Pallas kernels for 0% -> 2%
where the time goes in v1:
time: 1160 us; the launch traced here: 1150 us
  waiting for transfers between devices  393 us (34%)
  matrix products  313 us (27%)
  starting transfers between devices  134 us (12%)
  other arithmetic  122 us (11%)
  blocking collectives  90.6 us (8%)
  local copies, waits for them, and re-layouts  50.5 us (4%)
  Pallas kernels  25.9 us (2%)
  between operations  16.3 us (1%)
    ppermute x15, waiting for transfers between devices, line_gather(): lax.ppermute(down, 'col', [(i, i - 1) for i in range(1, count - step + 1)])  149 us
    ppermute x9, waiting for transfers between devices, line_scatter(): up = lax.ppermute(up_out, 'col', [(i, i + 1) for i in range(count - far)])  123 us
    dot_general x10, matrix products, dot_nn(): return jnp.dot(left, right, preferred_element_type=f32)  88.5 us
    dot_general x9, matrix products, dot_tn(): lax.dot_general(left, right, (((0,), (0,)), ((), ())), preferred_element_...  65.2 us
    dot_general x5, matrix products, dot_nt(): lax.dot_general(left, right, (((1,), (1,)), ((), ())), preferred_element_...  56.7 us
    reduce_scatter x3, waiting for transfers between devices, scattered(): lax.psum_scatter(values, 'row', scatter_dimension=axis, tiled=True)  52.5 us
    dot_general x2, matrix products, batch_tn(): return jnp.einsum('ecd,ecf->edf', left, right, preferred_element_type=f32)  43.5 us
    all_gather x1, blocking collectives, local(): lax.all_gather(jnp.stack([gain_attn, gain_ffn]), 'col', axis=1, tiled=True)  40.8 us
  transfers between devices with their start and end apart: 62, of which 27 were waited for; matrix products, arithmetic and copies ran while one was open for 31% of the time, Pallas kernels for 2%

profile of v1, /device:TPU:0, one launch (start us, length us, event | category | flops | bytes accessed | tf_op | source)
XLA Modules:
  0.0 1145.9 jit_solution(2553436581982901419)
XLA Ops:
  68.1 40.8 %all_gather.18 = f32[2,2048]{1,0:T(2,128)S(1)} all-gather(f32[2,512]{1,0:T(2,128)S(1)} %pad_maximum_fusion.20), channel_id=1, replica_groups=mesh['row'=8,'col'=4] {'col'}, dimensions={1}, use_global_device_ids=true | all-gather | bytes 20480 | tf_op jit(solution)/shard_map/all_gather | solution.py:300
  119.5 9.5 all_gather.22
  141.0 18.8 %collective-permute-done.3 = bf16[1024,512]{1,0:T(8,128)(2,1)S(1)} collective-permute-done((bf16[1024,512]{1,0:T(8,128)(2,1)}, bf16[1024,512]{1,0:T(8,128)(2,1)S(1)}, u32[]{:S(2)}, u32[]{:S(2)}) %collective-permute-start.3) | collective-permute-done | bytes 1048608 | tf_op jit(solution)/shard_map/ppermute | solution.py:55
  162.8 19.7 %collective-permute-done.27 = bf16[1024,512]{1,0:T(8,128)(2,1)} collective-permute-done((bf16[1024,512]{1,0:T(8,128)(2,1)}, bf16[1024,512]{1,0:T(8,128)(2,1)}, u32[]{:S(2)}, u32[]{:S(2)}) %collective-permute-start.27) | collective-permute-done | bytes 1048608 | tf_op jit(solution)/shard_map/ppermute | solution.py:55
  186.7 18.1 %collective-permute-done.5 = bf16[1024,512]{1,0:T(8,128)(2,1)S(1)} collective-permute-done((bf16[1024,512]{1,0:T(8,128)(2,1)S(1)}, bf16[1024,512]{1,0:T(8,128)(2,1)S(1)}, u32[]{:S(2)}, u32[]{:S(2)}) %collective-permute-start.5) | collective-permute-done | bytes 1048608 | tf_op jit(solution)/shard_map/ppermute | solution.py:55
  208.7 10.1 fusion.68.pre
  218.8 11.8 %shard_map.348 = (bf16[1024,512]{1,0:T(8,128)(2,1)S(1)}, bf16[1024,1536]{1,0:T(8,128)(2,1)S(1)}) custom-call(f32[1024,1536]{1,0:T(8,128)S(1)} %fusion.68.pre, f32[1,1536]{1,0:T(1,128)S(1)} %reshape.346.bias, f32[1024,128]{1,0:T(8,128)S(1)} %get-tuple-element.90.cosine, f32[1024,128]{1,0:T(8,128)S(1)} %get-tuple-element.91.sine, s32[1024,1]{1,0:T(8,128)S(1)} %copy.56.seg_col, ...), custom_call_target="tpu_custom_call" | custom-call | flops 1073741824 | bytes 15728640 | tf_op jit(solution)/shard_map/pallas_call | solution.py:171
  244.8 12.5 %collective-permute-done.7 = bf16[1024,512]{1,0:T(8,128)(2,1)S(1)} collective-permute-done((bf16[1024,512]{1,0:T(8,128)(2,1)S(1)}, bf16[1024,512]{1,0:T(8,128)(2,1)S(1)}, u32[]{:S(2)}, u32[]{:S(2)}) %collective-permute-start.7) | collective-permute-done | bytes 1048608 | tf_op jit(solution)/shard_map/ppermute | solution.py:55
  259.3 9.0 convolution_convert_fusion.2
  274.2 9.0 collective-permute-done.9
  289.7 19.7 %collective-permute-done.11 = bf16[1024,512]{1,0:T(8,128)(2,1)S(1)} collective-permute-done((bf16[1024,512]{1,0:T(8,128)(2,1)S(1)}, bf16[1024,512]{1,0:T(8,128)(2,1)S(1)}, u32[]{:S(2)}, u32[]{:S(2)}) %collective-permute-start.11) | collective-permute-done | bytes 1048608 | tf_op jit(solution)/shard_map/ppermute | solution.py:55
  310.8 13.3 %multiply_reduce_fusion.2 = (f32[1024]{0:T(1024)S(1)}, f32[1024,2048]{1,0:T(8,128)S(1)}) fusion(bf16[1024,2048]{1,0:T(8,128)(2,1)} %select_dynamic-update-slice_fusion.12, bf16[2048,2048]{1,0:T(8,128)(2,1)} %all-gather.7.cloned.1.call-done, bf16[1024,2048]{1,0:T(8,128)(2,1)} %copy-done.22), kind=kOutput, calls=%fused_computation.45 | convolution fusion | flops 8598322176 | bytes 25169920 | tf_op jit(solution)/shard_map/dot_general | solution.py:25
  337.9 23.2 %fusion.24 = bf16[2,576,2816]{2,1,0:T(8,128)(2,1)} fusion(bf16[2,576,2048]{2,1,0:T(8,128)(2,1)} %bitcast.246, bf16[3,2048,2816]{2,1,0:T(8,128)(2,1)} %all-gather.9.cloned.1.call-done), kind=kOutput, calls=%fused_computation.63 | convolution fusion | flops 13290799104 | bytes 34275328 | tf_op jit(solution)/shard_map/ecd,edf->ecf/dot_general | solution.py:37
  361.1 23.7 %all-gather.11.cloned.1.call-done = bf16[3,1408,2048]{2,1,0:T(8,128)(2,1)} async-done(((bf16[3,1408,256]{2,1,0:T(8,128)(2,1)}), bf16[3,1408,2048]{2,1,0:T(8,128)(2,1)}) %all-gather.11.cloned.1.call-update) | async-done | bytes 17301520 | tf_op jit(solution)/shard_map/all_gather | solution.py:290
  384.8 16.0 %multiply_reduce_fusion.3 = (f32[2,576]{1,0:T(2,128)S(1)}, f32[2,576]{1,0:T(2,128)S(1)}, bf16[2,576,1408]{2,1,0:T(8,128)(2,1)}, bf16[2,576,1408]{2,1,0:T(8,128)(2,1)}) fusion(bf16[2,576,2816]{2,1,0:T(8,128)(2,1)} %fusion.24, f32[2,576]{1,0:T(2,128)S(1)} %maximum_bitcast_fusion.1, bf16[2,576,2048]{2,1,0:T(8,128)(2,1)} %bitcast.244, ...), kind=kOutput, calls=%fused_computation.60 | convolution fusion | flops 6681081856 | bytes 29242880 | tf_op jit(solution)/shard_map/ecf,edf->ecd/dot_general | solution.py:41
  400.9 19.9 %fusion = bf16[2,576,2048]{2,1,0:T(8,128)(2,1)} fusion(bf16[3,2048,2816]{2,1,0:T(8,128)(2,1)} %all-gather.9.cloned.1.call-done, bf16[2,576,1408]{2,1,0:T(8,128)(2,1)} %get-tuple-element.39, bf16[2,576,1408]{2,1,0:T(8,128)(2,1)} %get-tuple-element.38), kind=kOutput, calls=%fused_computation.1 | convolution fusion | flops 13300531200 | bytes 34275328 | tf_op jit(solution)/shard_map/ecf,edf->ecd/dot_general | solution.py:41
  420.8 10.7 fusion.27
  431.5 15.8 %fusion.39 = bf16[1024,2816]{1,0:T(8,128)(2,1)S(1)} fusion(bf16[1024,2048]{1,0:T(8,128)(2,1)S(1)} %copy-done.15, bf16[3,2048,2816]{2,1,0:T(8,128)(2,1)} %all-gather.9.cloned.1.call-done), kind=kOutput, calls=%fused_computation.80 | convolution fusion | flops 11814043648 | bytes 21495808 | tf_op jit(solution)/shard_map/dot_general | solution.py:25
  447.4 16.2 %multiply_reduce_fusion.4 = (f32[1024]{0:T(1024)S(1)}, f32[1024]{0:T(1024)S(1)}, bf16[1024,1408]{1,0:T(8,128)(2,1)}, bf16[1024,1408]{1,0:T(8,128)(2,1)}) fusion(bf16[1024,2816]{1,0:T(8,128)(2,1)S(1)} %fusion.39, f32[1024]{0:T(1024)S(1)} %bitcast.224, bf16[1024,2048]{1,0:T(8,128)(2,1)} %select_dynamic-update-slice_fusion.6, ...), kind=kOutput, calls=%fused_computation.78 | convolution fusion | flops 5938739200 | bytes 21508096 | tf_op jit(solution)/shard_map/dot_general | solution.py:29
  463.6 19.4 %fusion.13 = bf16[1024,2048]{1,0:T(8,128)(2,1)} fusion(f32[1024,2048,1]{1,0,2:T(8,128)} %fusion.27, bf16[3,2048,2816]{2,1,0:T(8,128)(2,1)} %all-gather.9.cloned.1.call-done, bf16[1024,1408]{1,0:T(8,128)(2,1)} %get-tuple-element.41, bf16[1024,1408]{1,0:T(8,128)(2,1)} %get-tuple-element.40), kind=kOutput, calls=%fused_computation.39 | convolution fusion | flops 11826888704 | bytes 29884416 | tf_op jit(solution)/shard_map/dot_general | solution.py:29
  491.4 21.2 %collective-permute-done.30 = bf16[1024,512]{1,0:T(8,128)(2,1)} collective-permute-done((bf16[1024,512]{1,0:T(8,128)(2,1)}, bf16[1024,512]{1,0:T(8,128)(2,1)}, u32[]{:S(2)}, u32[]{:S(2)}) %collective-permute-start.30) | collective-permute-done | bytes 1048608 | tf_op jit(solution)/shard_map/ppermute | solution.py:79
  520.0 20.9 %collective-permute-done.31 = bf16[1024,512]{1,0:T(8,128)(2,1)S(1)} collective-permute-done((bf16[1024,512]{1,0:T(8,128)(2,1)S(1)}, bf16[1024,512]{1,0:T(8,128)(2,1)S(1)}, u32[]{:S(2)}, u32[]{:S(2)}) %collective-permute-start.31) | collective-permute-done | bytes 1048608 | tf_op jit(solution)/shard_map/ppermute | solution.py:79
  552.7 18.6 %collective-permute-done.36 = f32[4,1024]{1,0:T(4,128)S(1)} collective-permute-done((f32[4,1024]{1,0:T(4,128)S(1)}, f32[4,1024]{1,0:T(4,128)S(1)}, u32[]{:S(2)}, u32[]{:S(2)}) %collective-permute-start.36) | collective-permute-done | bytes 16416 | tf_op jit(solution)/shard_map/ppermute | solution.py:88
  577.6 16.0 %collective-permute-done.32 = bf16[1024,512]{1,0:T(8,128)(2,1)} collective-permute-done((bf16[1024,512]{1,0:T(8,128)(2,1)}, bf16[1024,512]{1,0:T(8,128)(2,1)}, u32[]{:S(2)}, u32[]{:S(2)}) %collective-permute-start.32) | collective-permute-done | bytes 1048608 | tf_op jit(solution)/shard_map/ppermute | solution.py:79
  610.3 16.1 %collective-permute-done.39 = bf16[1024,512]{1,0:T(8,128)(2,1)} collective-permute-done((bf16[1024,512]{1,0:T(8,128)(2,1)S(1)}, bf16[1024,512]{1,0:T(8,128)(2,1)}, u32[]{:S(2)}, u32[]{:S(2)}) %collective-permute-start.39) | collective-permute-done | bytes 1048608 | tf_op jit(solution)/shard_map/ppermute | solution.py:54
  637.0 18.5 %collective-permute-done.42 = bf16[1024,512]{1,0:T(8,128)(2,1)} collective-permute-done((bf16[1024,512]{1,0:T(8,128)(2,1)}, bf16[1024,512]{1,0:T(8,128)(2,1)}, u32[]{:S(2)}, u32[]{:S(2)}) %collective-permute-start.42) | collective-permute-done | bytes 1048608 | tf_op jit(solution)/shard_map/ppermute | solution.py:55
  665.0 11.9 %collective-permute-done.44 = bf16[1024,512]{1,0:T(8,128)(2,1)S(1)} collective-permute-done((bf16[1024,512]{1,0:T(8,128)(2,1)}, bf16[1024,512]{1,0:T(8,128)(2,1)S(1)}, u32[]{:S(2)}, u32[]{:S(2)}) %collective-permute-start.44) | collective-permute-done | bytes 1048608 | tf_op jit(solution)/shard_map/ppermute | solution.py:55
  688.5 14.1 %shard_map.349 = (bf16[1024,1536]{1,0:T(8,128)(2,1)S(1)}, f32[1,1536]{1,0:T(1,128)S(1)}) custom-call(bf16[1024,1536]{1,0:T(8,128)(2,1)S(1)} %copy-done.4, f32[1024,128]{1,0:T(8,128)S(1)} %get-tuple-element.90.cosine, f32[1024,128]{1,0:T(8,128)S(1)} %get-tuple-element.91.sine, s32[1024,1]{1,0:T(8,128)S(1)} %copy.56.seg_col, s32[1,1024]{1,0:T(1,128)S(1)} %copy-done.2, ...), custom_call_target="tpu_custom_call" | custom-call | flops 2684354560 | bytes 12582912 | tf_op jit(solution)/shard_map/pallas_call | solution.py:197
  704.3 9.7 convolution_convert_fusion.5
  714.1 8.3 pad_maximum_fusion.2
  723.1 18.6 %convolution_convert_fusion.1 = bf16[2,1408,2048]{2,1,0:T(8,128)(2,1)} fusion(bf16[2,576,2048]{2,1,0:T(8,128)(2,1)} %bitcast.245, f32[2,576]{1,0:T(2,128)S(1)} %copy-done.72, bf16[2,576,2816]{2,1,0:T(8,128)(2,1)} %fusion.24), kind=kOutput, calls=%fused_computation.17 | convolution fusion | flops 6664142848 | bytes 22745600 | tf_op jit(solution)/shard_map/ecd,ecf->edf/dot_general | solution.py:45
  741.7 12.2 %fusion.15 = bf16[1,1408,2048]{2,1,0:T(8,128)(2,1)S(1)} fusion(bf16[1024,2048]{1,0:T(8,128)(2,1)} %select_dynamic-update-slice_fusion.6, f32[1024]{0:T(1024)S(1)} %bitcast.225, bf16[1024,2816]{1,0:T(8,128)(2,1)} %copy-done.78), kind=kOutput, calls=%fused_computation.50 | convolution fusion | flops 5921439744 | bytes 15732736 | tf_op jit(solution)/shard_map/dot_general | solution.py:33
  753.9 7.0 pad_maximum_fusion.1
  761.0 18.7 %convert_bitcast_fusion = bf16[1,2048,2816]{2,1,0:T(8,128)(2,1)} fusion(bf16[1024,2048]{1,0:T(8,128)(2,1)} %copy-done.14, bf16[1024,1408]{1,0:T(8,128)(2,1)} %get-tuple-element.41, bf16[1024,1408]{1,0:T(8,128)(2,1)} %get-tuple-element.40), kind=kOutput, calls=%fused_computation.12 | convolution fusion | flops 11828461568 | bytes 21495808 | tf_op jit(solution)/shard_map/dot_general | solution.py:33
  779.7 24.9 %convolution_convert_fusion = bf16[2,2048,2816]{2,1,0:T(8,128)(2,1)} fusion(bf16[2,576,2048]{2,1,0:T(8,128)(2,1)} %bitcast.247, bf16[2,576,1408]{2,1,0:T(8,128)(2,1)S(1)} %copy-done.80, bf16[2,576,1408]{2,1,0:T(8,128)(2,1)S(1)} %copy-done.79), kind=kOutput, calls=%fused_computation.6 | convolution fusion | flops 13312065536 | bytes 34275328 | tf_op jit(solution)/shard_map/ecd,ecf->edf/dot_general | solution.py:45
  804.6 27.5 %pad_maximum_fusion = bf16[3,2048,2816]{2,1,0:T(8,128)(2,1)} fusion(bf16[1,2048,2816]{2,1,0:T(8,128)(2,1)} %convert_bitcast_fusion, bf16[2,2048,2816]{2,1,0:T(8,128)(2,1)} %convolution_convert_fusion), kind=kLoop, calls=%fused_computation | loop fusion | flops 17301504 | bytes 69206016 | tf_op jit(solution)/shard_map/concatenate | solution.py:430
  832.2 13.4 %fusion.41 = f32[1024,2048]{1,0:T(8,128)} fusion(bf16[3,1408,2048]{2,1,0:T(8,128)(2,1)} %all-gather.11.cloned.1.call-done, f32[1024]{0:T(1024)S(1)} %bitcast.226, bf16[1024,2816]{1,0:T(8,128)(2,1)} %copy-done.78), kind=kOutput, calls=%fused_computation.83 | convolution fusion | flops 5918556160 | bytes 19927040 | tf_op jit(solution)/shard_map/dot_general | solution.py:25
  845.6 22.5 %fusion.14 = bf16[1024,2048]{1,0:T(8,128)(2,1)} fusion(f32[1024,2048]{1,0:T(8,128)} %fusion.41, f32[1024,2]{0,1:T(2,128)S(1)} %copy-done.54, f32[576]{0:T(1024)S(1)} %copy-done.61, bf16[3,1408,2048]{2,1,0:T(8,128)(2,1)} %all-gather.11.cloned.1.call-done, f32[2,576]{1,0:T(2,128)S(1)} %copy-done.72, bf16[2,576,2816]{2,1,0:T(8,128)(2,1)} %fusion.24), kind=kOutput, calls=%fused_computation.41 | convolution fusion | flops 11497947136 | bytes 30620416 | tf_op jit(solution)/shard_map/dot_general | solution.py:25
  871.7 11.3 multiply_reduce_fusion
  885.8 9.3 collective-permute-done.18
  900.8 16.9 %collective-permute-done.45 = bf16[1024,512]{1,0:T(8,128)(2,1)S(1)} collective-permute-done((bf16[1024,512]{1,0:T(8,128)(2,1)S(1)}, bf16[1024,512]{1,0:T(8,128)(2,1)S(1)}, u32[]{:S(2)}, u32[]{:S(2)}) %collective-permute-start.45) | collective-permute-done | bytes 1048608 | tf_op jit(solution)/shard_map/ppermute | solution.py:79
  922.5 17.6 %collective-permute-done.19 = bf16[1024,512]{1,0:T(8,128)(2,1)S(1)} collective-permute-done((bf16[1024,512]{1,0:T(8,128)(2,1)S(1)}, bf16[1024,512]{1,0:T(8,128)(2,1)S(1)}, u32[]{:S(2)}, u32[]{:S(2)}) %collective-permute-start.19) | collective-permute-done | bytes 1048608 | tf_op jit(solution)/shard_map/ppermute | solution.py:79
  942.7 13.0 %collective-permute-done.46 = bf16[1024,512]{1,0:T(8,128)(2,1)S(1)} collective-permute-done((bf16[1024,512]{1,0:T(8,128)(2,1)S(1)}, bf16[1024,512]{1,0:T(8,128)(2,1)S(1)}, u32[]{:S(2)}, u32[]{:S(2)}) %collective-permute-start.46) | collective-permute-done | bytes 1048608 | tf_op jit(solution)/shard_map/ppermute | solution.py:79
  979.6 8.1 collective-permute-done.20
  995.1 10.2 collective-permute-start.53
  1005.3 14.7 %collective-permute-start.52 = (f32[1,1024]{1,0:T(1,128)S(1)}, f32[1,1024]{1,0:T(1,128)S(1)}, u32[]{:S(2)}, u32[]{:S(2)}) collective-permute-start(f32[1,1024]{1,0:T(1,128)S(1)} %bitcast.228), channel_id=1, source_target_pairs={{0,2},{1,3},{2,0},{3,1},{4,6},{5,7},{6,4},{7,5},{8,10},{9,11},{10,... | collective-permute-start | bytes 12296 | tf_op jit(solution)/shard_map/ppermute | solution.py:88
  1020.2 40.3 %psum.14 = f32[5,2048]{1,0:T(8,128)S(1)} all-reduce(f32[5,2048]{1,0:T(8,128)S(1)} %pad_maximum_fusion.15), channel_id=1, replica_groups=mesh['row'=8,'col'=4] {'row','col'}, use_global_device_ids=true, to_apply=%region_17.18 | all-reduce | flops 10240 | bytes 81920 | tf_op jit(solution)/shard_map/psum | solution.py:447
  1077.0 52.5 %reduce-scatter.6.cloned.1.call-done = bf16[3,256,2816]{2,1,0:T(8,128)(2,1)} async-done(((bf16[3,2048,2816]{2,1,0:T(8,128)(2,1)}), bf16[3,256,2816]{2,1,0:T(8,128)(2,1)}) %reduce-scatter.6.cloned.1.call-update) | async-done | bytes 4325392 | tf_op jit(solution)/shard_map/reduce_scatter | solution.py:426
  (423 shorter events, 298.1 us)
Async XLA Ops:
  7.2 201.5 %all-gather.5.cloned.1.call-start = ((), (), s32[]{:S(2)}) async-start(), calls=%async_computation.3 | async-start | bytes 7077888 | tf_op jit(solution)/shard_map/all_gather | solution.py:282
  11.5 299.3 %all-gather.7.cloned.1.call-start = ((), (), s32[]{:S(2)}) async-start(), calls=%async_computation.4 | async-start | bytes 9437184 | tf_op jit(solution)/shard_map/all_gather | solution.py:284
  45.7 292.2 %all-gather.9.cloned.1.call-start = ((), (), s32[]{:S(2)}) async-start(), calls=%async_computation.5 | async-start | bytes 38928384 | tf_op jit(solution)/shard_map/all_gather | solution.py:289
  50.4 334.4 %all-gather.11.cloned.1.call-start = ((), (), s32[]{:S(2)}) async-start(), calls=%async_computation.6 | async-start | bytes 19464192 | tf_op jit(solution)/shard_map/all_gather | solution.py:290
  54.3 912.2 %all-reduce.2.cloned.1.call-start = ((), (), s32[]{:S(2)}) async-start(), calls=%async_computation.8 | async-start | bytes 262144 | tf_op jit(solution)/shard_map/psum | solution.py:442
  54.4 76.5 %collective-permute-start.1 = (bf16[1024,512]{1,0:T(8,128)(2,1)S(1)}, bf16[1024,512]{1,0:T(8,128)(2,1)}, u32[]{:S(2)}, u32[]{:S(2)}) collective-permute-start(bf16[1024,512]{1,0:T(8,128)(2,1)S(1)} %copy-done.9), channel_id=1, source_target_pairs={{1,0},{2,1},{3,2},{5,4},{6,5},{7,6},{9,8},{10,9},{11,10},{13,12},{... | collective-permute-start | bytes 3145736 | tf_op jit(solution)/shard_map/ppermute | solution.py:55
  55.7 58.2 %collective-permute-start = (bf16[1024,512]{1,0:T(8,128)(2,1)S(1)}, bf16[1024,512]{1,0:T(8,128)(2,1)}, u32[]{:S(2)}, u32[]{:S(2)}) collective-permute-start(bf16[1024,512]{1,0:T(8,128)(2,1)S(1)} %copy-done.9), channel_id=1, source_target_pairs={{0,1},{1,2},{2,3},{4,5},{5,6},{6,7},{8,9},{9,10},{10,11},{12,13},{... | collective-permute-start | bytes 3145736 | tf_op jit(solution)/shard_map/ppermute | solution.py:54
  61.3 71.3 %collective-permute-start.25 = (bf16[1024,512]{1,0:T(8,128)(2,1)S(1)}, bf16[1024,512]{1,0:T(8,128)(2,1)}, u32[]{:S(2)}, u32[]{:S(2)}) collective-permute-start(bf16[1024,512]{1,0:T(8,128)(2,1)S(1)} %copy-done.7), channel_id=1, source_target_pairs={{1,0},{2,1},{3,2},{5,4},{6,5},{7,6},{9,8},{10,9},{11,10},{13,12},{... | collective-permute-start | bytes 3145736 | tf_op jit(solution)/shard_map/ppermute | solution.py:55
  62.6 71.6 %collective-permute-start.24 = (bf16[1024,512]{1,0:T(8,128)(2,1)S(1)}, bf16[1024,512]{1,0:T(8,128)(2,1)}, u32[]{:S(2)}, u32[]{:S(2)}) collective-permute-start(bf16[1024,512]{1,0:T(8,128)(2,1)S(1)} %copy-done.7), channel_id=1, source_target_pairs={{0,1},{1,2},{2,3},{4,5},{5,6},{6,7},{8,9},{9,10},{10,11},{12,13},{... | collective-permute-start | bytes 3145736 | tf_op jit(solution)/shard_map/ppermute | solution.py:54
  115.8 24.1 %collective-permute-start.2 = (bf16[1024,512]{1,0:T(8,128)(2,1)}, bf16[1024,512]{1,0:T(8,128)(2,1)}, u32[]{:S(2)}, u32[]{:S(2)}) collective-permute-start(bf16[1024,512]{1,0:T(8,128)(2,1)} %collective-permute-done), channel_id=1, source_target_pairs={{1,2},{2,3},{5,6},{6,7},{9,10},{10,11},{13,14},{14,15},{17,18},{18... | collective-permute-start | bytes 3145736 | tf_op jit(solution)/shard_map/ppermute | solution.py:54
  130.9 29.0 %collective-permute-start.3 = (bf16[1024,512]{1,0:T(8,128)(2,1)}, bf16[1024,512]{1,0:T(8,128)(2,1)S(1)}, u32[]{:S(2)}, u32[]{:S(2)}) collective-permute-start(bf16[1024,512]{1,0:T(8,128)(2,1)} %collective-permute-done.1), channel_id=1, source_target_pairs={{1,0},{2,1},{5,4},{6,5},{9,8},{10,9},{13,12},{14,13},{17,16},{18,1... | collective-permute-start | bytes 3145736 | tf_op jit(solution)/shard_map/ppermute | solution.py:55
  132.6 49.9 %collective-permute-start.27 = (bf16[1024,512]{1,0:T(8,128)(2,1)}, bf16[1024,512]{1,0:T(8,128)(2,1)}, u32[]{:S(2)}, u32[]{:S(2)}) collective-permute-start(bf16[1024,512]{1,0:T(8,128)(2,1)} %collective-permute-done.25), channel_id=1, source_target_pairs={{1,0},{2,1},{5,4},{6,5},{9,8},{10,9},{13,12},{14,13},{17,16},{18,1... | collective-permute-start | bytes 3145736 | tf_op jit(solution)/shard_map/ppermute | solution.py:55
  134.2 49.6 %collective-permute-start.26 = (bf16[1024,512]{1,0:T(8,128)(2,1)}, bf16[1024,512]{1,0:T(8,128)(2,1)}, u32[]{:S(2)}, u32[]{:S(2)}) collective-permute-start(bf16[1024,512]{1,0:T(8,128)(2,1)} %collective-permute-done.24), channel_id=1, source_target_pairs={{1,2},{2,3},{5,6},{6,7},{9,10},{10,11},{13,14},{14,15},{17,18},{18... | collective-permute-start | bytes 3145736 | tf_op jit(solution)/shard_map/ppermute | solution.py:54
  139.9 46.5 %collective-permute-start.4 = (bf16[1024,512]{1,0:T(8,128)(2,1)}, bf16[1024,512]{1,0:T(8,128)(2,1)S(1)}, u32[]{:S(2)}, u32[]{:S(2)}) collective-permute-start(bf16[1024,512]{1,0:T(8,128)(2,1)} %collective-permute-done.2), channel_id=1, source_target_pairs={{2,3},{6,7},{10,11},{14,15},{18,19},{22,23},{26,27},{30,31}} | collective-permute-start | bytes 3145736 | tf_op jit(solution)/shard_map/ppermute | solution.py:54
  159.9 44.9 %collective-permute-start.5 = (bf16[1024,512]{1,0:T(8,128)(2,1)S(1)}, bf16[1024,512]{1,0:T(8,128)(2,1)S(1)}, u32[]{:S(2)}, u32[]{:S(2)}) collective-permute-start(bf16[1024,512]{1,0:T(8,128)(2,1)S(1)} %collective-permute-done.3), channel_id=1, source_target_pairs={{1,0},{5,4},{9,8},{13,12},{17,16},{21,20},{25,24},{29,28}} | collective-permute-start | bytes 3145736 | tf_op jit(solution)/shard_map/ppermute | solution.py:55
  182.4 59.7 %collective-permute-start.29 = (bf16[1024,512]{1,0:T(8,128)(2,1)}, bf16[1024,512]{1,0:T(8,128)(2,1)}, u32[]{:S(2)}, u32[]{:S(2)}) collective-permute-start(bf16[1024,512]{1,0:T(8,128)(2,1)} %collective-permute-done.27), channel_id=1, source_target_pairs={{1,0},{5,4},{9,8},{13,12},{17,16},{21,20},{25,24},{29,28}} | collective-permute-start | bytes 3145736 | tf_op jit(solution)/shard_map/ppermute | solution.py:55
  183.7 57.1 %collective-permute-start.28 = (bf16[1024,512]{1,0:T(8,128)(2,1)}, bf16[1024,512]{1,0:T(8,128)(2,1)}, u32[]{:S(2)}, u32[]{:S(2)}) collective-permute-start(bf16[1024,512]{1,0:T(8,128)(2,1)} %collective-permute-done.26), channel_id=1, source_target_pairs={{2,3},{6,7},{10,11},{14,15},{18,19},{22,23},{26,27},{30,31}} | collective-permute-start | bytes 3145736 | tf_op jit(solution)/shard_map/ppermute | solution.py:54
  230.6 26.7 %collective-permute-start.7 = (bf16[1024,512]{1,0:T(8,128)(2,1)S(1)}, bf16[1024,512]{1,0:T(8,128)(2,1)S(1)}, u32[]{:S(2)}, u32[]{:S(2)}) collective-permute-start(bf16[1024,512]{1,0:T(8,128)(2,1)S(1)} %get-tuple-element.23), channel_id=1, source_target_pairs={{1,0},{2,1},{3,2},{5,4},{6,5},{7,6},{9,8},{10,9},{11,10},{13,12},{... | collective-permute-start | bytes 3145736 | tf_op jit(solution)/shard_map/ppermute | solution.py:55
  231.9 26.7 %collective-permute-start.6 = (bf16[1024,512]{1,0:T(8,128)(2,1)S(1)}, bf16[1024,512]{1,0:T(8,128)(2,1)S(1)}, u32[]{:S(2)}, u32[]{:S(2)}) collective-permute-start(bf16[1024,512]{1,0:T(8,128)(2,1)S(1)} %get-tuple-element.23), channel_id=1, source_target_pairs={{0,1},{1,2},{2,3},{4,5},{5,6},{6,7},{8,9},{9,10},{10,11},{12,13},{... | collective-permute-start | bytes 3145736 | tf_op jit(solution)/shard_map/ppermute | solution.py:54
  257.3 25.9 %collective-permute-start.9 = (bf16[1024,512]{1,0:T(8,128)(2,1)S(1)}, bf16[1024,512]{1,0:T(8,128)(2,1)S(1)}, u32[]{:S(2)}, u32[]{:S(2)}) collective-permute-start(bf16[1024,512]{1,0:T(8,128)(2,1)S(1)} %collective-permute-done.7), channel_id=1, source_target_pairs={{1,0},{2,1},{5,4},{6,5},{9,8},{10,9},{13,12},{14,13},{17,16},{18,1... | collective-permute-start | bytes 3145736 | tf_op jit(solution)/shard_map/ppermute | solution.py:55
  283.2 26.3 %collective-permute-start.11 = (bf16[1024,512]{1,0:T(8,128)(2,1)S(1)}, bf16[1024,512]{1,0:T(8,128)(2,1)S(1)}, u32[]{:S(2)}, u32[]{:S(2)}) collective-permute-start(bf16[1024,512]{1,0:T(8,128)(2,1)S(1)} %collective-permute-done.9), channel_id=1, source_target_pairs={{1,0},{5,4},{9,8},{13,12},{17,16},{21,20},{25,24},{29,28}} | collective-permute-start | bytes 3145736 | tf_op jit(solution)/shard_map/ppermute | solution.py:55
  486.1 26.5 %collective-permute-start.30 = (bf16[1024,512]{1,0:T(8,128)(2,1)}, bf16[1024,512]{1,0:T(8,128)(2,1)}, u32[]{:S(2)}, u32[]{:S(2)}) collective-permute-start(bf16[1024,512]{1,0:T(8,128)(2,1)} %get-tuple-element.52), channel_id=1, source_target_pairs={{0,1},{4,5},{8,9},{12,13},{16,17},{20,21},{24,25},{28,29}} | collective-permute-start | bytes 3145736 | tf_op jit(solution)/shard_map/ppermute | solution.py:79
  490.6 29.4 %collective-permute-start.33 = (bf16[1024,512]{1,0:T(8,128)(2,1)}, bf16[1024,512]{1,0:T(8,128)(2,1)S(1)}, u32[]{:S(2)}, u32[]{:S(2)}) collective-permute-start(bf16[1024,512]{1,0:T(8,128)(2,1)} %get-tuple-element.53), channel_id=1, source_target_pairs={{3,2},{7,6},{11,10},{15,14},{19,18},{23,22},{27,26},{31,30}} | collective-permute-start | bytes 3145736 | tf_op jit(solution)/shard_map/ppermute | solution.py:80
  514.5 26.4 %collective-permute-start.31 = (bf16[1024,512]{1,0:T(8,128)(2,1)S(1)}, bf16[1024,512]{1,0:T(8,128)(2,1)S(1)}, u32[]{:S(2)}, u32[]{:S(2)}) collective-permute-start(bf16[1024,512]{1,0:T(8,128)(2,1)S(1)} %add_convert_fusion.7), channel_id=1, source_target_pairs={{0,1},{1,2},{4,5},{5,6},{8,9},{9,10},{12,13},{13,14},{16,17},{17,1... | collective-permute-start | bytes 3145736 | tf_op jit(solution)/shard_map/ppermute | solution.py:79
  542.8 31.8 %collective-permute-start.34 = (bf16[1024,512]{1,0:T(8,128)(2,1)S(1)}, bf16[1024,512]{1,0:T(8,128)(2,1)S(1)}, u32[]{:S(2)}, u32[]{:S(2)}) collective-permute-start(bf16[1024,512]{1,0:T(8,128)(2,1)S(1)} %get-tuple-element.51), channel_id=1, source_target_pairs={{2,1},{3,2},{6,5},{7,6},{10,9},{11,10},{14,13},{15,14},{18,17},{19... | collective-permute-start | bytes 3145736 | tf_op jit(solution)/shard_map/ppermute | solution.py:80
  543.7 27.8 %collective-permute-start.37 = (f32[4,1024]{1,0:T(4,128)S(1)}, f32[4,1024]{1,0:T(4,128)S(1)}, u32[]{:S(2)}, u32[]{:S(2)}) collective-permute-start(f32[4,1024]{1,0:T(4,128)S(1)} %pad_maximum_fusion.16), channel_id=1, source_target_pairs={{0,2},{1,3},{2,0},{3,1},{4,6},{5,7},{6,4},{7,5},{8,10},{9,11},{10,... | collective-permute-start | bytes 49160 | tf_op jit(solution)/shard_map/ppermute | solution.py:88
  548.9 22.4 %collective-permute-start.36 = (f32[4,1024]{1,0:T(4,128)S(1)}, f32[4,1024]{1,0:T(4,128)S(1)}, u32[]{:S(2)}, u32[]{:S(2)}) collective-permute-start(f32[4,1024]{1,0:T(4,128)S(1)} %pad_maximum_fusion.16), channel_id=1, source_target_pairs={{0,1},{1,2},{2,3},{3,0},{4,5},{5,6},{6,7},{7,4},{8,9},{9,10},{10,1... | collective-permute-start | bytes 49160 | tf_op jit(solution)/shard_map/ppermute | solution.py:88
  549.3 28.1 %collective-permute-start.38 = (f32[4,1024]{1,0:T(4,128)S(1)}, f32[4,1024]{1,0:T(4,128)S(1)}, u32[]{:S(2)}, u32[]{:S(2)}) collective-permute-start(f32[4,1024]{1,0:T(4,128)S(1)} %pad_maximum_fusion.16), channel_id=1, source_target_pairs={{0,3},{1,0},{2,1},{3,2},{4,7},{5,4},{6,5},{7,6},{8,11},{9,8},{10,9... | collective-permute-start | bytes 49160 | tf_op jit(solution)/shard_map/ppermute | solution.py:88
  576.0 24.1 %collective-permute-start.35 = (bf16[1024,512]{1,0:T(8,128)(2,1)}, bf16[1024,512]{1,0:T(8,128)(2,1)}, u32[]{:S(2)}, u32[]{:S(2)}) collective-permute-start(bf16[1024,512]{1,0:T(8,128)(2,1)} %add_convert_fusion.4), channel_id=1, source_target_pairs={{1,0},{2,1},{3,2},{5,4},{6,5},{7,6},{9,8},{10,9},{11,10},{13,12},{... | collective-permute-start | bytes 3145736 | tf_op jit(solution)/shard_map/ppermute | solution.py:80
  609.0 23.1 %collective-permute-start.40 = (bf16[1024,512]{1,0:T(8,128)(2,1)S(1)}, bf16[1024,512]{1,0:T(8,128)(2,1)}, u32[]{:S(2)}, u32[]{:S(2)}) collective-permute-start(bf16[1024,512]{1,0:T(8,128)(2,1)S(1)} %get-tuple-element.36), channel_id=1, source_target_pairs={{1,0},{2,1},{3,2},{5,4},{6,5},{7,6},{9,8},{10,9},{11,10},{13,12},{... | collective-permute-start | bytes 3145736 | tf_op jit(solution)/shard_map/ppermute | solution.py:55
  632.1 23.3 %collective-permute-start.42 = (bf16[1024,512]{1,0:T(8,128)(2,1)}, bf16[1024,512]{1,0:T(8,128)(2,1)}, u32[]{:S(2)}, u32[]{:S(2)}) collective-permute-start(bf16[1024,512]{1,0:T(8,128)(2,1)} %collective-permute-done.40), channel_id=1, source_target_pairs={{1,0},{2,1},{5,4},{6,5},{9,8},{10,9},{13,12},{14,13},{17,16},{18,1... | collective-permute-start | bytes 3145736 | tf_op jit(solution)/shard_map/ppermute | solution.py:55
  634.8 431.9 %reduce-scatter.4.cloned.1.call-start = ((), (), s32[]{:S(2)}) async-start(), calls=%async_computation.7 | async-start | bytes 9437184 | tf_op jit(solution)/shard_map/reduce_scatter | solution.py:426
  634.8 28.8 %collective-permute-start.43 = (bf16[1024,512]{1,0:T(8,128)(2,1)}, bf16[1024,512]{1,0:T(8,128)(2,1)S(1)}, u32[]{:S(2)}, u32[]{:S(2)}) collective-permute-start(bf16[1024,512]{1,0:T(8,128)(2,1)} %collective-permute-done.41), channel_id=1, source_target_pairs={{2,3},{6,7},{10,11},{14,15},{18,19},{22,23},{26,27},{30,31}} | collective-permute-start | bytes 3145736 | tf_op jit(solution)/shard_map/ppermute | solution.py:54
  722.4 349.7 %reduce-scatter.8.cloned.1.call-start = ((), (), s32[]{:S(2)}) async-start(), calls=%async_computation.10 | async-start | bytes 19464192 | tf_op jit(solution)/shard_map/reduce_scatter | solution.py:426
  760.9 368.6 %reduce-scatter.6.cloned.1.call-start = ((), (), s32[]{:S(2)}) async-start(), calls=%async_computation.9 | async-start | bytes 38928384 | tf_op jit(solution)/shard_map/reduce_scatter | solution.py:426
  869.9 25.3 %collective-permute-start.18 = (bf16[1024,512]{1,0:T(8,128)(2,1)S(1)}, bf16[1024,512]{1,0:T(8,128)(2,1)S(1)}, u32[]{:S(2)}, u32[]{:S(2)}) collective-permute-start(bf16[1024,512]{1,0:T(8,128)(2,1)S(1)} %get-tuple-element.56), channel_id=1, source_target_pairs={{0,1},{4,5},{8,9},{12,13},{16,17},{20,21},{24,25},{28,29}} | collective-permute-start | bytes 3145736 | tf_op jit(solution)/shard_map/ppermute | solution.py:79
  883.2 34.4 %collective-permute-start.45 = (bf16[1024,512]{1,0:T(8,128)(2,1)S(1)}, bf16[1024,512]{1,0:T(8,128)(2,1)S(1)}, u32[]{:S(2)}, u32[]{:S(2)}) collective-permute-start(bf16[1024,512]{1,0:T(8,128)(2,1)S(1)} %get-tuple-element.48), channel_id=1, source_target_pairs={{0,1},{4,5},{8,9},{12,13},{16,17},{20,21},{24,25},{28,29}} | collective-permute-start | bytes 3145736 | tf_op jit(solution)/shard_map/ppermute | solution.py:79
  885.0 37.5 %collective-permute-start.21 = (bf16[1024,512]{1,0:T(8,128)(2,1)S(1)}, bf16[1024,512]{1,0:T(8,128)(2,1)S(1)}, u32[]{:S(2)}, u32[]{:S(2)}) collective-permute-start(bf16[1024,512]{1,0:T(8,128)(2,1)S(1)} %get-tuple-element.57), channel_id=1, source_target_pairs={{3,2},{7,6},{11,10},{15,14},{19,18},{23,22},{27,26},{31,30}} | collective-permute-start | bytes 3145736 | tf_op jit(solution)/shard_map/ppermute | solution.py:80
  895.6 44.5 %collective-permute-start.19 = (bf16[1024,512]{1,0:T(8,128)(2,1)S(1)}, bf16[1024,512]{1,0:T(8,128)(2,1)S(1)}, u32[]{:S(2)}, u32[]{:S(2)}) collective-permute-start(bf16[1024,512]{1,0:T(8,128)(2,1)S(1)} %add_convert_fusion.11), channel_id=1, source_target_pairs={{0,1},{1,2},{4,5},{5,6},{8,9},{9,10},{12,13},{13,14},{16,17},{17,1... | collective-permute-start | bytes 3145736 | tf_op jit(solution)/shard_map/ppermute | solution.py:79
  900.0 42.7 %collective-permute-start.48 = (bf16[1024,512]{1,0:T(8,128)(2,1)S(1)}, bf16[1024,512]{1,0:T(8,128)(2,1)S(1)}, u32[]{:S(2)}, u32[]{:S(2)}) collective-permute-start(bf16[1024,512]{1,0:T(8,128)(2,1)S(1)} %get-tuple-element.49), channel_id=1, source_target_pairs={{3,2},{7,6},{11,10},{15,14},{19,18},{23,22},{27,26},{31,30}} | collective-permute-start | bytes 3145736 | tf_op jit(solution)/shard_map/ppermute | solution.py:80
  918.1 37.6 %collective-permute-start.46 = (bf16[1024,512]{1,0:T(8,128)(2,1)S(1)}, bf16[1024,512]{1,0:T(8,128)(2,1)S(1)}, u32[]{:S(2)}, u32[]{:S(2)}) collective-permute-start(bf16[1024,512]{1,0:T(8,128)(2,1)S(1)} %add_convert_fusion.3), channel_id=1, source_target_pairs={{0,1},{1,2},{4,5},{5,6},{8,9},{9,10},{12,13},{13,14},{16,17},{17,1... | collective-permute-start | bytes 3145736 | tf_op jit(solution)/shard_map/ppermute | solution.py:79
  959.7 28.0 %collective-permute-start.20 = (bf16[1024,512]{1,0:T(8,128)(2,1)}, bf16[1024,512]{1,0:T(8,128)(2,1)S(1)}, u32[]{:S(2)}, u32[]{:S(2)}) collective-permute-start(bf16[1024,512]{1,0:T(8,128)(2,1)} %get-tuple-element.54), channel_id=1, source_target_pairs={{0,1},{1,2},{2,3},{4,5},{5,6},{6,7},{8,9},{9,10},{10,11},{12,13},{... | collective-permute-start | bytes 3145736 | tf_op jit(solution)/shard_map/ppermute | solution.py:79
  965.2 22.4 %collective-permute-start.23 = (bf16[1024,512]{1,0:T(8,128)(2,1)}, bf16[1024,512]{1,0:T(8,128)(2,1)S(1)}, u32[]{:S(2)}, u32[]{:S(2)}) collective-permute-start(bf16[1024,512]{1,0:T(8,128)(2,1)} %add_convert_fusion.8), channel_id=1, source_target_pairs={{1,0},{2,1},{3,2},{5,4},{6,5},{7,6},{9,8},{10,9},{11,10},{13,12},{... | collective-permute-start | bytes 3145736 | tf_op jit(solution)/shard_map/ppermute | solution.py:80
  969.1 92.7 %collective-permute-start.47 = (bf16[1024,512]{1,0:T(8,128)(2,1)}, bf16[1024,512]{1,0:T(8,128)(2,1)}, u32[]{:S(2)}, u32[]{:S(2)}) collective-permute-start(bf16[1024,512]{1,0:T(8,128)(2,1)} %get-tuple-element.46), channel_id=1, source_target_pairs={{0,1},{1,2},{2,3},{4,5},{5,6},{6,7},{8,9},{9,10},{10,11},{12,13},{... | collective-permute-start | bytes 3145736 | tf_op jit(solution)/shard_map/ppermute | solution.py:79
  978.3 83.5 %collective-permute-start.50 = (bf16[1024,512]{1,0:T(8,128)(2,1)}, bf16[1024,512]{1,0:T(8,128)(2,1)}, u32[]{:S(2)}, u32[]{:S(2)}) collective-permute-start(bf16[1024,512]{1,0:T(8,128)(2,1)} %add_convert_fusion), channel_id=1, source_target_pairs={{1,0},{2,1},{3,2},{5,4},{6,5},{7,6},{9,8},{10,9},{11,10},{13,12},{... | collective-permute-start | bytes 3145736 | tf_op jit(solution)/shard_map/ppermute | solution.py:80
  995.1 66.3 %collective-permute-start.53 = (f32[1,1024]{1,0:T(1,128)S(1)}, f32[1,1024]{1,0:T(1,128)S(1)}, u32[]{:S(2)}, u32[]{:S(2)}) collective-permute-start(f32[1,1024]{1,0:T(1,128)S(1)} %bitcast.227), channel_id=1, source_target_pairs={{0,3},{1,0},{2,1},{3,2},{4,7},{5,4},{6,5},{7,6},{8,11},{9,8},{10,9... | collective-permute-start | bytes 12296 | tf_op jit(solution)/shard_map/ppermute | solution.py:88
  1005.3 56.0 %collective-permute-start.52 = (f32[1,1024]{1,0:T(1,128)S(1)}, f32[1,1024]{1,0:T(1,128)S(1)}, u32[]{:S(2)}, u32[]{:S(2)}) collective-permute-start(f32[1,1024]{1,0:T(1,128)S(1)} %bitcast.228), channel_id=1, source_target_pairs={{0,2},{1,3},{2,0},{3,1},{4,6},{5,7},{6,4},{7,5},{8,10},{9,11},{10,... | collective-permute-start | bytes 12296 | tf_op jit(solution)/shard_map/ppermute | solution.py:88
  1020.0 41.2 %collective-permute-start.51 = (f32[1,1024]{1,0:T(1,128)S(1)}, f32[1,1024]{1,0:T(1,128)S(1)}, u32[]{:S(2)}, u32[]{:S(2)}) collective-permute-start(f32[1,1024]{1,0:T(1,128)S(1)} %bitcast.229), channel_id=1, source_target_pairs={{0,1},{1,2},{2,3},{3,0},{4,5},{5,6},{6,7},{7,4},{8,9},{9,10},{10,1... | collective-permute-start | bytes 12296 | tf_op jit(solution)/shard_map/ppermute | solution.py:88
  (95 other events, 2316.7 us)
Sparse Core Ops, SparseCore 0:
  11.7 49.3 all-gather.4
  63.5 55.9 all-gather.6
  121.4 165.5 all-gather.8
  289.3 95.4 all-gather.10
  634.9 53.1 all-reduce.1
  722.5 68.5 reduce-scatter.3
  794.8 118.5 reduce-scatter.7
  917.5 211.9 reduce-scatter.5

commit v2 on v1

v2 whole, which is shorter than its diff:
```python
import functools

import jax
import jax.numpy as jnp
from jax import lax
from jax.experimental import pallas as pl
from jax.experimental.pallas import tpu as pltpu
from jax.sharding import PartitionSpec as P

HEAD_DIM = 128
EXPERTS = 8
TOP = 4
CAP = 576
SPAN = 256

EPSILON = 1e-06
THETA = 1000000.0
NEGATIVE = -1e30

f32 = jnp.float32
bf16 = jnp.bfloat16


def dot_nn(left, right):
    return jnp.dot(left, right, preferred_element_type=f32)


def dot_nt(left, right):
    return lax.dot_general(left, right, (((1,), (1,)), ((), ())), preferred_element_type=f32)


def dot_tn(left, right):
    return lax.dot_general(left, right, (((0,), (0,)), ((), ())), preferred_element_type=f32)


def batch_nn(left, right):
    return jnp.einsum("ecd,edf->ecf", left, right, preferred_element_type=f32)


def batch_nt(left, right):
    return jnp.einsum("ecf,edf->ecd", left, right, preferred_element_type=f32)


def batch_tn(left, right):
    return jnp.einsum("ecd,ecf->edf", left, right, preferred_element_type=f32)


def after(values, *earlier):
    if not earlier:
        return values
    leaves, tree = jax.tree.flatten(values)
    anywhere = pl.BlockSpec(memory_space=pl.ANY)
    leaves = pl.pallas_call(
        lambda *refs: None,
        in_specs=[anywhere] * (len(leaves) + len(earlier)),
        out_specs=[anywhere] * len(leaves),
        out_shape=[jax.ShapeDtypeStruct(leaf.shape, leaf.dtype) for leaf in leaves],
        input_output_aliases={i: i for i in range(len(leaves))},
    )(*leaves, *earlier)
    return jax.tree.unflatten(tree, leaves)


class Gather:
    def __init__(self, block, count, me):
        self.block, self.count, self.me, self.hops = block, count, me, 0
        self.up = self.down = block
        full = jnp.zeros((block.shape[0], count * block.shape[1]), block.dtype)
        self.full = lax.dynamic_update_slice_in_dim(full, block, me * block.shape[1], 1)

    def place(self, piece, there, index):
        piece, index = jnp.where(there, piece, self.block), jnp.where(there, index, self.me)
        self.full = lax.dynamic_update_slice_in_dim(self.full, piece, index * self.block.shape[1], 1)

    def placed(self):
        if self.hops:
            self.place(self.up, self.me >= self.hops, self.me - self.hops)
            self.place(self.down, self.me + self.hops < self.count, self.me + self.hops)

    def hop(self, *earlier):
        if earlier:
            self.up, self.down = after((self.up, self.down), *earlier)
        self.up_before = self.up
        self.placed()
        done, count = self.hops, self.count
        self.up = lax.ppermute(self.up, "col", [(i, i + 1) for i in range(done, count - 1)])
        self.down = lax.ppermute(self.down, "col", [(i, i - 1) for i in range(1, count - done)])
        self.hops += 1

    def result(self):
        while self.hops < self.count - 1:
            self.hop()
        self.placed()
        return self.full


def hop_kernel(first, where, *refs):
    del where
    up_out, down_out = refs[-2:]
    if first:
        up_out[...], down_out[...] = refs[0][...], refs[1][...]
    else:
        up_out[...] = (refs[0][...].astype(f32) + refs[2][...].astype(f32)).astype(bf16)
        down_out[...] = (refs[1][...].astype(f32) + refs[3][...].astype(f32)).astype(bf16)


def hop_blocks(partial, width, where, sums, earlier):
    rows = partial.shape[0]
    tile = max(size for size in range(16, 257, 16) if rows % size == 0)
    plain = pl.BlockSpec((tile, width), lambda i, where: (i, 0))
    return pl.pallas_call(
        functools.partial(hop_kernel, not sums),
        grid_spec=pltpu.PrefetchScalarGridSpec(
            num_scalar_prefetch=1,
            grid=(rows // tile,),
            in_specs=[
                pl.BlockSpec((tile, width), lambda i, where: (i, where[0])),
                pl.BlockSpec((tile, width), lambda i, where: (i, where[1])),
                *[plain for _ in sums],
                *[pl.BlockSpec(memory_space=pl.ANY) for _ in earlier],
            ],
            out_specs=[plain, plain],
        ),
        out_shape=[jax.ShapeDtypeStruct((rows, width), bf16)] * 2,
        compiler_params=pltpu.CompilerParams(vmem_limit_bytes=16 << 20),
        cost_estimate=pl.CostEstimate(flops=2 * rows * width, bytes_accessed=12 * rows * width, transcendentals=0),
    )(where, partial, partial, *sums, *earlier)


class Scatter:
    def __init__(self, partial, count, me):
        self.partial, self.count, self.me, self.hops = partial, count, me, 0
        self.width = partial.shape[1] // count
        self.sums = ()

    def hop(self, *earlier):
        far = self.count - 1 - self.hops
        where = jnp.stack([jnp.minimum(self.me + far, self.count - 1), jnp.maximum(self.me - far, 0)])
        up, down = hop_blocks(self.partial, self.width, where.astype(jnp.int32), self.sums, earlier)
        self.sent = up
        up = lax.ppermute(up, "col", [(i, i + 1) for i in range(self.count - far)])
        down = lax.ppermute(down, "col", [(i, i - 1) for i in range(far, self.count)])
        self.sums = (up, down)
        self.hops += 1

    def result(self):
        while self.hops < self.count - 1:
            self.hop()
        own = lax.dynamic_slice_in_dim(self.partial, self.me * self.width, self.width, 1)
        return own.astype(f32) + self.sums[0].astype(f32) + self.sums[1].astype(f32)


def all_of_col(block, count, me):
    full = jnp.zeros((count,) + block.shape, block.dtype)
    full = lax.dynamic_update_slice_in_dim(full, block[None], me, 0)
    for step in range(1, count):
        got = lax.ppermute(block, "col", [(i, (i + step) % count) for i in range(count)])
        full = lax.dynamic_update_slice_in_dim(full, got[None], lax.rem(me + count - step, count), 0)
    return full


def spans(length):
    return [(max(0, first - SPAN), first, first + SPAN) for first in range(0, length, SPAN)]


def turned(values, cosine, sine):
    return values * cosine + pltpu.roll(values, HEAD_DIM // 2, 1) * sine


def turned_back(values, cosine, sine):
    return values * cosine - pltpu.roll(values, HEAD_DIM // 2, 1) * sine


def soft_weights(query, key, seg_col, seg_row, low, first, high):
    scores = dot_nt(query, key) * HEAD_DIM ** (-0.5)
    shape = (high - first, high - low)
    at_query = first + lax.broadcasted_iota(jnp.int32, shape, 0)
    at_key = low + lax.broadcasted_iota(jnp.int32, shape, 1)
    allowed = (at_key <= at_query) & (seg_col[first:high, :] == seg_row[:, low:high])
    scores = jnp.where(allowed, scores, NEGATIVE)
    weights = jnp.exp(scores - jnp.max(scores, axis=1, keepdims=True))
    return weights / jnp.sum(weights, axis=1, keepdims=True)


def attend_kernel(pre_q, pre_k, pre_v, bias, cosine, sine, seg_col, seg_row, mixed, query, key, value):
    length = pre_q.shape[0]
    query[...] = turned(pre_q[...] + bias[0:1, :], cosine[...], sine[...]).astype(bf16)
    key[...] = turned(pre_k[...] + bias[1:2, :], cosine[...], sine[...]).astype(bf16)
    value[...] = (pre_v[...] + bias[2:3, :]).astype(bf16)
    for low, first, high in spans(length):
        weights = soft_weights(query[first:high, :], key[low:high, :], seg_col, seg_row, low, first, high)
        mixed[first:high, :] = dot_nn(weights.astype(bf16), value[low:high, :]).astype(bf16)


def attend_back_kernel(
    query, key, value, cosine, sine, seg_col, seg_row, grad_mixed, grad_pre, grad_bias, key_sum, value_sum
):
    length = query.shape[0]
    scale = HEAD_DIM ** (-0.5)
    part = pl.program_id(1)

    @pl.when(part == 0)
    def _():
        key_sum[...] = jnp.zeros_like(key_sum)
        value_sum[...] = jnp.zeros_like(value_sum)
        query_bias = jnp.zeros((1, HEAD_DIM), f32)
        for low, first, high in spans(length):
            q, k, v = query[first:high, :], key[low:high, :], value[low:high, :]
            grad = grad_mixed[first:high, :]
            weights = soft_weights(q, k, seg_col, seg_row, low, first, high)
            grad_soft = dot_nt(grad, v)
            inner = jnp.sum(weights * grad_soft, axis=1, keepdims=True)
            grad_scores = (weights * (grad_soft - inner)).astype(bf16)
            grad_query = dot_nn(grad_scores, k) * scale
            grad_query = turned_back(grad_query, cosine[first:high, :], sine[first:high, :]).astype(bf16)
            grad_pre[first:high, :] = grad_query
            query_bias += jnp.sum(grad_query.astype(f32), axis=0, keepdims=True)
            key_sum[low:high, :] += dot_tn(grad_scores, q) * scale
            value_sum[low:high, :] += dot_tn(weights.astype(bf16), grad)
        grad_bias[0:1, :] = query_bias

    @pl.when(part == 1)
    def _():
        grad_key = turned_back(key_sum[...], cosine[...], sine[...]).astype(bf16)
        grad_pre[...] = grad_key
        grad_bias[1:2, :] = jnp.sum(grad_key.astype(f32), axis=0, keepdims=True)

    @pl.when(part == 2)
    def _():
        grad_value = value_sum[...].astype(bf16)
        grad_pre[...] = grad_value
        grad_bias[2:3, :] = jnp.sum(grad_value.astype(f32), axis=0, keepdims=True)


def head_spec(rows, skip=0):
    return pl.BlockSpec((rows, HEAD_DIM), lambda h, *_: (0, skip + h))


def whole_spec(array):
    return pl.BlockSpec(array.shape, lambda *_: (0, 0))


def attend(pre, bias, cosine, sine, seg_col, seg_row):
    length, width = pre.shape[0], pre.shape[1] // 3
    heads = width // HEAD_DIM
    tables = (cosine, sine, seg_col, seg_row)
    return pl.pallas_call(
        attend_kernel,
        grid=(heads,),
        in_specs=[
            head_spec(length),
            head_spec(length, heads),
            head_spec(length, 2 * heads),
            head_spec(3),
            *[whole_spec(table) for table in tables],
        ],
        out_specs=[head_spec(length)] * 4,
        out_shape=[jax.ShapeDtypeStruct((length, width), bf16)] * 4,
        compiler_params=pltpu.CompilerParams(vmem_limit_bytes=32 << 20),
        cost_estimate=pl.CostEstimate(
            flops=width * length * 2 * SPAN * 4, bytes_accessed=20 * length * width, transcendentals=0
        ),
    )(pre, pre, pre, bias, *tables)


def attend_back(query, key, value, cosine, sine, seg_col, seg_row, grad_mixed):
    length, width = query.shape
    heads = width // HEAD_DIM
    tables = (cosine, sine, seg_col, seg_row)
    return pl.pallas_call(
        attend_back_kernel,
        grid=(heads, 3),
        in_specs=[
            *[head_spec(length)] * 3,
            *[whole_spec(table) for table in tables],
            head_spec(length),
        ],
        out_specs=[pl.BlockSpec((length, HEAD_DIM), lambda h, part: (0, part * heads + h)), head_spec(3)],
        out_shape=[
            jax.ShapeDtypeStruct((length, 3 * width), bf16),
            jax.ShapeDtypeStruct((3, width), f32),
        ],
        scratch_shapes=[pltpu.VMEM((length, HEAD_DIM), f32), pltpu.VMEM((length, HEAD_DIM), f32)],
        compiler_params=pltpu.CompilerParams(vmem_limit_bytes=32 << 20),
        cost_estimate=pl.CostEstimate(
            flops=width * length * 2 * SPAN * 10, bytes_accessed=14 * length * width, transcendentals=0
        ),
    )(query, key, value, *tables, grad_mixed)


def tile_of(size, most):
    return max(tile for tile in range(128, most + 1, 128) if size % tile == 0)


def batch_nt_kernel(left, right, *refs):
    refs[-1][0] = dot_nt(left[0], right[0]).astype(bf16)


def batch_nt_tiles(left, right, *earlier):
    count, rows, depth = left.shape
    columns = right.shape[1]
    tile = tile_of(columns, 512)
    return pl.pallas_call(
        batch_nt_kernel,
        grid=(count, columns // tile),
        in_specs=[
            pl.BlockSpec((1, rows, depth), lambda e, n: (e, 0, 0)),
            pl.BlockSpec((1, tile, depth), lambda e, n: (e, n, 0)),
            *[pl.BlockSpec(memory_space=pl.ANY) for _ in earlier],
        ],
        out_specs=pl.BlockSpec((1, rows, tile), lambda e, n: (e, 0, n)),
        out_shape=jax.ShapeDtypeStruct((count, rows, columns), bf16),
        compiler_params=pltpu.CompilerParams(vmem_limit_bytes=56 << 20),
        cost_estimate=pl.CostEstimate(
            flops=2 * count * rows * depth * columns,
            bytes_accessed=2 * count * (rows * depth + depth * columns + rows * columns),
            transcendentals=0,
        ),
    )(left, right, *earlier)


def two_products_kernel(turn, slots, routed, left, right, *refs):
    dot = dot_nt if turn else dot_nn
    refs[-1][...] = (dot_nn(slots[...], routed[...]) + dot(left[...], right[0])).astype(bf16)


def two_products(slots, routed, left, right, turn, *earlier):
    length, depth = slots.shape
    last = right.shape[0] - 1
    inner, columns = left.shape[1], routed.shape[1]
    tile = tile_of(columns, 256)
    return pl.pallas_call(
        functools.partial(two_products_kernel, turn),
        grid=(columns // tile,),
        in_specs=[
            pl.BlockSpec((length, depth), lambda n: (0, 0)),
            pl.BlockSpec((depth, tile), lambda n: (0, n)),
            pl.BlockSpec((length, inner), lambda n: (0, 0)),
            pl.BlockSpec((1, tile, inner), lambda n: (last, n, 0))
            if turn
            else pl.BlockSpec((1, inner, tile), lambda n: (last, 0, n)),
            *[pl.BlockSpec(memory_space=pl.ANY) for _ in earlier],
        ],
        out_specs=pl.BlockSpec((length, tile), lambda n: (0, n)),
        out_shape=jax.ShapeDtypeStruct((length, columns), bf16),
        compiler_params=pltpu.CompilerParams(vmem_limit_bytes=56 << 20),
        cost_estimate=pl.CostEstimate(
            flops=2 * length * columns * (depth + inner),
            bytes_accessed=2 * (length + columns) * (depth + inner),
            transcendentals=0,
        ),
    )(slots, routed, left, right, *earlier)


def rotary_tables(length):
    position = jnp.arange(length).astype(f32)
    exponent = jnp.arange(HEAD_DIM // 2).astype(f32) * (2.0 / HEAD_DIM)
    angles = position[:, None] * jnp.exp(-exponent * jnp.log(THETA))[None, :]
    cosine, sine = jnp.cos(angles), jnp.sin(angles)
    return jnp.concatenate([cosine, cosine], 1), jnp.concatenate([-sine, sine], 1)


def two_terms(values):
    high = values.astype(bf16)
    return high, (values - high.astype(f32)).astype(bf16)


def unwritten(shape, dtype):
    return pl.pallas_call(
        lambda out: None,
        out_specs=pl.BlockSpec(memory_space=pl.ANY),
        out_shape=jax.ShapeDtypeStruct(shape, dtype),
    )()


def stacked(first, last):
    count = first.shape[0]
    both = unwritten((count + last.shape[0],) + first.shape[1:], first.dtype)
    both = lax.dynamic_update_slice_in_dim(both, first, 0, 0)
    return lax.dynamic_update_slice_in_dim(both, last, count, 0)


def beside(parts):
    whole = unwritten((parts[0].shape[0], sum(part.shape[1] for part in parts)), bf16)
    start = 0
    for part in parts:
        whole = lax.dynamic_update_slice_in_dim(whole, part.astype(bf16), start, 1)
        start += part.shape[1]
    return whole


def local(
    rows,
    cols,
    inputs,
    segments,
    routes,
    gain_attn,
    w_query,
    w_key,
    w_value,
    b_query,
    b_key,
    b_value,
    w_out,
    gain_ffn,
    w_router,
    w_expert_gate,
    w_expert_up,
    w_expert_down,
    w_shared_gate,
    w_shared_up,
    w_shared_down,
    w_shared_mix,
    cotangent,
):
    length, part = inputs.shape
    width = part * cols
    experts, depth, hidden = w_expert_gate.shape
    hidden_shared = w_shared_gate.shape[1]
    head_width = w_query.shape[1]
    alike = hidden == hidden_shared
    col = lax.axis_index("col")

    def mine(array, axis=1):
        return lax.dynamic_slice_in_dim(array, col * part, part, axis)

    gain_rows = jnp.stack([*two_terms(gain_attn), *two_terms(gain_ffn)])
    riders = jnp.concatenate([gain_rows, jnp.zeros((12, part), bf16)], 0)
    inputs_gather = Gather(jnp.concatenate([inputs, riders], 0), cols, col)
    inputs_gather.hop()
    first_hop = inputs_gather.up, inputs_gather.down
    inputs_full = inputs_gather.result()
    gain_rows = inputs_full[length : length + 4].astype(f32)
    full_gain_attn = gain_rows[0:1] + gain_rows[1:2]
    full_gain_ffn = gain_rows[2:3] + gain_rows[3:4]

    all_heads = lax.all_gather(jnp.concatenate([w_query, w_key, w_value], 1), "row", axis=0, tiled=True)
    small_rows = jnp.concatenate([w_router.T, w_shared_mix[None], jnp.zeros((7, depth), bf16)], 0)
    expert_in = jnp.concatenate([w_expert_gate, w_expert_up], axis=2)
    shared_in = jnp.concatenate([w_shared_gate, w_shared_up], axis=1)[None]
    shared_down = w_shared_down[None]
    if alike:
        all_in = lax.all_gather(jnp.concatenate([expert_in, shared_in], 0), "row", axis=1, tiled=True)
        all_in = [all_in, all_in]
    else:
        all_in = [lax.all_gather(part, "row", axis=1, tiled=True) for part in (expert_in, shared_in)]
    out_rows = unwritten((width + small_rows.shape[0], depth), bf16)
    out_rows = lax.dynamic_update_slice_in_dim(out_rows, small_rows, width, 0)
    out_block = after(w_out, *first_hop)
    out_rows = lax.dynamic_update_slice_in_dim(out_rows, out_block, col * head_width, 0)
    for step in range(1, cols):
        got = lax.ppermute(out_block, "col", [(i, (i + step) % cols) for i in range(cols)])
        out_rows = lax.dynamic_update_slice_in_dim(out_rows, got, lax.rem(col + cols - step, cols) * head_width, 0)
    all_out = lax.all_gather(out_rows, "row", axis=1, tiled=True)
    all_small = all_out[width:]

    named = jnp.any(routes[:, :, None] == jnp.arange(EXPERTS)[None, None, :], axis=1)
    at = jnp.arange(length)
    earlier = (at[None, :] < at[:, None]).astype(bf16)
    place = dot_nn(earlier, named.astype(bf16))
    kept = named & (place < CAP)
    place_here = lax.dynamic_slice_in_dim(jnp.where(kept, place, -1.0), col * experts, experts, 1)
    slots = (place_here[:, :, None] == jnp.arange(CAP).astype(f32)[None, None, :]).astype(bf16)
    slots = slots.reshape(length, experts * CAP)

    cosine, sine = rotary_tables(length)
    seg_row = segments
    seg_col = segments.T

    inputs_wide = inputs_full[:length].astype(f32)
    inverse_attn = lax.rsqrt(jnp.mean(inputs_wide * inputs_wide, axis=1, keepdims=True) + EPSILON)
    normed = (inputs_wide * inverse_attn * full_gain_attn).astype(bf16)
    bias = jnp.stack([b_query, b_key, b_value])
    mixed, *heads = attend(dot_nn(normed, all_heads), bias, cosine, sine, seg_col, seg_row)
    mixed_full = Gather(mixed, cols, col).result()
    cotangent_gather = Gather(after(cotangent, mixed_full), cols, col)
    cotangent_gather.hop()
    if alike:
        all_down = [jnp.concatenate([w_expert_down, shared_down], 0)]
    else:
        all_down = [w_expert_down, shared_down]
    all_down = [lax.all_gather(after(part, mixed), "row", axis=2, tiled=True) for part in all_down]
    residual = inputs_wide + dot_nn(mixed_full, all_out[:width])
    inverse_ffn = lax.rsqrt(jnp.mean(residual * residual, axis=1, keepdims=True) + EPSILON)
    normed_ffn = (residual * inverse_ffn * full_gain_ffn).astype(bf16)
    residual_mine = mine(residual)
    cotangent_gather.hop(normed_ffn)

    logits = dot_nt(normed_ffn, all_small)[:, : EXPERTS + 1]
    probs = jax.nn.softmax(logits[:, :EXPERTS], axis=-1)
    mix_gate = jax.nn.sigmoid(logits[:, EXPERTS:])
    probs_here = lax.dynamic_slice_in_dim(probs, col * experts, experts, 1)
    slot_gates = sum(dot_tn(slots, term) for term in two_terms(probs_here))
    slot_gate = jnp.concatenate(
        [slot_gates[e * CAP : (e + 1) * CAP, e : e + 1][None] for e in range(experts)], axis=0
    )

    buffer = dot_tn(slots, normed_ffn).astype(bf16).reshape(experts, CAP, width)
    expert_pre = batch_nn(buffer, all_in[0][:experts]).astype(bf16)
    shared_pre = dot_nn(normed_ffn, all_in[1][-1]).astype(bf16)

    def halves(pre):
        half = pre.shape[-1] // 2
        return pre[..., :half].astype(f32), pre[..., half:].astype(f32)

    def activated(pre, scale):
        gate, up = halves(pre)
        return (gate * jax.nn.sigmoid(gate) * up * scale).astype(bf16)

    cotangent_gather.hop(expert_pre)
    cotangent_full = after(cotangent_gather.result(), shared_pre)
    expert_act = activated(expert_pre, slot_gate)
    shared_act = activated(shared_pre, mix_gate)
    cotangent_slot = dot_tn(slots, cotangent_full).astype(bf16).reshape(experts, CAP, width)
    grad_expert_down = batch_tn(expert_act, cotangent_slot).astype(bf16)
    grad_shared_down = dot_tn(shared_act, cotangent_full).astype(bf16)[None]
    if alike:
        grad_downs = [(stacked(grad_expert_down, grad_shared_down), 2)]
    else:
        grad_downs = [(grad_expert_down, 2), (grad_shared_down, 2)]
    all_down = [after(part, *[grad for grad, _ in grad_downs]) for part in all_down]
    expert_down, shared_down = all_down[0][:experts], all_down[-1][-1]

    def pre_back(pre, grad_act, scale):
        gate, up = halves(pre)
        sigmoid = jax.nn.sigmoid(gate)
        silu = gate * sigmoid
        dots = jnp.sum(silu * up * grad_act, axis=-1)
        scaled = grad_act * scale
        grad_gate = scaled * up * sigmoid * (1.0 + gate * (1.0 - sigmoid))
        grad_up = scaled * silu
        stat = jnp.sum(grad_gate * gate + grad_up * up, axis=-1)
        return jnp.concatenate([grad_gate.astype(bf16), grad_up.astype(bf16)], axis=-1), dots, stat

    grad_expert_pre, expert_dots, expert_stat = pre_back(
        expert_pre, batch_nt(cotangent_slot, expert_down), slot_gate
    )
    grad_shared_pre, shared_dots, shared_stat = pre_back(
        shared_pre, dot_nt(cotangent_full, shared_down), mix_gate
    )
    told = []
    stat_sum = shared_stat
    for e in range(experts):
        terms = jnp.stack([*two_terms(expert_dots[e]), *two_terms(expert_stat[e])], axis=1)
        found = dot_nn(slots[:, e * CAP : (e + 1) * CAP], terms)
        told.append(found[:, 0] + found[:, 1])
        stat_sum = stat_sum + found[:, 2] + found[:, 3]
    told_here = jnp.stack([*told, shared_dots, stat_sum])

    told = all_of_col(told_here, cols, col)
    grad_buffer = batch_nt_tiles(grad_expert_pre, all_in[0], told_here).reshape(experts * CAP, width)
    grad_partial = two_products(slots, grad_buffer, grad_shared_pre, all_in[1], True, told)

    scatter = Scatter(grad_partial, cols, col)
    scatter.hop()
    grad_expert_in = batch_tn(buffer, after(grad_expert_pre, grad_partial)).astype(bf16)
    scatter.hop(grad_expert_in)
    grad_shared_in = dot_tn(normed_ffn, after(grad_shared_pre, grad_partial, grad_expert_in)).astype(bf16)[None]
    if alike:
        grad_ins = [(stacked(grad_expert_in, grad_shared_in), 1)]
    else:
        grad_ins = [(grad_expert_in, 1), (grad_shared_in, 1)]
    scatter.hop(grad_ins[-1][0])
    expert_out = batch_nn(after(expert_act, scatter.sent), expert_down).astype(bf16).reshape(experts * CAP, width)
    sums_mark = scatter.sent
    grad_probs = told[:, :experts].reshape(EXPERTS, length).T
    grad_mix = jnp.sum(told[:, experts], axis=0)[:, None] * mix_gate * (1.0 - mix_gate)
    grad_logits = probs * (grad_probs - jnp.sum(probs * grad_probs, axis=1, keepdims=True))
    grad_small = jnp.concatenate([grad_logits, grad_mix], axis=1)
    ffn_stat = (
        jnp.sum(told[:, experts + 1], axis=0)[:, None] + jnp.sum(grad_small * logits, axis=1, keepdims=True)
    ) / inverse_ffn

    grad_ffn = scatter.result() + dot_nt(grad_small.astype(bf16), mine(all_small, 1)[: EXPERTS + 1].T)
    grad_gain_ffn = jnp.sum(grad_ffn * residual_mine * inverse_ffn, axis=0)
    grad_residual = (
        cotangent.astype(f32)
        + gain_ffn[None, :] * grad_ffn * inverse_ffn
        - residual_mine * (inverse_ffn**3 * ffn_stat / width)
    )

    def scattered(grads):
        return [lax.psum_scatter(grad, "row", scatter_dimension=axis, tiled=True) for grad, axis in grads]

    downs = scattered(grad_downs)
    ins = scattered([(after(grad, downs[-1], sums_mark), axis) for grad, axis in grad_ins])
    grad_expert_down, grad_shared_down = (downs[0][:experts], downs[0][experts]) if alike else (downs[0], downs[1][0])
    grad_expert_down, grad_shared_down = grad_expert_down.astype(f32), grad_shared_down.astype(f32)

    gather = Gather(after(grad_residual.astype(bf16), expert_out), cols, col)
    gather.hop()
    ffn_partial = two_products(slots, expert_out, shared_act, all_down[-1], False, grad_residual)
    scatter = Scatter(ffn_partial, cols, col)
    gather.hop(ffn_partial)
    scatter.hop(gather.up_before)
    while gather.hops < cols - 1:
        gather.hop(*scatter.sums)
        scatter.hop(gather.up_before)
    grad_res_full = after(gather.result(), *scatter.sums)
    output = residual_mine + scatter.result()
    out_sums = scatter.sums

    out_mine = lax.dynamic_slice_in_dim(all_out, col * head_width, head_width, 0)
    grad_mixed = dot_nt(grad_res_full, out_mine).astype(bf16)
    grad_heads, grad_bias = attend_back(*heads, cosine, sine, seg_col, seg_row, grad_mixed)
    grad_heads = after(grad_heads, *out_sums)
    normed_partial = dot_nt(grad_heads, all_heads)
    attn_stat = jnp.sum(normed_partial * inputs_wide * full_gain_attn, axis=1)
    stat_rows = attn_stat.astype(bf16).reshape(-1, part)
    stat_rows = jnp.concatenate([stat_rows, jnp.zeros((16 - length // part % 16, part), bf16)], 0)
    normed_partial = normed_partial.astype(bf16)
    ridden = unwritten((length + stat_rows.shape[0], width), bf16)
    ridden = lax.dynamic_update_slice_in_dim(ridden, normed_partial, 0, 0)
    ridden = lax.dynamic_update_slice_in_dim(ridden, jnp.tile(stat_rows, (1, cols)), length, 0)
    scatter = Scatter(ridden, cols, col)
    scatter.hop(output)
    late_heads = after(grad_heads, ridden)
    small_columns = dot_tn(normed_ffn, grad_small.astype(bf16))
    small_columns = jnp.concatenate([small_columns, jnp.zeros((width, 119), f32)], 1)
    attention = beside(
        [dot_tn(normed, late_heads), dot_tn(grad_res_full, mixed), small_columns]
    )
    scatter.hop(attention, grad_expert_down, grad_shared_down)
    attention_mark = scatter.sent
    grad_attn = scatter.result()
    attn_stat = grad_attn[length : length + length // part].reshape(-1, 1)
    grad_attn = grad_attn[:length]
    grad_gain_attn = jnp.sum(grad_attn * inputs.astype(f32) * inverse_attn, axis=0)
    input_grad = (
        grad_residual
        + gain_attn[None, :] * grad_attn * inverse_attn
        - inputs.astype(f32) * (inverse_attn**3 * attn_stat / width)
    )

    if alike:
        grad_expert_in, grad_shared_in = ins[0][:experts], ins[0][experts]
    else:
        grad_expert_in, grad_shared_in = ins[0], ins[1][0]
    grad_expert_in, grad_shared_in = grad_expert_in.astype(f32), grad_shared_in.astype(f32)
    [attention] = scattered([(after(attention, ins[-1], attention_mark), 0)])
    attention = attention.astype(f32)
    grad_query, grad_key, grad_value, grad_out = [
        attention[:, i * head_width : (i + 1) * head_width] for i in range(4)
    ]
    grad_out = grad_out.T
    grad_small = attention[:, 4 * head_width :]

    vectors = jnp.concatenate([grad_gain_attn[None], grad_gain_ffn[None], grad_bias], 0)
    sums = lax.psum(vectors, "row")
    return (
        output,
        input_grad,
        sums[0],
        grad_query,
        grad_key,
        grad_value,
        sums[2],
        sums[3],
        sums[4],
        grad_out,
        sums[1],
        grad_small[:, :EXPERTS],
        grad_expert_in[:, :, :hidden],
        grad_expert_in[:, :, hidden:],
        grad_expert_down,
        grad_shared_in[:, :hidden_shared],
        grad_shared_in[:, hidden_shared:],
        grad_shared_down,
        grad_small[:, EXPERTS],
    )


def solution(mesh):
    in_specs = (
        P("row", "col"),
        P("row", None),
        P("row", None),
        P("col"),
        P("row", "col"),
        P("row", "col"),
        P("row", "col"),
        P("col"),
        P("col"),
        P("col"),
        P("col", "row"),
        P("col"),
        P("row", None),
        P("col", "row", None),
        P("col", "row", None),
        P("col", None, "row"),
        P("row", "col"),
        P("row", "col"),
        P("col", "row"),
        P("row"),
        P("row", "col"),
    )
    out_specs = (
        P("row", "col"),
        P("row", "col"),
        P("col"),
        P("row", "col"),
        P("row", "col"),
        P("row", "col"),
        P("col"),
        P("col"),
        P("col"),
        P("col", "row"),
        P("col"),
        P("row", None),
        P("col", "row", None),
        P("col", "row", None),
        P("col", None, "row"),
        P("row", "col"),
        P("row", "col"),
        P("col", "row"),
        P("row"),
    )
    body = functools.partial(local, mesh.shape["row"], mesh.shape["col"])
    return jax.shard_map(body, mesh=mesh, in_specs=in_specs, out_specs=out_specs, check_vma=False)
```

time: 1160 us -> 888 us (0.77)
  waiting for transfers between devices: 393 us -> 224 us
  Pallas kernels: 25.9 us -> 107 us
  matrix products: 313 us -> 235 us
  blocking collectives: 90.6 us -> 22.6 us
  local copies, waits for them, and re-layouts: 50.5 us -> 99.4 us
  other arithmetic: 122 us -> 80.8 us
  starting transfers between devices: 134 us -> 95 us
    ppermute x48 -> x45, waiting for transfers between devices: 298 us -> 201 us  [the longest x12 91.9 us: hop(): lax.ppermute(self.down, 'col', [(i, i - 1) for i in range(1, count - done)])]
    pallas_call x2 -> x37, Pallas kernels: 25.9 us -> 107 us  [the longest x2 42.9 us: two_products(): pl.pallas_call(functools.partial(two_products_kernel, turn), grid=(column...]
    reduce_scatter x3, waiting for transfers between devices: 52.5 us -> 0.01 us  [scattered(): lax.psum_scatter(grad, 'row', scatter_dimension=axis, tiled=True)]
    all_gather x2 -> x0, blocking collectives: 50.3 us -> none  [the longest x1 40.8 us: local(): lax.all_gather(jnp.stack([gain_attn, gain_ffn]), 'col', axis=1, tiled=True)]
    dot_general x10 -> x6, matrix products: 88.5 us -> 43.2 us  [dot_nn(): return jnp.dot(left, right, preferred_element_type=f32)]
    unnamed x166 -> x241, local copies, waits for them, and re-layouts: 18 us -> 57.9 us
    concatenate x8 -> x5, other arithmetic: 46.8 us -> 9.7 us  [the longest x2 6.11 us: pre_back(): jnp.concatenate([grad_gate.astype(bf16), grad_up.astype(bf16)], axis=-1)]
    ppermute x6 -> x3, starting transfers between devices: 33.9 us -> 5.42 us  [all_of_col(): lax.ppermute(block, 'col', [(i, (i + step) % count) for i in range(count)])]
  transfers between devices with their start and end apart: 62 -> 55, of which waited for: 27 -> 23; matrix products, arithmetic and copies ran while one was open for 31% -> 40% of each run, Pallas kernels for 2% -> 12%
where the time goes in v2:
time: 888 us; the launch traced here: 881 us
  matrix products  235 us (26%)
  waiting for transfers between devices  224 us (25%)
  Pallas kernels  107 us (12%)
  local copies, waits for them, and re-layouts  99.4 us (11%)
  starting transfers between devices  95 us (11%)
  other arithmetic  80.8 us (9%)
  blocking collectives  22.6 us (3%)
  between operations  16.4 us (2%)
    ppermute x12, waiting for transfers between devices, hop(): lax.ppermute(self.down, 'col', [(i, i - 1) for i in range(1, count - done)])  91.9 us
    ppermute x9, waiting for transfers between devices, hop(): up = lax.ppermute(up, 'col', [(i, i + 1) for i in range(self.count - far)])  62.6 us
    dot_general x9, matrix products, dot_tn(): lax.dot_general(left, right, (((0,), (0,)), ((), ())), preferred_element_...  60.5 us
    unnamed x241, local copies, waits for them, and re-layouts  57.9 us
    dot_general x6, matrix products, dot_nn(): return jnp.dot(left, right, preferred_element_type=f32)  43.2 us
    pallas_call x2, Pallas kernels, two_products(): pl.pallas_call(functools.partial(two_products_kernel, turn), grid=(column...  42.9 us
    dot_general x5, matrix products, dot_nt(): lax.dot_general(left, right, (((1,), (1,)), ((), ())), preferred_element_...  41.3 us
    ppermute x9, starting transfers between devices, hop(): up = lax.ppermute(up, 'col', [(i, i + 1) for i in range(self.count - far)])  39.4 us
  transfers between devices with their start and end apart: 55, of which 23 were waited for; matrix products, arithmetic and copies ran while one was open for 40% of the time, Pallas kernels for 12%

profile of v2, /device:TPU:0, one launch (start us, length us, event | category | flops | bytes accessed | tf_op | source)
XLA Modules:
  0.0 880.6 jit_solution(13490035223564505867)
XLA Ops:
  16.6 6.0 collective-permute-start
  24.0 20.3 %collective-permute-done.refs_1_ = bf16[1040,512]{1,0:T(8,128)(2,1)} collective-permute-done((bf16[1040,512]{1,0:T(8,128)(2,1)S(1)}, bf16[1040,512]{1,0:T(8,128)(2,1)}, u32[]{:S(2)}, u32[]{:S(2)}) %collective-permute-start) | collective-permute-done | bytes 1064992 | tf_op jit(solution)/shard_map/ppermute | solution.py:85
  44.3 5.1 collective-permute-done.1.refs_2_
  63.5 7.4 collective-permute-done.13
  87.9 26.4 %collective-permute-done.3 = bf16[1040,512]{1,0:T(8,128)(2,1)S(1)} collective-permute-done((bf16[1040,512]{1,0:T(8,128)(2,1)S(1)}, bf16[1040,512]{1,0:T(8,128)(2,1)S(1)}, u32[]{:S(2)}, u32[]{:S(2)}) %collective-permute-start.3) | collective-permute-done | bytes 1064992 | tf_op jit(solution)/shard_map/ppermute | solution.py:86
  117.0 22.4 %collective-permute-done.5 = bf16[1040,512]{1,0:T(8,128)(2,1)S(1)} collective-permute-done((bf16[1040,512]{1,0:T(8,128)(2,1)S(1)}, bf16[1040,512]{1,0:T(8,128)(2,1)S(1)}, u32[]{:S(2)}, u32[]{:S(2)}) %collective-permute-start.5) | collective-permute-done | bytes 1064992 | tf_op jit(solution)/shard_map/ppermute | solution.py:86
  141.8 12.1 %fusion.62.pre_q.pre_k.pre_v = f32[1024,1536]{1,0:T(8,128)S(1)} fusion(bf16[2048,1536]{1,0:T(8,128)(2,1)} %all-gather.5.cloned.1.call-done, f32[2048]{0:T(1024)S(1)} %bitcast.187, f32[1024]{0:T(1024)S(1)} %add_rsqrt_fusion.1, bf16[1040,2048]{1,0:T(8,128)(2,1)} %copy-done.58), kind=kOutput, calls=%fused_computation.137 | convolution fusion | flops 6450839552 | bytes 16789504 | tf_op jit(solution)/shard_map/dot_general | solution.py:25
  154.0 12.4 %shard_map.348 = (bf16[1024,512]{1,0:T(8,128)(2,1)S(1)}, bf16[1024,512]{1,0:T(8,128)(2,1)S(1)}, bf16[1024,512]{1,0:T(8,128)(2,1)S(1)}, bf16[1024,512]{1,0:T(8,128)(2,1)S(1)}) custom-call(f32[1024,1536]{1,0:T(8,128)S(1)} %fusion.62.pre_q.pre_k.pre_v, f32[1024,1536]{1,0:T(8,128)S(1)} %fusion.62.pre_q.pre_k.pre_v, f32[1024,1536]{1,0:T(8,128)S(1)} %fusion.62.pre_q.pre_k.pre_v, ...), custom_call_target="tpu_custom_call" | custom-call | flops 1073741824 | bytes 10485760 | tf_op jit(solution)/shard_map/pallas_call | solution.py:246
  180.6 6.1 copy.81
  209.3 10.8 %collective-permute-done.9 = bf16[1024,512]{1,0:T(8,128)(2,1)S(1)} collective-permute-done((bf16[1024,512]{1,0:T(8,128)(2,1)S(1)}, bf16[1024,512]{1,0:T(8,128)(2,1)S(1)}, u32[]{:S(2)}, u32[]{:S(2)}) %collective-permute-start.9) | collective-permute-done | bytes 1048608 | tf_op jit(solution)/shard_map/ppermute | solution.py:86
  227.0 13.6 %collective-permute-done.11 = bf16[1024,512]{1,0:T(8,128)(2,1)S(1)} collective-permute-done((bf16[1024,512]{1,0:T(8,128)(2,1)S(1)}, bf16[1024,512]{1,0:T(8,128)(2,1)S(1)}, u32[]{:S(2)}, u32[]{:S(2)}) %collective-permute-start.11) | collective-permute-done | bytes 1048608 | tf_op jit(solution)/shard_map/ppermute | solution.py:86
  248.5 13.4 %multiply_reduce_fusion = (f32[1024]{0:T(1024)S(1)}, f32[1024,2048]{1,0:T(8,128)S(1)}) fusion(bf16[1024,2048]{1,0:T(8,128)(2,1)} %select_dynamic-update-slice_fusion.18.refs_1_, bf16[2064,2048]{1,0:T(8,128)(2,1)} %all-gather.7.cloned.1.call-done, bf16[1040,2048]{1,0:T(8,128)(2,1)} %copy-done.58), kind=kOutput, calls=%fused_computation.37 | convolution fusion | flops 8598322176 | bytes 25169920 | tf_op jit(solution)/shard_map/dot_general | solution.py:25
  280.3 6.9 convolution_convert_fusion.2
  287.2 13.9 %all-gather.9.cloned.1.call-done.right = bf16[3,2048,2816]{2,1,0:T(8,128)(2,1)} async-done(((bf16[3,256,2816]{2,1,0:T(8,128)(2,1)}), bf16[3,2048,2816]{2,1,0:T(8,128)(2,1)}) %all-gather.9.cloned.1.call-update) | async-done | bytes 34603024 | tf_op jit(solution)/shard_map/all_gather | solution.py:443
  301.0 22.4 %fusion.25.refs_2_ = bf16[2,576,2816]{2,1,0:T(8,128)(2,1)} fusion(bf16[2,576,2048]{2,1,0:T(8,128)(2,1)} %bitcast.209, bf16[3,2048,2816]{2,1,0:T(8,128)(2,1)} %all-gather.9.cloned.1.call-done.right), kind=kOutput, calls=%fused_computation.57 | convolution fusion | flops 13290799104 | bytes 34275328 | tf_op jit(solution)/shard_map/ecd,edf->ecf/dot_general | solution.py:37
  325.9 5.7 multiply_convert_fusion.1.refs_0_
  331.6 15.8 %fusion.37.refs_1_ = bf16[1024,2816]{1,0:T(8,128)(2,1)S(1)} fusion(bf16[1024,2048]{1,0:T(8,128)(2,1)S(1)} %copy-done.55, bf16[3,2048,2816]{2,1,0:T(8,128)(2,1)} %all-gather.9.cloned.1.call-done.right), kind=kOutput, calls=%fused_computation.71 | convolution fusion | flops 11814043648 | bytes 21495808 | tf_op jit(solution)/shard_map/dot_general | solution.py:25
  357.9 7.9 convolution_convert_fusion.1
  365.9 12.1 %convert_dynamic-update-slice_fusion = bf16[3,1408,2048]{2,1,0:T(8,128)(2,1)} fusion(bf16[3,1408,2048]{2,1,0:T(8,128)(2,1)} %shard_map.356, bf16[2,576,1408]{2,1,0:T(8,128)(2,1)S(1)} %copy-done.62, bf16[2,576,2048]{2,1,0:T(8,128)(2,1)S(1)} %bitcast.211), kind=kOutput, calls=%fused_computation.10 | convolution fusion | flops 6649544704 | bytes 19496960 | tf_op jit(solution)/shard_map/ecd,ecf->edf/dot_general | solution.py:45
  378.0 10.6 %fusion.16.refs_1_ = bf16[3,1408,2048]{2,1,0:T(8,128)(2,1)} fusion(bf16[3,1408,2048]{2,1,0:T(8,128)(2,1)} %convert_dynamic-update-slice_fusion, bf16[1024,1408]{1,0:T(8,128)(2,1)S(1)} %copy-done.77, bf16[1024,2048]{1,0:T(8,128)(2,1)} %shard_map.354), kind=kOutput, calls=%fused_computation.44 | convolution fusion | flops 5908463616 | bytes 12845056 | tf_op jit(solution)/shard_map/dot_general | solution.py:33
  389.0 9.8 %all-gather.11.cloned.1.call-done.refs_0_ = bf16[3,1408,2048]{2,1,0:T(8,128)(2,1)} async-done(((bf16[3,1408,256]{2,1,0:T(8,128)(2,1)}), bf16[3,1408,2048]{2,1,0:T(8,128)(2,1)}) %all-gather.11.cloned.1.call-update) | async-done | bytes 17301520 | tf_op jit(solution)/shard_map/all_gather | solution.py:482
  398.8 14.9 %multiply_reduce_fusion.1 = (f32[2,576]{1,0:T(2,128)S(1)}, f32[2,576]{1,0:T(2,128)S(1)}, bf16[2,576,1408]{2,1,0:T(8,128)(2,1)S(1)}, bf16[2,576,1408]{2,1,0:T(8,128)(2,1)S(1)}) fusion(bf16[2,576,2816]{2,1,0:T(8,128)(2,1)} %fusion.25.refs_2_, f32[2,576]{1,0:T(2,128)S(1)} %maximum_bitcast_fusion.1, bf16[2,576,2048]{2,1,0:T(8,128)(2,1)} %bitcast.212, ...), kind=kOutput, calls=%fused_computation.54 | convolution fusion | flops 6681081856 | bytes 29242880 | tf_op jit(solution)/shard_map/ecf,edf->ecd/dot_general | solution.py:41
  415.3 16.2 %multiply_reduce_fusion.2 = (f32[1024]{0:T(1024)S(1)}, f32[1024]{0:T(1024)S(1)}, bf16[1024,1408]{1,0:T(8,128)(2,1)S(1)}, bf16[1024,1408]{1,0:T(8,128)(2,1)S(1)}) fusion(bf16[1024,2816]{1,0:T(8,128)(2,1)} %copy-done.60, f32[1024]{0:T(1024)S(1)} %bitcast.192, bf16[1024,2048]{1,0:T(8,128)(2,1)} %shard_map.354, bf16[3,1408,2048]{2,1,0:T(8,128)(2,1)} %shard_map.357.right), kind=kOutput, calls=%fused_computation.69 | convolution fusion | flops 5938739200 | bytes 21508096 | tf_op jit(solution)/shard_map/dot_general | solution.py:29
  443.0 21.2 %shard_map.358 = bf16[2,576,2048]{2,1,0:T(8,128)(2,1)} custom-call(bf16[2,576,2816]{2,1,0:T(8,128)(2,1)} %pad_maximum_fusion.left.refs_0_, bf16[3,2048,2816]{2,1,0:T(8,128)(2,1)} %all-gather.9.cloned.1.call-done.right, f32[4,1024]{1,0:T(4,128)} %copy-done.100), custom_call_target="tpu_custom_call" | custom-call | flops 13287555072 | bytes 34275328 | tf_op jit(solution)/shard_map/pallas_call | solution.py:302
  465.0 24.4 %shard_map.359.refs_0_.refs_1_ = bf16[1024,2048]{1,0:T(8,128)(2,1)} custom-call(bf16[1024,1152]{1,0:T(8,128)(2,1)} %get-tuple-element.171.slots, bf16[1152,2048]{1,0:T(8,128)(2,1)} %bitcast.213, bf16[1024,2816]{1,0:T(8,128)(2,1)} %pad_maximum_fusion.1.left.refs_0_, bf16[3,2048,2816]{2,1,0:T(8,128)(2,1)} %all-gather.9.cloned.1.call-done.right, ...), custom_call_target="tpu_custom_call" | custom-call | flops 16642998272 | bytes 24379392 | tf_op jit(solution)/shard_map/pallas_call | solution.py:331
  496.7 26.3 %constant_dynamic-update-slice_fusion.2 = (bf16[3,2048,2816]{2,1,0:T(8,128)(2,1)}, bf16[2,2048,2816]{2,1,0:T(8,128)(2,1)}) fusion(bf16[3,2048,2816]{2,1,0:T(8,128)(2,1)} %shard_map.363, bf16[2,576,2048]{2,1,0:T(8,128)(2,1)} %bitcast.210, bf16[2,576,2816]{2,1,0:T(8,128)(2,1)} %shard_map.361), kind=kOutput, calls=%fused_computation.176 | convolution fusion | flops 13299089408 | bytes 57344000 | tf_op jit(solution)/shard_map/ecd,ecf->edf/dot_general | solution.py:45
  525.2 7.6 copy-done.9
  536.7 15.4 %bitcast_dynamic-update-slice_fusion.refs_4_.refs_0_ = bf16[3,2048,2816]{2,1,0:T(8,128)(2,1)} fusion(bf16[3,2048,2816]{2,1,0:T(8,128)(2,1)} %get-tuple-element.209, bf16[1024,2048]{1,0:T(8,128)(2,1)S(1)} %copy-done.56, bf16[1024,2816]{1,0:T(8,128)(2,1)S(1)} %copy-done.59), kind=kOutput, calls=%fused_computation.9 | convolution fusion | flops 11816927232 | bytes 21495808 | tf_op jit(solution)/shard_map/dot_general | solution.py:33
  552.1 6.3 collective-permute-done.26.refs_2_
  562.0 7.5 collective-permute-start.28
  571.2 14.4 %fusion.41 = bf16[2,576,2048]{2,1,0:T(8,128)(2,1)} fusion(bf16[2,576,1408]{2,1,0:T(8,128)(2,1)} %shard_map.366, bf16[3,1408,2048]{2,1,0:T(8,128)(2,1)} %shard_map.357.right), kind=kOutput, calls=%fused_computation.77 | convolution fusion | flops 6646136832 | bytes 19496960 | tf_op jit(solution)/shard_map/ecd,edf->ecf/dot_general | solution.py:37
  589.5 5.5 collective-permute-done.29
  594.9 5.0 fusion.122
  602.8 18.5 %shard_map.367.refs_2_.refs_0_.refs_1_ = bf16[1024,2048]{1,0:T(8,128)(2,1)} custom-call(bf16[1024,1152]{1,0:T(8,128)(2,1)} %get-tuple-element.171.slots, bf16[1152,2048]{1,0:T(8,128)(2,1)} %bitcast.183, bf16[1024,1408]{1,0:T(8,128)(2,1)} %multiply_convert_fusion.2.left, bf16[3,1408,2048]{2,1,0:T(8,128)(2,1)} %shard_map.357.right, ...), custom_call_target="tpu_custom_call" | custom-call | flops 10737418240 | bytes 15728640 | tf_op jit(solution)/shard_map/pallas_call | solution.py:331
  646.4 9.4 %collective-permute-done.32.refs_2_ = bf16[1024,512]{1,0:T(8,128)(2,1)S(1)} collective-permute-done((bf16[1024,512]{1,0:T(8,128)(2,1)}, bf16[1024,512]{1,0:T(8,128)(2,1)S(1)}, u32[]{:S(2)}, u32[]{:S(2)}) %collective-permute-start.32) | collective-permute-done | bytes 1048608 | tf_op jit(solution)/shard_map/ppermute | solution.py:140
  655.8 4.9 collective-permute-done.35.refs_1_
  680.6 8.1 collective-permute-done.36.refs_2_.refs_1_
  691.3 7.2 collective-permute-start.38
  703.0 5.4 fusion.55.grad_mixed
  708.5 15.3 %shard_map.376 = (bf16[1024,1536]{1,0:T(8,128)(2,1)S(1)}, f32[3,512]{1,0:T(4,128)S(1)}) custom-call(bf16[1024,512]{1,0:T(8,128)(2,1)S(1)} %copy-done.47, bf16[1024,512]{1,0:T(8,128)(2,1)S(1)} %copy-done.49, bf16[1024,512]{1,0:T(8,128)(2,1)S(1)} %copy-done.51, f32[1024,128]{1,0:T(8,128)S(1)} %copy-done.33, f32[1024,128]{1,0:T(8,128)S(1)} %copy-done.35, ...), custom_call_target="tpu_custom_call" | custom-call | flops 2684354560 | bytes 7340032 | tf_op jit(solution)/shard_map/pallas_call | solution.py:269
  726.8 11.3 %convert_dynamic-update-slice_fusion.1 = (bf16[1040,2048]{1,0:T(8,128)(2,1)}, f32[1024,2048]{1,0:T(8,128)S(1)}) fusion(bf16[1040,2048]{1,0:T(8,128)(2,1)} %shard_map.374, bf16[1024,1536]{1,0:T(8,128)(2,1)} %shard_map.377.refs_0_, bf16[2048,1536]{1,0:T(8,128)(2,1)} %all-gather.5.cloned.1.call-done), kind=kOutput, calls=%fused_computation.74 | convolution fusion | flops 6444548096 | bytes 22020096 | tf_op jit(solution)/shard_map/dot_general | solution.py:29
  746.7 5.0 collective-permute-start.42
  752.8 9.1 %fusion.14 = bf16[2048,2176]{1,0:T(8,128)(2,1)} fusion(bf16[2048,2176]{1,0:T(8,128)(2,1)} %shard_map.379, bf16[1024,1536]{1,0:T(8,128)(2,1)S(1)} %copy-done.14, f32[2048]{0:T(1024)S(1)} %bitcast.189, f32[1024]{0:T(1024)S(1)} %copy-done.98, bf16[1040,2048]{1,0:T(8,128)(2,1)S(1)} %bitcast.178), kind=kOutput, calls=%fused_computation.41 | convolution fusion | flops 6453985280 | bytes 13643776 | tf_op jit(solution)/shard_map/dot_general | solution.py:33
  761.9 6.1 fusion.44
  782.3 17.9 %collective-permute-done.44.refs_2_ = bf16[1040,512]{1,0:T(8,128)(2,1)S(1)} collective-permute-done((bf16[1040,512]{1,0:T(8,128)(2,1)S(1)}, bf16[1040,512]{1,0:T(8,128)(2,1)S(1)}, u32[]{:S(2)}, u32[]{:S(2)}) %collective-permute-start.44) | collective-permute-done | bytes 1064992 | tf_op jit(solution)/shard_map/ppermute | solution.py:140
  803.9 7.7 collective-permute-start.46
  813.0 17.1 %collective-permute-done.46 = bf16[1040,512]{1,0:T(8,128)(2,1)S(1)} collective-permute-done((bf16[1040,512]{1,0:T(8,128)(2,1)S(1)}, bf16[1040,512]{1,0:T(8,128)(2,1)S(1)}, u32[]{:S(2)}, u32[]{:S(2)}) %collective-permute-start.46) | collective-permute-done | bytes 1064992 | tf_op jit(solution)/shard_map/ppermute | solution.py:140
  838.3 22.6 %psum.7 = f32[5,512]{1,0:T(8,128)S(1)} all-reduce(f32[5,512]{1,0:T(8,128)S(1)} %pad_maximum_fusion.9), channel_id=1, replica_groups=mesh['row'=8,'col'=4] {'row'}, use_global_device_ids=true, to_apply=%region_17.18 | all-reduce | flops 2560 | bytes 20480 | tf_op jit(solution)/shard_map/psum | solution.py:649
  (508 shorter events, 272.6 us)
Async XLA Ops:
  7.2 134.6 %all-gather.5.cloned.1.call-start = ((), (), s32[]{:S(2)}) async-start(), calls=%async_computation.3 | async-start | bytes 7077888 | tf_op jit(solution)/shard_map/all_gather | solution.py:437
  11.0 237.5 %all-gather.7.cloned.1.call-start = ((), (), s32[]{:S(2)}) async-start(), calls=%async_computation.4 | async-start | bytes 9510912 | tf_op jit(solution)/shard_map/all_gather | solution.py:454
  16.6 27.7 %collective-permute-start = (bf16[1040,512]{1,0:T(8,128)(2,1)S(1)}, bf16[1040,512]{1,0:T(8,128)(2,1)}, u32[]{:S(2)}, u32[]{:S(2)}) collective-permute-start(bf16[1040,512]{1,0:T(8,128)(2,1)S(1)} %concatenate.48), channel_id=1, source_target_pairs={{0,1},{1,2},{2,3},{4,5},{5,6},{6,7},{8,9},{9,10},{10,11},{12,13},{... | collective-permute-start | bytes 3194888 | tf_op jit(solution)/shard_map/ppermute | solution.py:85
  22.6 26.9 %collective-permute-start.1 = (bf16[1040,512]{1,0:T(8,128)(2,1)S(1)}, bf16[1040,512]{1,0:T(8,128)(2,1)S(1)}, u32[]{:S(2)}, u32[]{:S(2)}) collective-permute-start(bf16[1040,512]{1,0:T(8,128)(2,1)S(1)} %concatenate.48), channel_id=1, source_target_pairs={{1,0},{2,1},{3,2},{5,4},{6,5},{7,6},{9,8},{10,9},{11,10},{13,12},{... | collective-permute-start | bytes 3194888 | tf_op jit(solution)/shard_map/ppermute | solution.py:86
  51.0 19.9 %collective-permute-start.13 = (bf16[512,256]{1,0:T(8,128)(2,1)}, bf16[512,256]{1,0:T(8,128)(2,1)}, u32[]{:S(2)}, u32[]{:S(2)}) collective-permute-start(bf16[512,256]{1,0:T(8,128)(2,1)} %shard_map.350), channel_id=1, source_target_pairs={{0,2},{1,3},{2,0},{3,1},{4,6},{5,7},{6,4},{7,5},{8,10},{9,11},{10,... | collective-permute-start | bytes 786440 | tf_op jit(solution)/shard_map/ppermute | solution.py:452
  52.7 19.9 %collective-permute-start.14 = (bf16[512,256]{1,0:T(8,128)(2,1)}, bf16[512,256]{1,0:T(8,128)(2,1)S(1)}, u32[]{:S(2)}, u32[]{:S(2)}) collective-permute-start(bf16[512,256]{1,0:T(8,128)(2,1)} %shard_map.350), channel_id=1, source_target_pairs={{0,3},{1,0},{2,1},{3,2},{4,7},{5,4},{6,5},{7,6},{8,11},{9,8},{10,9... | collective-permute-start | bytes 786440 | tf_op jit(solution)/shard_map/ppermute | solution.py:452
  73.4 227.7 %all-gather.9.cloned.1.call-start = ((), (), s32[]{:S(2)}) async-start(), calls=%async_computation.5 | async-start | bytes 38928384 | tf_op jit(solution)/shard_map/all_gather | solution.py:443
  78.0 320.8 %all-gather.11.cloned.1.call-start = ((), (), s32[]{:S(2)}) async-start(), calls=%async_computation.6 | async-start | bytes 19464192 | tf_op jit(solution)/shard_map/all_gather | solution.py:482
  85.1 29.2 %collective-permute-start.3 = (bf16[1040,512]{1,0:T(8,128)(2,1)S(1)}, bf16[1040,512]{1,0:T(8,128)(2,1)S(1)}, u32[]{:S(2)}, u32[]{:S(2)}) collective-permute-start(bf16[1040,512]{1,0:T(8,128)(2,1)S(1)} %copy-done.67), channel_id=1, source_target_pairs={{1,0},{2,1},{5,4},{6,5},{9,8},{10,9},{13,12},{14,13},{17,16},{18,1... | collective-permute-start | bytes 3194888 | tf_op jit(solution)/shard_map/ppermute | solution.py:86
  87.2 29.4 %collective-permute-start.4 = (bf16[1040,512]{1,0:T(8,128)(2,1)S(1)}, bf16[1040,512]{1,0:T(8,128)(2,1)S(1)}, u32[]{:S(2)}, u32[]{:S(2)}) collective-permute-start(bf16[1040,512]{1,0:T(8,128)(2,1)S(1)} %collective-permute-done.2), channel_id=1, source_target_pairs={{2,3},{6,7},{10,11},{14,15},{18,19},{22,23},{26,27},{30,31}} | collective-permute-start | bytes 3194888 | tf_op jit(solution)/shard_map/ppermute | solution.py:85
  114.3 25.1 %collective-permute-start.5 = (bf16[1040,512]{1,0:T(8,128)(2,1)S(1)}, bf16[1040,512]{1,0:T(8,128)(2,1)S(1)}, u32[]{:S(2)}, u32[]{:S(2)}) collective-permute-start(bf16[1040,512]{1,0:T(8,128)(2,1)S(1)} %collective-permute-done.3), channel_id=1, source_target_pairs={{1,0},{5,4},{9,8},{13,12},{17,16},{21,20},{25,24},{29,28}} | collective-permute-start | bytes 3194888 | tf_op jit(solution)/shard_map/ppermute | solution.py:86
  170.3 390.3 %reduce-scatter.4.cloned.1.call-start = ((), (), s32[]{:S(2)}) async-start(), calls=%async_computation.7 | async-start | bytes 19464192 | tf_op jit(solution)/shard_map/reduce_scatter | solution.py:583
  171.5 19.0 %collective-permute-start.6 = (bf16[1024,512]{1,0:T(8,128)(2,1)S(1)}, bf16[1024,512]{1,0:T(8,128)(2,1)}, u32[]{:S(2)}, u32[]{:S(2)}) collective-permute-start(bf16[1024,512]{1,0:T(8,128)(2,1)S(1)} %copy-done.11), channel_id=1, source_target_pairs={{0,1},{1,2},{2,3},{4,5},{5,6},{6,7},{8,9},{9,10},{10,11},{12,13},{... | collective-permute-start | bytes 3145736 | tf_op jit(solution)/shard_map/ppermute | solution.py:85
  173.8 23.0 %collective-permute-start.7 = (bf16[1024,512]{1,0:T(8,128)(2,1)S(1)}, bf16[1024,512]{1,0:T(8,128)(2,1)S(1)}, u32[]{:S(2)}, u32[]{:S(2)}) collective-permute-start(bf16[1024,512]{1,0:T(8,128)(2,1)S(1)} %copy-done.11), channel_id=1, source_target_pairs={{1,0},{2,1},{3,2},{5,4},{6,5},{7,6},{9,8},{10,9},{11,10},{13,12},{... | collective-permute-start | bytes 3145736 | tf_op jit(solution)/shard_map/ppermute | solution.py:86
  196.8 23.2 %collective-permute-start.9 = (bf16[1024,512]{1,0:T(8,128)(2,1)S(1)}, bf16[1024,512]{1,0:T(8,128)(2,1)S(1)}, u32[]{:S(2)}, u32[]{:S(2)}) collective-permute-start(bf16[1024,512]{1,0:T(8,128)(2,1)S(1)} %collective-permute-done.7), channel_id=1, source_target_pairs={{1,0},{2,1},{5,4},{6,5},{9,8},{10,9},{13,12},{14,13},{17,16},{18,1... | collective-permute-start | bytes 3145736 | tf_op jit(solution)/shard_map/ppermute | solution.py:86
  220.0 20.6 %collective-permute-start.11 = (bf16[1024,512]{1,0:T(8,128)(2,1)S(1)}, bf16[1024,512]{1,0:T(8,128)(2,1)S(1)}, u32[]{:S(2)}, u32[]{:S(2)}) collective-permute-start(bf16[1024,512]{1,0:T(8,128)(2,1)S(1)} %collective-permute-done.9), channel_id=1, source_target_pairs={{1,0},{5,4},{9,8},{13,12},{17,16},{21,20},{25,24},{29,28}} | collective-permute-start | bytes 3145736 | tf_op jit(solution)/shard_map/ppermute | solution.py:86
  241.9 24.6 %collective-permute-start.15 = (bf16[1024,512]{1,0:T(8,128)(2,1)}, bf16[1024,512]{1,0:T(8,128)(2,1)S(1)}, u32[]{:S(2)}, u32[]{:S(2)}) collective-permute-start(bf16[1024,512]{1,0:T(8,128)(2,1)} %shard_map.351), channel_id=1, source_target_pairs={{0,1},{1,2},{2,3},{4,5},{5,6},{6,7},{8,9},{9,10},{10,11},{12,13},{... | collective-permute-start | bytes 3145736 | tf_op jit(solution)/shard_map/ppermute | solution.py:85
  243.6 22.9 %collective-permute-start.16 = (bf16[1024,512]{1,0:T(8,128)(2,1)}, bf16[1024,512]{1,0:T(8,128)(2,1)}, u32[]{:S(2)}, u32[]{:S(2)}) collective-permute-start(bf16[1024,512]{1,0:T(8,128)(2,1)} %shard_map.351), channel_id=1, source_target_pairs={{1,0},{2,1},{3,2},{5,4},{6,5},{7,6},{9,8},{10,9},{11,10},{13,12},{... | collective-permute-start | bytes 3145736 | tf_op jit(solution)/shard_map/ppermute | solution.py:86
  267.5 55.9 %collective-permute-start.17 = (bf16[1024,512]{1,0:T(8,128)(2,1)}, bf16[1024,512]{1,0:T(8,128)(2,1)}, u32[]{:S(2)}, u32[]{:S(2)}) collective-permute-start(bf16[1024,512]{1,0:T(8,128)(2,1)} %get-tuple-element.52), channel_id=1, source_target_pairs={{1,2},{2,3},{5,6},{6,7},{9,10},{10,11},{13,14},{14,15},{17,18},{18... | collective-permute-start | bytes 3145736 | tf_op jit(solution)/shard_map/ppermute | solution.py:85
  269.3 54.1 %collective-permute-start.18 = (bf16[1024,512]{1,0:T(8,128)(2,1)}, bf16[1024,512]{1,0:T(8,128)(2,1)}, u32[]{:S(2)}, u32[]{:S(2)}) collective-permute-start(bf16[1024,512]{1,0:T(8,128)(2,1)} %get-tuple-element.53), channel_id=1, source_target_pairs={{1,0},{2,1},{5,4},{6,5},{9,8},{10,9},{13,12},{14,13},{17,16},{18,1... | collective-permute-start | bytes 3145736 | tf_op jit(solution)/shard_map/ppermute | solution.py:86
  323.4 31.8 %collective-permute-start.19 = (bf16[1024,512]{1,0:T(8,128)(2,1)}, bf16[1024,512]{1,0:T(8,128)(2,1)S(1)}, u32[]{:S(2)}, u32[]{:S(2)}) collective-permute-start(bf16[1024,512]{1,0:T(8,128)(2,1)} %get-tuple-element.54), channel_id=1, source_target_pairs={{2,3},{6,7},{10,11},{14,15},{18,19},{22,23},{26,27},{30,31}} | collective-permute-start | bytes 3145736 | tf_op jit(solution)/shard_map/ppermute | solution.py:85
  324.2 32.4 %collective-permute-start.20 = (bf16[1024,512]{1,0:T(8,128)(2,1)}, bf16[1024,512]{1,0:T(8,128)(2,1)S(1)}, u32[]{:S(2)}, u32[]{:S(2)}) collective-permute-start(bf16[1024,512]{1,0:T(8,128)(2,1)} %get-tuple-element.55), channel_id=1, source_target_pairs={{1,0},{5,4},{9,8},{13,12},{17,16},{21,20},{25,24},{29,28}} | collective-permute-start | bytes 3145736 | tf_op jit(solution)/shard_map/ppermute | solution.py:86
  388.7 389.0 %reduce-scatter.6.cloned.1.call-start = ((), (), s32[]{:S(2)}) async-start(), calls=%async_computation.8 | async-start | bytes 38928384 | tf_op jit(solution)/shard_map/reduce_scatter | solution.py:583
  431.5 32.8 %collective-permute-start.21 = (f32[4,1024]{1,0:T(4,128)S(1)}, f32[4,1024]{1,0:T(4,128)S(1)}, u32[]{:S(2)}, u32[]{:S(2)}) collective-permute-start(f32[4,1024]{1,0:T(4,128)S(1)} %pad_maximum_fusion.8.refs_0_), channel_id=1, source_target_pairs={{0,1},{1,2},{2,3},{3,0},{4,5},{5,6},{6,7},{7,4},{8,9},{9,10},{10,1... | collective-permute-start | bytes 49160 | tf_op jit(solution)/shard_map/ppermute | solution.py:156
  433.1 31.3 %collective-permute-start.22 = (f32[4,1024]{1,0:T(4,128)S(1)}, f32[4,1024]{1,0:T(4,128)S(1)}, u32[]{:S(2)}, u32[]{:S(2)}) collective-permute-start(f32[4,1024]{1,0:T(4,128)S(1)} %pad_maximum_fusion.8.refs_0_), channel_id=1, source_target_pairs={{0,2},{1,3},{2,0},{3,1},{4,6},{5,7},{6,4},{7,5},{8,10},{9,11},{10,... | collective-permute-start | bytes 49160 | tf_op jit(solution)/shard_map/ppermute | solution.py:156
  435.5 28.9 %collective-permute-start.23 = (f32[4,1024]{1,0:T(4,128)S(1)}, f32[4,1024]{1,0:T(4,128)S(1)}, u32[]{:S(2)}, u32[]{:S(2)}) collective-permute-start(f32[4,1024]{1,0:T(4,128)S(1)} %pad_maximum_fusion.8.refs_0_), channel_id=1, source_target_pairs={{0,3},{1,0},{2,1},{3,2},{4,7},{5,4},{6,5},{7,6},{8,11},{9,8},{10,9... | collective-permute-start | bytes 49160 | tf_op jit(solution)/shard_map/ppermute | solution.py:156
  493.9 29.1 %collective-permute-start.24 = (bf16[1024,512]{1,0:T(8,128)(2,1)}, bf16[1024,512]{1,0:T(8,128)(2,1)S(1)}, u32[]{:S(2)}, u32[]{:S(2)}) collective-permute-start(bf16[1024,512]{1,0:T(8,128)(2,1)} %get-tuple-element.56), channel_id=1, source_target_pairs={{0,1},{4,5},{8,9},{12,13},{16,17},{20,21},{24,25},{28,29}} | collective-permute-start | bytes 3145736 | tf_op jit(solution)/shard_map/ppermute | solution.py:140
  496.0 27.0 %collective-permute-start.25 = (bf16[1024,512]{1,0:T(8,128)(2,1)S(1)}, bf16[1024,512]{1,0:T(8,128)(2,1)S(1)}, u32[]{:S(2)}, u32[]{:S(2)}) collective-permute-start(bf16[1024,512]{1,0:T(8,128)(2,1)S(1)} %get-tuple-element.57), channel_id=1, source_target_pairs={{3,2},{7,6},{11,10},{15,14},{19,18},{23,22},{27,26},{31,30}} | collective-permute-start | bytes 3145736 | tf_op jit(solution)/shard_map/ppermute | solution.py:141
  534.1 24.3 %collective-permute-start.26 = (bf16[1024,512]{1,0:T(8,128)(2,1)S(1)}, bf16[1024,512]{1,0:T(8,128)(2,1)S(1)}, u32[]{:S(2)}, u32[]{:S(2)}) collective-permute-start(bf16[1024,512]{1,0:T(8,128)(2,1)S(1)} %get-tuple-element.58), channel_id=1, source_target_pairs={{0,1},{1,2},{4,5},{5,6},{8,9},{9,10},{12,13},{13,14},{16,17},{17,1... | collective-permute-start | bytes 3145736 | tf_op jit(solution)/shard_map/ppermute | solution.py:140
  535.9 22.5 %collective-permute-start.27 = (bf16[1024,512]{1,0:T(8,128)(2,1)S(1)}, bf16[1024,512]{1,0:T(8,128)(2,1)S(1)}, u32[]{:S(2)}, u32[]{:S(2)}) collective-permute-start(bf16[1024,512]{1,0:T(8,128)(2,1)S(1)} %get-tuple-element.59), channel_id=1, source_target_pairs={{2,1},{3,2},{6,5},{7,6},{10,9},{11,10},{14,13},{15,14},{18,17},{19... | collective-permute-start | bytes 3145736 | tf_op jit(solution)/shard_map/ppermute | solution.py:141
  560.7 307.6 %reduce-scatter.8.cloned.1.call-start = ((), (), s32[]{:S(2)}) async-start(), calls=%async_computation.9 | async-start | bytes 10027008 | tf_op jit(solution)/shard_map/reduce_scatter | solution.py:583
  562.0 27.5 %collective-permute-start.28 = (bf16[1024,512]{1,0:T(8,128)(2,1)S(1)}, bf16[1024,512]{1,0:T(8,128)(2,1)}, u32[]{:S(2)}, u32[]{:S(2)}) collective-permute-start(bf16[1024,512]{1,0:T(8,128)(2,1)S(1)} %copy-done.25), channel_id=1, source_target_pairs={{0,1},{1,2},{2,3},{4,5},{5,6},{6,7},{8,9},{9,10},{10,11},{12,13},{... | collective-permute-start | bytes 3145736 | tf_op jit(solution)/shard_map/ppermute | solution.py:140
  569.6 25.4 %collective-permute-start.29 = (bf16[1024,512]{1,0:T(8,128)(2,1)S(1)}, bf16[1024,512]{1,0:T(8,128)(2,1)S(1)}, u32[]{:S(2)}, u32[]{:S(2)}) collective-permute-start(bf16[1024,512]{1,0:T(8,128)(2,1)S(1)} %get-tuple-element.61), channel_id=1, source_target_pairs={{1,0},{2,1},{3,2},{5,4},{6,5},{7,6},{9,8},{10,9},{11,10},{13,12},{... | collective-permute-start | bytes 3145736 | tf_op jit(solution)/shard_map/ppermute | solution.py:141
  600.0 21.6 %collective-permute-start.30 = (bf16[1024,512]{1,0:T(8,128)(2,1)}, bf16[1024,512]{1,0:T(8,128)(2,1)S(1)}, u32[]{:S(2)}, u32[]{:S(2)}) collective-permute-start(bf16[1024,512]{1,0:T(8,128)(2,1)} %shard_map.368), channel_id=1, source_target_pairs={{0,1},{1,2},{2,3},{4,5},{5,6},{6,7},{8,9},{9,10},{10,11},{12,13},{... | collective-permute-start | bytes 3145736 | tf_op jit(solution)/shard_map/ppermute | solution.py:85
  601.5 24.3 %collective-permute-start.31 = (bf16[1024,512]{1,0:T(8,128)(2,1)}, bf16[1024,512]{1,0:T(8,128)(2,1)}, u32[]{:S(2)}, u32[]{:S(2)}) collective-permute-start(bf16[1024,512]{1,0:T(8,128)(2,1)} %shard_map.368), channel_id=1, source_target_pairs={{1,0},{2,1},{3,2},{5,4},{6,5},{7,6},{9,8},{10,9},{11,10},{13,12},{... | collective-permute-start | bytes 3145736 | tf_op jit(solution)/shard_map/ppermute | solution.py:86
  625.8 30.0 %collective-permute-start.34 = (bf16[1024,512]{1,0:T(8,128)(2,1)}, bf16[1024,512]{1,0:T(8,128)(2,1)S(1)}, u32[]{:S(2)}, u32[]{:S(2)}) collective-permute-start(bf16[1024,512]{1,0:T(8,128)(2,1)} %get-tuple-element.62.refs_2_), channel_id=1, source_target_pairs={{1,2},{2,3},{5,6},{6,7},{9,10},{10,11},{13,14},{14,15},{17,18},{18... | collective-permute-start | bytes 3145736 | tf_op jit(solution)/shard_map/ppermute | solution.py:85
  632.7 23.0 %collective-permute-start.32 = (bf16[1024,512]{1,0:T(8,128)(2,1)}, bf16[1024,512]{1,0:T(8,128)(2,1)S(1)}, u32[]{:S(2)}, u32[]{:S(2)}) collective-permute-start(bf16[1024,512]{1,0:T(8,128)(2,1)} %get-tuple-element.63), channel_id=1, source_target_pairs={{0,1},{4,5},{8,9},{12,13},{16,17},{20,21},{24,25},{28,29}} | collective-permute-start | bytes 3145736 | tf_op jit(solution)/shard_map/ppermute | solution.py:140
  636.6 19.2 %collective-permute-start.33 = (bf16[1024,512]{1,0:T(8,128)(2,1)}, bf16[1024,512]{1,0:T(8,128)(2,1)S(1)}, u32[]{:S(2)}, u32[]{:S(2)}) collective-permute-start(bf16[1024,512]{1,0:T(8,128)(2,1)} %get-tuple-element.64), channel_id=1, source_target_pairs={{3,2},{7,6},{11,10},{15,14},{19,18},{23,22},{27,26},{31,30}} | collective-permute-start | bytes 3145736 | tf_op jit(solution)/shard_map/ppermute | solution.py:141
  637.3 23.4 %collective-permute-start.35 = (bf16[1024,512]{1,0:T(8,128)(2,1)}, bf16[1024,512]{1,0:T(8,128)(2,1)}, u32[]{:S(2)}, u32[]{:S(2)}) collective-permute-start(bf16[1024,512]{1,0:T(8,128)(2,1)} %get-tuple-element.65), channel_id=1, source_target_pairs={{1,0},{2,1},{5,4},{6,5},{9,8},{10,9},{13,12},{14,13},{17,16},{18,1... | collective-permute-start | bytes 3145736 | tf_op jit(solution)/shard_map/ppermute | solution.py:86
  660.7 39.6 %collective-permute-start.40 = (bf16[1024,512]{1,0:T(8,128)(2,1)}, bf16[1024,512]{1,0:T(8,128)(2,1)S(1)}, u32[]{:S(2)}, u32[]{:S(2)}) collective-permute-start(bf16[1024,512]{1,0:T(8,128)(2,1)} %get-tuple-element.66.refs_4_), channel_id=1, source_target_pairs={{2,3},{6,7},{10,11},{14,15},{18,19},{22,23},{26,27},{30,31}} | collective-permute-start | bytes 3145736 | tf_op jit(solution)/shard_map/ppermute | solution.py:85
  669.0 19.6 %collective-permute-start.36 = (bf16[1024,512]{1,0:T(8,128)(2,1)S(1)}, bf16[1024,512]{1,0:T(8,128)(2,1)S(1)}, u32[]{:S(2)}, u32[]{:S(2)}) collective-permute-start(bf16[1024,512]{1,0:T(8,128)(2,1)S(1)} %get-tuple-element.67), channel_id=1, source_target_pairs={{0,1},{1,2},{4,5},{5,6},{8,9},{9,10},{12,13},{13,14},{16,17},{17,1... | collective-permute-start | bytes 3145736 | tf_op jit(solution)/shard_map/ppermute | solution.py:140
  672.6 28.9 %collective-permute-start.41 = (bf16[1024,512]{1,0:T(8,128)(2,1)}, bf16[1024,512]{1,0:T(8,128)(2,1)S(1)}, u32[]{:S(2)}, u32[]{:S(2)}) collective-permute-start(bf16[1024,512]{1,0:T(8,128)(2,1)} %get-tuple-element.74), channel_id=1, source_target_pairs={{1,0},{5,4},{9,8},{13,12},{17,16},{21,20},{25,24},{29,28}} | collective-permute-start | bytes 3145736 | tf_op jit(solution)/shard_map/ppermute | solution.py:86
  691.3 34.1 %collective-permute-start.38 = (bf16[1024,512]{1,0:T(8,128)(2,1)}, bf16[1024,512]{1,0:T(8,128)(2,1)S(1)}, u32[]{:S(2)}, u32[]{:S(2)}) collective-permute-start(bf16[1024,512]{1,0:T(8,128)(2,1)} %get-tuple-element.69), channel_id=1, source_target_pairs={{0,1},{1,2},{2,3},{4,5},{5,6},{6,7},{8,9},{9,10},{10,11},{12,13},{... | collective-permute-start | bytes 3145736 | tf_op jit(solution)/shard_map/ppermute | solution.py:140
  698.5 26.9 %collective-permute-start.39 = (bf16[1024,512]{1,0:T(8,128)(2,1)}, bf16[1024,512]{1,0:T(8,128)(2,1)S(1)}, u32[]{:S(2)}, u32[]{:S(2)}) collective-permute-start(bf16[1024,512]{1,0:T(8,128)(2,1)} %get-tuple-element.70), channel_id=1, source_target_pairs={{1,0},{2,1},{3,2},{5,4},{6,5},{7,6},{9,8},{10,9},{11,10},{13,12},{... | collective-permute-start | bytes 3145736 | tf_op jit(solution)/shard_map/ppermute | solution.py:141
  746.7 22.7 %collective-permute-start.42 = (bf16[1040,512]{1,0:T(8,128)(2,1)S(1)}, bf16[1040,512]{1,0:T(8,128)(2,1)S(1)}, u32[]{:S(2)}, u32[]{:S(2)}) collective-permute-start(bf16[1040,512]{1,0:T(8,128)(2,1)S(1)} %get-tuple-element.76), channel_id=1, source_target_pairs={{0,1},{4,5},{8,9},{12,13},{16,17},{20,21},{24,25},{28,29}} | collective-permute-start | bytes 3194888 | tf_op jit(solution)/shard_map/ppermute | solution.py:140
  778.9 21.3 %collective-permute-start.44 = (bf16[1040,512]{1,0:T(8,128)(2,1)S(1)}, bf16[1040,512]{1,0:T(8,128)(2,1)S(1)}, u32[]{:S(2)}, u32[]{:S(2)}) collective-permute-start(bf16[1040,512]{1,0:T(8,128)(2,1)S(1)} %copy-done.39), channel_id=1, source_target_pairs={{0,1},{1,2},{4,5},{5,6},{8,9},{9,10},{12,13},{13,14},{16,17},{17,1... | collective-permute-start | bytes 3194888 | tf_op jit(solution)/shard_map/ppermute | solution.py:140
  803.9 26.1 %collective-permute-start.46 = (bf16[1040,512]{1,0:T(8,128)(2,1)S(1)}, bf16[1040,512]{1,0:T(8,128)(2,1)S(1)}, u32[]{:S(2)}, u32[]{:S(2)}) collective-permute-start(bf16[1040,512]{1,0:T(8,128)(2,1)S(1)} %get-tuple-element.80), channel_id=1, source_target_pairs={{0,1},{1,2},{2,3},{4,5},{5,6},{6,7},{8,9},{9,10},{10,11},{12,13},{... | collective-permute-start | bytes 3194888 | tf_op jit(solution)/shard_map/ppermute | solution.py:140
  811.7 22.5 %collective-permute-start.47 = (bf16[1040,512]{1,0:T(8,128)(2,1)S(1)}, bf16[1040,512]{1,0:T(8,128)(2,1)S(1)}, u32[]{:S(2)}, u32[]{:S(2)}) collective-permute-start(bf16[1040,512]{1,0:T(8,128)(2,1)S(1)} %get-tuple-element.81), channel_id=1, source_target_pairs={{1,0},{2,1},{3,2},{5,4},{6,5},{7,6},{9,8},{10,9},{11,10},{13,12},{... | collective-permute-start | bytes 3194888 | tf_op jit(solution)/shard_map/ppermute | solution.py:141
  (125 other events, 1261.7 us)
Sparse Core Ops, SparseCore 0:
  11.1 48.2 all-gather.4
  73.5 59.9 all-gather.6
  135.4 165.5 all-gather.8
  303.3 95.4 all-gather.10
  402.3 118.5 reduce-scatter.3
  560.9 211.9 reduce-scatter.5
  777.8 72.9 reduce-scatter.7
